TPU v7x, 32 devices: a whole 2x2x4 slice. The times are simulated.
32 devices in a mesh: dp: 4 (over x, core), fsdp: 8 (over z, y).
Axes of the slice: x: 2, y: 2, z: 4, core: 2. Of those that a mesh axis runs over, the one named last changes fastest.
Arguments:
- token_ids: int32 [64, 512], P(('dp', 'fsdp')), may hold values from 0 to 30521
- lengths: int32 [64], P(('dp', 'fsdp')), may hold values from 128 to 512
- pair_ids: int32 [3, 24], replicated, may hold values from 0 to 63
- scores: float32 [2, 24], replicated, may hold values from -0.5 to 1
- word_table: float32 [30720, 768], P('fsdp'), may hold values from -0.21875 to 0.21875
- pos_table: float32 [512, 768], P('fsdp'), may hold values from -0.21875 to 0.21875
- qkv_weight: float32 [768, 2304], P('fsdp'), may hold values from -0.21875 to 0.21875
- out_weight: float32 [768, 768], P('fsdp'), may hold values from -1.75 to 1.75
- up_weight: float32 [768, 3072], P('fsdp'), may hold values from -0.21875 to 0.21875
- down_weight: float32 [3072, 768], P('fsdp'), may hold values from -0.21875 to 0.21875
- small_params: float32 [14, 768], P(None, 'fsdp')
- word_moment: float32 [30720, 768], P('fsdp'), may hold values from -1.5258789e-05 to 1.5258789e-05
- pos_moment: float32 [512, 768], P('fsdp'), may hold values from -0.00015258789 to 0.00015258789
- qkv_moment: float32 [768, 2304], P('fsdp'), may hold values from -0.00015258789 to 0.00015258789
- out_moment: float32 [768, 768], P('fsdp'), may hold values from -0.00015258789 to 0.00015258789
- up_moment: float32 [768, 3072], P('fsdp'), may hold values from -0.00015258789 to 0.00015258789
- down_moment: float32 [3072, 768], P('fsdp'), may hold values from -0.00015258789 to 0.00015258789
- small_moment: float32 [14, 768], P(None, 'fsdp'), may hold values from -0.0004272461 to 0.0004272461
- word_average: float32 [30720, 768], P('fsdp'), may hold values from -0.21875 to 0.21875
- pos_average: float32 [512, 768], P('fsdp'), may hold values from -0.21875 to 0.21875
- qkv_average: float32 [768, 2304], P('fsdp'), may hold values from -0.21875 to 0.21875
- out_average: float32 [768, 768], P('fsdp'), may hold values from -1.75 to 1.75
- up_average: float32 [768, 3072], P('fsdp'), may hold values from -0.21875 to 0.21875
- down_average: float32 [3072, 768], P('fsdp'), may hold values from -0.21875 to 0.21875
- small_average: float32 [14, 768], P(None, 'fsdp'), may hold values from 0.5 to 1.5
Outputs:
- loss_sum: float32 [], replicated
- grad_norm: float32 [], replicated
- new_word_table: float32 [30720, 768], P('fsdp')
- new_pos_table: float32 [512, 768], P('fsdp')
- new_qkv_weight: float32 [768, 2304], P('fsdp')
- new_out_weight: float32 [768, 768], P('fsdp')
- new_up_weight: float32 [768, 3072], P('fsdp')
- new_down_weight: float32 [3072, 768], P('fsdp')
- new_small_params: float32 [14, 768], P(None, 'fsdp')
- new_word_moment: float32 [30720, 768], P('fsdp')
- new_pos_moment: float32 [512, 768], P('fsdp')
- new_qkv_moment: float32 [768, 2304], P('fsdp')
- new_out_moment: float32 [768, 768], P('fsdp')
- new_up_moment: float32 [768, 3072], P('fsdp')
- new_down_moment: float32 [3072, 768], P('fsdp')
- new_small_moment: float32 [14, 768], P(None, 'fsdp')
- new_word_average: float32 [30720, 768], P('fsdp')
- new_pos_average: float32 [512, 768], P('fsdp')
- new_qkv_average: float32 [768, 2304], P('fsdp')
- new_out_average: float32 [768, 768], P('fsdp')
- new_up_average: float32 [768, 3072], P('fsdp')
- new_down_average: float32 [3072, 768], P('fsdp')
- new_small_average: float32 [14, 768], P(None, 'fsdp')
All inputs are finite; a program needn't handle non-finite values.
Results may differ from a plain program's by a relative error of at most 0.013.
The roundings to bfloat16 on the way count: a program that leaves them out, or rounds other values in their place, can miss the bound.
Values may be sent and summed in bfloat16 or wider, within the bound.
A program may use at most 576 MiB of HBM per device.

v0:
```python
import math

import jax
import jax.numpy as jnp
from jax import lax
from jax.sharding import PartitionSpec as P

D = 768
H = 12
FF = 3072
VOCAB = 30720
LEN = 512


MOMENTUM = 0.9
RATE = 3000.0
KEEP = 0.9


def layer_norm(v, gain, shift):
    mean = jnp.mean(v, -1, keepdims=True)
    cent = v - mean
    var = jnp.mean(cent * cent, -1, keepdims=True)
    return cent * lax.rsqrt(var + 1e-12) * gain + shift


def gelu_exact(v):
    return jax.nn.gelu(v, approximate=False)


def matmul(left, right):
    return jnp.dot(left, right, preferred_element_type=jnp.float32)


def outer_sum(left, right):
    return lax.dot_general(
        left, right, (((0,), (0,)), ((), ())), preferred_element_type=jnp.float32
    )


def back_mul(grad, weight):
    return lax.dot_general(
        grad, weight, (((1,), (1,)), ((), ())), preferred_element_type=jnp.float32
    )


def cosine(first, second):
    dots = jnp.sum(first * second, -1)
    return (
        dots
        * lax.rsqrt(jnp.sum(first * first, -1) + 1e-06)
        * lax.rsqrt(jnp.sum(second * second, -1) + 1e-06)
    )


def pair_loss(pooled, pair_ids, scores):
    anchors = pooled[pair_ids[0]]
    near = cosine(anchors, pooled[pair_ids[1]]) - scores[0]
    far = cosine(anchors, pooled[pair_ids[2]]) - scores[1]
    return jnp.sum(near * near) + jnp.sum(far * far)


def take_rows(table, ids):
    count = table.shape[0]
    inside = (ids >= 0) & (ids < count)
    rows = jnp.take(table, jnp.clip(ids, 0, count - 1), axis=0)
    return jnp.where(inside[:, None], rows, jnp.zeros_like(rows))


def add_into_rows(values, ids, count):
    inside = (ids >= 0) & (ids < count)
    slots = jnp.where(inside, ids, count)
    return jax.ops.segment_sum(values, slots, num_segments=count + 1)[:count]


def attention_logits(query, keys, live_bias, scale):
    raw = jnp.einsum("bqhd,bkhd->bhqk", query, keys, preferred_element_type=jnp.float32) * scale
    return raw + live_bias[:, None, None, :]


def layer_forward(x, params, live_bias, batch, seq):
    qkv_w, out_w, up_w, down_w, small = params
    width = x.shape[1]
    size = width // H
    scale = size ** (-0.5)
    h0 = layer_norm(x, small[0], small[1])
    qkv_bias = jnp.concatenate([small[2], jnp.zeros_like(small[2]), small[3]])
    qkv = matmul(h0.astype(jnp.bfloat16), qkv_w) + qkv_bias
    parts = qkv.astype(jnp.bfloat16).reshape(batch, seq, 3, H, size)
    query, keys, values = (parts[:, :, 0], parts[:, :, 1], parts[:, :, 2])
    logits = attention_logits(query, keys, live_bias, scale)
    top = jnp.max(logits, -1, keepdims=True)
    total_log = top + jnp.log(jnp.sum(jnp.exp(logits - top), -1, keepdims=True))
    probs = jnp.exp(logits - total_log).astype(jnp.bfloat16)
    mixed = jnp.einsum("bhqk,bkhd->bqhd", probs, values, preferred_element_type=jnp.float32)
    mixed = mixed.astype(jnp.bfloat16).reshape(-1, width)
    first_sum = h0 + (matmul(mixed, out_w) + small[4])
    h1 = layer_norm(first_sum, small[5], small[6])
    up = matmul(h1.astype(jnp.bfloat16), up_w) + small[7:11].reshape(-1)
    act = gelu_exact(up).astype(jnp.bfloat16)
    second_sum = h1 + (matmul(act, down_w) + small[11])
    h2 = layer_norm(second_sum, small[12], small[13])
    kept = (x, h0, query, keys, values, total_log, mixed, first_sum, h1, up, act, second_sum)
    return (h2, kept)


def layer_backward(grad_h2, kept, params, live_bias):
    qkv_w, out_w, up_w, down_w, small = params
    x, h0, query, keys, values, total_log, mixed, first_sum, h1, up, act, second_sum = kept
    batch, seq, heads, size = query.shape
    width = heads * size
    scale = size ** (-0.5)
    _, pull_two = jax.vjp(layer_norm, second_sum, small[12], small[13])
    grad_r2, grad_g2, grad_b2 = pull_two(grad_h2)
    grad_ffn = grad_r2.astype(jnp.bfloat16)
    grad_down = outer_sum(act, grad_ffn)
    grad_act = back_mul(grad_ffn, down_w)
    _, pull_gelu = jax.vjp(gelu_exact, up)
    grad_up = pull_gelu(grad_act)[0]
    grad_upb = grad_up.astype(jnp.bfloat16)
    grad_upw = outer_sum(h1.astype(jnp.bfloat16), grad_upb)
    grad_h1 = grad_r2 + back_mul(grad_upb, up_w)
    _, pull_one = jax.vjp(layer_norm, first_sum, small[5], small[6])
    grad_r1, grad_g1, grad_b1 = pull_one(grad_h1)
    grad_att = grad_r1.astype(jnp.bfloat16)
    grad_outw = outer_sum(mixed, grad_att)
    grad_mixed = back_mul(grad_att, out_w).astype(jnp.bfloat16).reshape(batch, seq, heads, size)
    logits = attention_logits(query, keys, live_bias, scale)
    probs = jnp.exp(logits - total_log)
    grad_probs = jnp.einsum(
        "bqhd,bkhd->bhqk", grad_mixed, values, preferred_element_type=jnp.float32
    )
    grad_values = jnp.einsum(
        "bhqk,bqhd->bkhd",
        probs.astype(jnp.bfloat16),
        grad_mixed,
        preferred_element_type=jnp.float32,
    )
    inner = jnp.sum(probs * grad_probs, -1, keepdims=True)
    grad_logits = (probs * (grad_probs - inner)).astype(jnp.bfloat16)
    grad_query = (
        jnp.einsum("bhqk,bkhd->bqhd", grad_logits, keys, preferred_element_type=jnp.float32) * scale
    )
    grad_keys = (
        jnp.einsum("bhqk,bqhd->bkhd", grad_logits, query, preferred_element_type=jnp.float32)
        * scale
    )
    grad_qkv = jnp.stack([grad_query, grad_keys, grad_values], 2).reshape(-1, 3 * width)
    grad_qkvb = grad_qkv.astype(jnp.bfloat16)
    grad_qkvw = outer_sum(h0.astype(jnp.bfloat16), grad_qkvb)
    grad_h0 = grad_r1 + back_mul(grad_qkvb, qkv_w)
    _, pull_zero = jax.vjp(layer_norm, x, small[0], small[1])
    grad_x, grad_g0, grad_b0 = pull_zero(grad_h0)
    column_sums = jnp.sum(grad_qkv, 0)
    head_rows = jnp.stack(
        [
            grad_g0,
            grad_b0,
            column_sums[:width],
            column_sums[2 * width :],
            jnp.sum(grad_r1, 0),
            grad_g1,
            grad_b1,
        ]
    )
    tail_rows = jnp.stack([jnp.sum(grad_r2, 0), grad_g2, grad_b2])
    grad_small = jnp.concatenate([head_rows, jnp.sum(grad_up, 0).reshape(4, width), tail_rows], 0)
    return (grad_x, (grad_qkvw, grad_outw, grad_upw, grad_down, grad_small))


def renew(weight, moment, average, grad, factor):
    step = factor * grad
    buffer = MOMENTUM * moment + step
    fresh = weight - RATE * (step + MOMENTUM * buffer)
    return (fresh, buffer, KEEP * average + (1.0 - KEEP) * fresh)


def shards(
    token_ids,
    lengths,
    pair_ids,
    scores,
    word_table,
    pos_table,
    qkv_weight,
    out_weight,
    up_weight,
    down_weight,
    small_params,
    word_moment,
    pos_moment,
    qkv_moment,
    out_moment,
    up_moment,
    down_moment,
    small_moment,
    word_average,
    pos_average,
    qkv_average,
    out_average,
    up_average,
    down_average,
    small_average,
):
    batch, seq = token_ids.shape
    width = D
    pos_low = pos_table.astype(jnp.bfloat16)
    qkv_low = qkv_weight.astype(jnp.bfloat16)
    out_low = out_weight.astype(jnp.bfloat16)
    up_low = up_weight.astype(jnp.bfloat16)
    down_low = down_weight.astype(jnp.bfloat16)
    small_low = small_params.astype(jnp.bfloat16)
    word_low = word_table.astype(jnp.bfloat16)
    gathered = (
        lax.all_gather(pos_low, "fsdp", axis=0, tiled=True),
        lax.all_gather(qkv_low, "fsdp", axis=0, tiled=True),
        lax.all_gather(out_low, "fsdp", axis=0, tiled=True),
        lax.all_gather(up_low, "fsdp", axis=0, tiled=True),
        lax.all_gather(down_low, "fsdp", axis=0, tiled=True),
        lax.all_gather(small_low, "fsdp", axis=1, tiled=True),
    )
    params = (gathered[1], gathered[2], gathered[3], gathered[4], gathered[5].astype(jnp.float32))
    flat_ids = token_ids.reshape(-1)
    own_rows = word_table.shape[0]
    words = take_rows(lax.all_gather(word_low, "fsdp", axis=0, tiled=True), flat_ids).astype(
        jnp.float32
    )
    x = (words.reshape(batch, seq, width) + gathered[0].astype(jnp.float32)[None]).reshape(
        -1, width
    )
    live = lax.iota(jnp.int32, seq)[None, :] < lengths[:, None]
    live_bias = jnp.where(live, 0.0, -1000000000.0).astype(jnp.float32)
    live_f = live.astype(jnp.float32)
    counts = lengths.astype(jnp.float32)
    h2, kept = layer_forward(x, params, live_bias, batch, seq)
    pooled = jnp.sum(h2.reshape(batch, seq, width) * live_f[:, :, None], 1) / counts[:, None]
    everyone = lax.all_gather(pooled, ("dp", "fsdp"), axis=0, tiled=True)
    loss, pull_loss = jax.vjp(lambda rows: pair_loss(rows, pair_ids, scores), everyone)
    grad_all = pull_loss(jnp.ones((), jnp.float32))[0]
    grad_pooled = lax.dynamic_slice_in_dim(
        grad_all, lax.axis_index(("dp", "fsdp")) * batch, batch, 0
    )
    grad_h2 = (live_f[:, :, None] * (grad_pooled / counts[:, None])[:, None, :]).reshape(-1, width)
    again = (
        lax.all_gather(qkv_low, "fsdp", axis=0, tiled=True),
        lax.all_gather(out_low, "fsdp", axis=0, tiled=True),
        lax.all_gather(up_low, "fsdp", axis=0, tiled=True),
        lax.all_gather(down_low, "fsdp", axis=0, tiled=True),
        lax.all_gather(small_low, "fsdp", axis=1, tiled=True),
    )
    back_params = (again[0], again[1], again[2], again[3], again[4].astype(jnp.float32))
    grad_x, layer_grads = layer_backward(grad_h2, kept, back_params, live_bias)
    grad_pos = jnp.sum(grad_x.reshape(batch, seq, width), 0)
    reduced = (
        lax.psum_scatter(grad_pos, "fsdp", scatter_dimension=0, tiled=True),
        lax.psum_scatter(layer_grads[0], "fsdp", scatter_dimension=0, tiled=True),
        lax.psum_scatter(layer_grads[1], "fsdp", scatter_dimension=0, tiled=True),
        lax.psum_scatter(layer_grads[2], "fsdp", scatter_dimension=0, tiled=True),
        lax.psum_scatter(layer_grads[3], "fsdp", scatter_dimension=0, tiled=True),
        lax.psum_scatter(layer_grads[4], "fsdp", scatter_dimension=1, tiled=True),
    )
    grad_table = lax.psum_scatter(
        add_into_rows(grad_x, flat_ids, own_rows * lax.axis_size("fsdp")),
        "fsdp",
        scatter_dimension=0,
        tiled=True,
    )
    summed = (
        lax.psum(grad_table.astype(jnp.bfloat16), "dp").astype(jnp.float32),
        lax.psum(reduced[0].astype(jnp.bfloat16), "dp").astype(jnp.float32),
        lax.psum(reduced[1].astype(jnp.bfloat16), "dp").astype(jnp.float32),
        lax.psum(reduced[2].astype(jnp.bfloat16), "dp").astype(jnp.float32),
        lax.psum(reduced[3].astype(jnp.bfloat16), "dp").astype(jnp.float32),
        lax.psum(reduced[4].astype(jnp.bfloat16), "dp").astype(jnp.float32),
        lax.psum(reduced[5].astype(jnp.bfloat16), "dp").astype(jnp.float32),
    )
    local_squares = jnp.zeros((), jnp.float32)
    for grad in summed:
        local_squares = local_squares + jnp.sum(grad * grad)
    total = lax.psum(local_squares, "fsdp")
    norm = jnp.sqrt(total)
    limit = 1e-05 * math.sqrt((VOCAB + LEN + 4 * D + 2 * FF + 14) * D)
    factor = jnp.minimum(1.0, limit / (norm + 1e-06))
    weights = (word_table, pos_table, qkv_weight, out_weight, up_weight, down_weight, small_params)
    moments = (
        word_moment,
        pos_moment,
        qkv_moment,
        out_moment,
        up_moment,
        down_moment,
        small_moment,
    )
    averages = (
        word_average,
        pos_average,
        qkv_average,
        out_average,
        up_average,
        down_average,
        small_average,
    )
    new_w = []
    new_m = []
    new_a = []
    for weight, moment, average, grad in zip(weights, moments, averages, summed):
        fresh, buffer, mean_new = renew(weight, moment, average, grad, factor)
        new_w.append(fresh)
        new_m.append(buffer)
        new_a.append(mean_new)
    return (
        loss,
        norm,
        new_w[0],
        new_w[1],
        new_w[2],
        new_w[3],
        new_w[4],
        new_w[5],
        new_w[6],
        new_m[0],
        new_m[1],
        new_m[2],
        new_m[3],
        new_m[4],
        new_m[5],
        new_m[6],
        new_a[0],
        new_a[1],
        new_a[2],
        new_a[3],
        new_a[4],
        new_a[5],
        new_a[6],
    )


def solution(mesh):
    placed = (
        P(("dp", "fsdp"), None),
        P(("dp", "fsdp")),
        P(),
        P(),
        P("fsdp", None),
        P("fsdp", None),
        P("fsdp", None),
        P("fsdp", None),
        P("fsdp", None),
        P("fsdp", None),
        P(None, "fsdp"),
        P("fsdp", None),
        P("fsdp", None),
        P("fsdp", None),
        P("fsdp", None),
        P("fsdp", None),
        P("fsdp", None),
        P(None, "fsdp"),
        P("fsdp", None),
        P("fsdp", None),
        P("fsdp", None),
        P("fsdp", None),
        P("fsdp", None),
        P("fsdp", None),
        P(None, "fsdp"),
    )
    return jax.shard_map(
        shards,
        mesh=mesh,
        in_specs=placed,
        out_specs=(
            P(),
            P(),
            P("fsdp", None),
            P("fsdp", None),
            P("fsdp", None),
            P("fsdp", None),
            P("fsdp", None),
            P("fsdp", None),
            P(None, "fsdp"),
            P("fsdp", None),
            P("fsdp", None),
            P("fsdp", None),
            P("fsdp", None),
            P("fsdp", None),
            P("fsdp", None),
            P(None, "fsdp"),
            P("fsdp", None),
            P("fsdp", None),
            P("fsdp", None),
            P("fsdp", None),
            P("fsdp", None),
            P("fsdp", None),
            P(None, "fsdp"),
        ),
        check_vma=False,
    )
```

profile of v0, /device:TPU:0, one launch (start us, length us, event | category | flops | bytes accessed | tf_op | source)
XLA Modules:
  0.0 3791.9 jit_solution(9835769256957172389)
XLA Ops:
  7.2 7.5 convert_element_type.173
  20.8 105.1 %all-gather = bf16[8,96,14]{1,2,0:T(8,128)(2,1)S(1)} all-gather(bf16[1,96,14]{1,2,0:T(8,128)(2,1)S(1)} %convert_bitcast_fusion), channel_id=1, replica_groups=mesh['dp'=4,'fsdp'=8] {'fsdp'}, dimensions={0}, use_global_device_ids=true | all-gather | bytes 24192 | tf_op jit(solution)/shard_map/all_gather | solution.py:220
  130.4 47.0 %all_gather.30 = bf16[512,768]{1,0:T(8,128)(2,1)S(1)} all-gather(bf16[64,768]{1,0:T(8,128)(2,1)S(1)} %convert_element_type.175), channel_id=1, replica_groups=mesh['dp'=4,'fsdp'=8] {'fsdp'}, dimensions={0}, use_global_device_ids=true | all-gather | bytes 884736 | tf_op jit(solution)/shard_map/all_gather | solution.py:215
  177.6 748.8 %all-gather.8.cloned.1.call-done = bf16[30720,768]{1,0:T(8,128)(2,1)} async-done(((bf16[3840,768]{1,0:T(8,128)(2,1)}), bf16[30720,768]{1,0:T(8,128)(2,1)}) %all-gather.8.cloned.1.call-update) | async-done | bytes 47185936 | tf_op jit(solution)/shard_map/all_gather | solution.py:225
  926.3 13.3 gather_fusion
  941.9 3.3 fusion.28
  945.1 49.1 %all-gather.10.cloned.1.call-done = bf16[768,2304]{1,0:T(8,128)(2,1)} async-done(((bf16[96,2304]{1,0:T(8,128)(2,1)}), bf16[768,2304]{1,0:T(8,128)(2,1)}) %all-gather.10.cloned.1.call-update) | async-done | bytes 3538960 | tf_op jit(solution)/shard_map/all_gather | solution.py:216
  994.3 8.5 add_convert_fusion
  1002.8 6.6 copy.86
  1009.4 8.8 reshape.646
  1018.2 4.9 fusion.121
  1023.1 11.0 fusion
  1034.2 11.0 exponential_reduce_fusion
  1045.3 11.9 fusion.32
  1060.5 4.2 fusion.123
  1066.8 51.1 %all-gather.14.cloned.1.call-done = bf16[768,3072]{1,0:T(8,128)(2,1)} async-done(((bf16[96,3072]{1,0:T(8,128)(2,1)}), bf16[768,3072]{1,0:T(8,128)(2,1)}) %all-gather.14.cloned.1.call-update) | async-done | bytes 4718608 | tf_op jit(solution)/shard_map/all_gather | solution.py:218
  1117.9 38.4 %multiply_convert_fusion.1 = (bf16[1024,3072]{1,0:T(8,128)(2,1)}, f32[1024,3072]{1,0:T(8,128)}, f32[1024,3072]{1,0:T(8,128)}) fusion(f32[3072]{0:T(1024)S(1)} %add.392, bf16[768,3072]{1,0:T(8,128)(2,1)} %all-gather.14.cloned.1.call-done, f32[1024,768]{1,0:T(8,128)} %copy-done.4, f32[768]{0:T(1024)S(1)} %get-tuple-element.39, ...), kind=kOutput, calls=%fused_computation.21 | convolution fusion | flops 5043388416 | bytes 39348224 | tf_op jit(solution)/shard_map/dot_general | solution.py:32
  1156.3 42.3 %all-gather.16.cloned.1.call-done = bf16[3072,768]{1,0:T(8,128)(2,1)} async-done(((bf16[384,768]{1,0:T(8,128)(2,1)}), bf16[3072,768]{1,0:T(8,128)(2,1)}) %all-gather.16.cloned.1.call-update) | async-done | bytes 4718608 | tf_op jit(solution)/shard_map/all_gather | solution.py:219
  1198.6 8.8 fusion.124
  1209.1 66.3 %all-gather.1 = f32[32,2,768]{2,1,0:T(2,128)S(1)} all-gather(f32[1,2,768]{2,1,0:T(2,128)S(1)} %divide_bitcast_fusion), channel_id=1, replica_groups=mesh['dp'=4,'fsdp'=8] {'dp','fsdp'}, dimensions={0}, use_global_device_ids=true | all-gather | bytes 202752 | tf_op jit(solution)/shard_map/all_gather | solution.py:237
  1282.6 2.0 scatter_custom_fusion.1
  1286.8 3.4 fusion.21
  1290.2 2.7 fusion.119
  1292.9 19.5 fusion.125
  1312.4 10.5 multiply_reduce_fusion.2
  1328.5 2.4 reshape.649
  1330.8 11.9 convolution_bitcast_fusion
  1342.7 20.2 multiply_reduce_fusion
  1362.9 21.7 multiply_convert_fusion
  1384.6 8.6 multiply_bitcast_fusion
  1393.2 7.7 multiply_bitcast_fusion.1
  1402.7 2.8 fusion.14
  1405.5 9.4 copy.98
  1415.0 4.1 copy.112
  1419.2 9.8 multiply_reduce_fusion.3
  1429.1 2.0 fusion.117
  1431.1 2.1 broadcast_add_fusion
  1433.2 3.4 reduce_sum.391
  1436.8 5.3 fusion.99
  1442.2 2.7 add_convert_fusion.1
  1444.9 8.4 fusion.126
  1455.3 10.7 fusion.22
  1467.9 10.7 fusion.98
  1478.7 30.2 broadcast_in_dim.125
  1508.9 130.9 %scatter_fusion = f32[30721,768]{1,0:T(8,128)} fusion(f32[30721,768]{1,0:T(8,128)} %broadcast_in_dim.125, s32[1024]{0:T(1024)S(1)} %bitcast.172, f32[1024,768]{1,0:T(8,128)S(1)} %copy-done.17), kind=kCustom, calls=%fused_computation.6 | custom fusion | flops 786432 | bytes 9441280 | tf_op jit(solution)/shard_map/scatter-add | solution.py:73
  1639.8 63.9 %slice.115 = f32[30720,768]{1,0:T(8,128)} slice(f32[30721,768]{1,0:T(8,128)} %scatter_fusion), slice={[0:30720], [0:768]} | slice | bytes 188743680 | tf_op jit(solution)/shard_map/slice | solution.py:73
  1704.7 2.3 add_reduce_fusion
  1707.1 2.6 add_reduce_fusion.1
  1717.0 153.1 %reduce-scatter.18.cloned.1.call-done = f32[96,3072]{1,0:T(8,128)} async-done(((f32[768,3072]{1,0:T(8,128)}), f32[96,3072]{1,0:T(8,128)}) %reduce-scatter.18.cloned.1.call-update) | async-done | bytes 1179664 | tf_op jit(solution)/shard_map/reduce_scatter | solution.py:258
  1870.1 2.2 convert_element_type.213
  1872.3 164.3 %reduce-scatter.20.cloned.1.call-done = f32[384,768]{1,0:T(8,128)} async-done(((f32[3072,768]{1,0:T(8,128)}), f32[384,768]{1,0:T(8,128)}) %reduce-scatter.20.cloned.1.call-update) | async-done | bytes 1179664 | tf_op jit(solution)/shard_map/reduce_scatter | solution.py:259
  2036.6 2.1 convert_element_type.215
  2038.7 1446.5 %reduce-scatter.10.cloned.1.call-done = f32[3840,768]{1,0:T(8,128)} async-done(((f32[30720,768]{1,0:T(8,128)}), f32[3840,768]{1,0:T(8,128)}) %reduce-scatter.10.cloned.1.call-update) | async-done | bytes 11796496 | tf_op jit(solution)/shard_map/reduce_scatter | solution.py:262
  3485.2 7.5 convert_element_type.202
  3492.8 57.1 %reduce-scatter.22.cloned.1.call-done = f32[96,14]{1,0:T(8,128)} async-done(((f32[768,14]{1,0:T(8,128)}), f32[96,14]{1,0:T(8,128)}) %reduce-scatter.22.cloned.1.call-update) | async-done | bytes 5392
  3550.7 5.7 psum.62
  3557.0 141.0 %all-reduce.3.cloned.1.call-done = (bf16[3840,768]{1,0:T(8,128)(2,1)}, bf16[64,768]{1,0:T(8,128)(2,1)}, bf16[96,2304]{1,0:T(8,128)(2,1)}, bf16[96,768]{1,0:T(8,1...) async-done(((bf16[3840,768]{1,0:T(8,128)(2,1)}, bf16[64,768]{1,0:T(8,128)(2,1)}, bf16[96,2304]{1,0:T(8,128)(2,1)}, bf16[96,768]{1,0:T(8,128)(2,1)}, ...) | async-done | bytes 7766032 | tf_op jit(solution)/shard_map/psum | solution.py:269
  3707.0 6.5 fusion.12
  3719.2 21.9 psum.63
  3743.2 2.0 multiply_add_fusion.10
  3745.2 2.0 multiply_add_fusion.9
  3750.4 2.2 multiply_add_fusion.7
  3753.8 2.1 multiply_add_fusion.6
  3756.0 26.9 multiply_add_fusion.2
  (329 shorter events, 64.7 us)
Async XLA Ops:
  7.2 919.1 %all-gather.8.cloned.1.call-start = ((), (), s32[]{:S(2)}) async-start(), calls=%async_computation.7 | async-start | bytes 53084160 | tf_op jit(solution)/shard_map/all_gather | solution.py:225
  14.8 979.5 %all-gather.10.cloned.1.call-start = ((), (), s32[]{:S(2)}) async-start(), calls=%async_computation.8 | async-start | bytes 3981312 | tf_op jit(solution)/shard_map/all_gather | solution.py:216
  16.7 110.0 %copy-start.100 = (s32[3,24]{1,0:T(4,128)S(1)}, s32[3,24]{1,0:T(4,128)}, u32[]{:S(2)}) copy-start(s32[3,24]{1,0:T(4,128)} %param.27) | copy-start | bytes 868
  16.7 113.7 %copy-start.45 = (f32[64,768]{1,0:T(8,128)S(1)}, f32[64,768]{1,0:T(8,128)}, u32[]{:S(2)}) copy-start(f32[64,768]{1,0:T(8,128)} %param.30) | copy-start | bytes 589828
  16.8 1043.6 %all-gather.12.cloned.1.call-start = ((), (), s32[]{:S(2)}) async-start(), calls=%async_computation.9 | async-start | bytes 1327104 | tf_op jit(solution)/shard_map/all_gather | solution.py:217
  17.5 1100.4 %all-gather.14.cloned.1.call-start = ((), (), s32[]{:S(2)}) async-start(), calls=%async_computation.10 | async-start | bytes 5308416 | tf_op jit(solution)/shard_map/all_gather | solution.py:218
  18.5 1180.1 %all-gather.16.cloned.1.call-start = ((), (), s32[]{:S(2)}) async-start(), calls=%async_computation.11 | async-start | bytes 5308416 | tf_op jit(solution)/shard_map/all_gather | solution.py:219
  19.4 1692.3 %reduce-scatter.12.cloned.1.call-start = ((), (), s32[]{:S(2)}) async-start(), calls=%async_computation.13 | async-start | bytes 1769472 | tf_op jit(solution)/shard_map/reduce_scatter | solution.py:255
  20.1 1025.2 %copy-start.47 = (f32[2,512]{1,0:T(2,128)}, f32[2,512]{1,0:T(2,128)S(1)}, u32[]{:S(2)}) copy-start(f32[2,512]{1,0:T(2,128)S(1)} %fusion.88) | copy-start | bytes 12292
  20.1 919.5 %copy-start.83 = (pred[2,512]{1,0:T(4,128)(4,1)}, pred[2,512]{1,0:T(4,128)(4,1)S(1)}, u32[]{:S(2)}) copy-start(pred[2,512]{1,0:T(4,128)(4,1)S(1)} %get-tuple-element.96) | copy-start | bytes 3076
  20.1 919.5 %copy-start.85 = (pred[2,512]{1,0:T(4,128)(4,1)}, pred[2,512]{1,0:T(4,128)(4,1)S(1)}, u32[]{:S(2)}) copy-start(pred[2,512]{1,0:T(4,128)(4,1)S(1)} %get-tuple-element.97) | copy-start | bytes 3076
  126.7 933.7 %copy-start.53 = (f32[768]{0:T(1024)}, f32[768]{0:T(1024)S(1)}, u32[]{:S(2)}) copy-start(f32[768]{0:T(1024)S(1)} %get-tuple-element.45) | copy-start | bytes 9220
  126.7 933.7 %copy-start.63 = (f32[768]{0:T(1024)}, f32[768]{0:T(1024)S(1)}, u32[]{:S(2)}) copy-start(f32[768]{0:T(1024)S(1)} %get-tuple-element.44) | copy-start | bytes 9220
  126.7 1071.9 %copy-start.57 = (f32[768]{0:T(1024)}, f32[768]{0:T(1024)S(1)}, u32[]{:S(2)}) copy-start(f32[768]{0:T(1024)S(1)} %get-tuple-element.39) | copy-start | bytes 9220
  129.1 931.3 %copy-start.81 = (pred[1024]{0:T(1024)(128)(4,1)}, pred[1024]{0:T(1024)(128)(4,1)S(1)}, u32[]{:S(2)}) copy-start(pred[1024]{0:T(1024)(128)(4,1)S(1)} %compare_and_fusion.2) | copy-start | bytes 3076
  129.8 930.6 %copy-start.65 = (pred[1024]{0:T(1024)(128)(4,1)}, pred[1024]{0:T(1024)(128)(4,1)S(1)}, u32[]{:S(2)}) copy-start(pred[1024]{0:T(1024)(128)(4,1)S(1)} %and.33) | copy-start | bytes 3076
  130.4 987.5 %copy-start.92 = (f32[3072]{0:T(1024)}, f32[3072]{0:T(1024)S(1)}, u32[]{:S(2)}) copy-start(f32[3072]{0:T(1024)S(1)} %add.392) | copy-start | bytes 36868
  177.5 882.9 %copy-start = (f32[512,768]{1,0:T(8,128)}, f32[512,768]{1,0:T(8,128)S(1)}, u32[]{:S(2)}) copy-start(f32[512,768]{1,0:T(8,128)S(1)} %convert_element_type.176) | copy-start | bytes 4718596
  939.7 120.8 %copy-start.2 = (bf16[1024,768]{1,0:T(8,128)(2,1)}, bf16[1024,768]{1,0:T(8,128)(2,1)S(1)}, u32[]{:S(2)}) copy-start(bf16[1024,768]{1,0:T(8,128)(2,1)S(1)} %gather_fusion) | copy-start | bytes 4718596
  940.5 119.9 %copy-start.49 = (f32[1024]{0:T(1024)}, f32[1024]{0:T(1024)S(1)}, u32[]{:S(2)}) copy-start(f32[1024]{0:T(1024)S(1)} %broadcast_multiply_fusion.2) | copy-start | bytes 12292
  941.8 60.9 %copy-start.70 = (f32[1024]{0:T(1024)}, f32[1024]{0:T(1024)S(1)}, u32[]{:S(2)}) copy-start(f32[1024]{0:T(1024)S(1)} %multiply_reduce_fusion.9) | copy-start | bytes 12292
  941.8 118.6 %copy-start.51 = (f32[1024]{0:T(1024)}, f32[1024]{0:T(1024)S(1)}, u32[]{:S(2)}) copy-start(f32[1024]{0:T(1024)S(1)} %fusion.89) | copy-start | bytes 12292
  1023.1 11.1 copy-start.18
  1023.1 11.0 copy-start.21
  1023.1 22.1 copy-start.24
  1045.2 11.9 copy-start.41
  1066.8 89.5 %copy-start.72 = (f32[1024]{0:T(1024)}, f32[1024]{0:T(1024)S(1)}, u32[]{:S(2)}) copy-start(f32[1024]{0:T(1024)S(1)} %multiply_reduce_fusion.8) | copy-start | bytes 12292
  1117.9 80.7 %copy-start.5 = (f32[1024,768]{1,0:T(8,128)S(1)}, f32[1024,768]{1,0:T(8,128)}, u32[]{:S(2)}) copy-start(f32[1024,768]{1,0:T(8,128)} %copy-done.4) | copy-start | bytes 9437188
  1275.5 11.2 copy-start.60
  1275.6 11.2 copy-start.62
  1275.6 11.2 copy-start.67
  1275.6 14.6 copy-start.75
  1285.8 4.4 copy-start.8
  1286.7 6.1 copy-start.55
  1312.4 10.6 copy-start.73
  1324.5 112.2 %copy-start.77 = (f32[1024]{0:T(1024)}, f32[1024]{0:T(1024)S(1)}, u32[]{:S(2)}) copy-start(f32[1024]{0:T(1024)S(1)} %negate_multiply_fusion.2) | copy-start | bytes 12292
  1342.7 58.2 %copy-start.11 = (f32[2,512,1,12,64]{1,4,3,0,2:T(8,128)}, f32[2,512,1,12,64]{1,4,3,0,2:T(8,128)S(1)}, u32[]{:S(2)}) copy-start(f32[2,512,1,12,64]{1,4,3,0,2:T(8,128)S(1)} %convolution_bitcast_fusion) | copy-start | bytes 9437188
  1362.9 21.7 copy-start.22
  1384.6 8.6 copy-start.19
  1393.2 7.8 copy-start.13
  1419.1 10.0 copy-start.20
  1419.2 9.9 copy-start.71
  1436.7 5.5 copy-start.64
  1436.7 5.5 copy-start.84
  1436.7 5.5 copy-start.86
  1436.7 276.6 %reduce-scatter.16.cloned.1.call-start = ((), (), s32[]{:S(2)}) async-start(), calls=%async_computation.15 | async-start | bytes 2654208 | tf_op jit(solution)/shard_map/reduce_scatter | solution.py:257
  1442.1 272.9 %reduce-scatter.14.cloned.1.call-start = ((), (), s32[]{:S(2)}) async-start(), calls=%async_computation.14 | async-start | bytes 7962624 | tf_op jit(solution)/shard_map/reduce_scatter | solution.py:256
  1453.4 416.8 %reduce-scatter.18.cloned.1.call-start = ((), (), s32[]{:S(2)}) async-start(), calls=%async_computation.16 | async-start | bytes 10616832 | tf_op jit(solution)/shard_map/reduce_scatter | solution.py:258
  1466.0 570.6 %reduce-scatter.20.cloned.1.call-start = ((), (), s32[]{:S(2)}) async-start(), calls=%async_computation.17 | async-start | bytes 10616832 | tf_op jit(solution)/shard_map/reduce_scatter | solution.py:259
  1478.6 2006.6 %reduce-scatter.10.cloned.1.call-start = ((), (), s32[]{:S(2)}) async-start(), calls=%async_computation.12 | async-start | bytes 106168320 | tf_op jit(solution)/shard_map/reduce_scatter | solution.py:262
  1478.7 30.2 copy-start.17
  1478.7 30.2 copy-start.91
  1703.7 6.0 copy-start.14
  1703.7 1846.2 %reduce-scatter.22.cloned.1.call-start = ((), (), s32[]{:S(2)}) async-start(), calls=%async_computation.18 | async-start | bytes 442368
  1704.7 4.9 copy-start.10
  1704.7 4.9 copy-start.12
  1711.6 1986.4 %all-reduce.3.cloned.1.call-start = ((), (), s32[]{:S(2)}) async-start(), calls=%async_computation.19 | async-start | bytes 15532032 | tf_op jit(solution)/shard_map/psum | solution.py:269
  3703.6 38.3 %copy-start.80 = (f32[14,96]{1,0:T(8,128)S(1)}, f32[14,96]{1,0:T(8,128)}, u32[]{:S(2)}) copy-start(f32[14,96]{1,0:T(8,128)} %param.35) | copy-start | bytes 16132
  3707.0 38.3 %copy-start.35 = (f32[96,768]{1,0:T(8,128)S(1)}, f32[96,768]{1,0:T(8,128)}, u32[]{:S(2)}) copy-start(f32[96,768]{1,0:T(8,128)} %param.32) | copy-start | bytes 884740
  3707.0 38.3 %copy-start.46 = (bf16[96,768]{1,0:T(8,128)(2,1)S(1)}, bf16[96,768]{1,0:T(8,128)(2,1)}, u32[]{:S(2)}) copy-start(bf16[96,768]{1,0:T(8,128)(2,1)} %get-tuple-element.49) | copy-start | bytes 442372
  3707.0 40.3 %copy-start.30 = (f32[96,2304]{1,0:T(8,128)S(1)}, f32[96,2304]{1,0:T(8,128)}, u32[]{:S(2)}) copy-start(f32[96,2304]{1,0:T(8,128)} %param.31) | copy-start | bytes 2654212
  3707.0 40.3 %copy-start.33 = (bf16[96,2304]{1,0:T(8,128)(2,1)S(1)}, bf16[96,2304]{1,0:T(8,128)(2,1)}, u32[]{:S(2)}) copy-start(bf16[96,2304]{1,0:T(8,128)(2,1)} %get-tuple-element.48) | copy-start | bytes 1327108
  3707.0 40.3 %copy-start.43 = (f32[96,2304]{1,0:T(8,128)S(1)}, f32[96,2304]{1,0:T(8,128)}, u32[]{:S(2)}) copy-start(f32[96,2304]{1,0:T(8,128)} %param.45) | copy-start | bytes 2654212
  3707.0 40.3 %copy-start.44 = (f32[96,2304]{1,0:T(8,128)S(1)}, f32[96,2304]{1,0:T(8,128)}, u32[]{:S(2)}) copy-start(f32[96,2304]{1,0:T(8,128)} %param.38) | copy-start | bytes 2654212
  (50 other events, 115.7 us)
Sparse Core Ops, SparseCore 0:
  14.9 911.3 all-gather.7
  929.1 65.1 all-gather.9
  997.0 39.5 all-gather.11
  1039.2 78.6 all-gather.13
  1120.5 78.0 all-gather.15
  1436.8 61.9 reduce-scatter.11
  1502.6 68.0 reduce-scatter.15
  1575.5 128.0 reduce-scatter.13
  1707.7 162.3 reduce-scatter.17
  1874.1 162.3 reduce-scatter.19
  2040.5 1444.7 reduce-scatter.9
  3489.3 60.5 reduce-scatter.21
  3554.5 143.4 all-reduce.2
where the time goes:
time: 3800 us; the launch traced here: 3790 us
  waiting for transfers between devices  2850 us (75%)
  other arithmetic  292 us (8%)
  blocking collectives  246 us (6%)
  matrix products  208 us (5%)
  local copies, waits for them, and re-layouts  168 us (4%)
    reduce_scatter x1, waiting for transfers between devices, shards(): lax.psum_scatter(add_into_rows(grad_x, flat_ids, own_rows * lax.axis_size...  1450 us
    all_gather x1, waiting for transfers between devices, shards(): lax.all_gather(word_low, 'fsdp', axis=0, tiled=True)  749 us
    reduce_scatter x1, waiting for transfers between devices, shards(): lax.psum_scatter(layer_grads[3], 'fsdp', scatter_dimension=0, tiled=True)  164 us
    reduce_scatter x1, waiting for transfers between devices, shards(): lax.psum_scatter(layer_grads[2], 'fsdp', scatter_dimension=0, tiled=True)  153 us
    psum x1, waiting for transfers between devices, shards(): lax.psum(grad_table.astype(jnp.bfloat16), 'dp').astype(jnp.float32)  141 us
    scatter-add x1, other arithmetic, add_into_rows(): return jax.ops.segment_sum(values, slots, num_segments=count + 1)[:count]  131 us
    all_gather x1, blocking collectives, shards(): lax.all_gather(small_low, 'fsdp', axis=1, tiled=True)  105 us
  transfers between devices with their start and end apart: 13, of which 9 were waited for; matrix products, arithmetic and copies ran while one was open for 11% of the time, Pallas kernels for 0%

commit v1 on v0

--- a/solution.py
+++ b/solution.py
@@ -1,8 +1,11 @@
+import functools
 import math
 
 import jax
 import jax.numpy as jnp
 from jax import lax
+from jax.experimental import pallas as pl
+from jax.experimental.pallas import tpu as pltpu
 from jax.sharding import PartitionSpec as P
 
 D = 768
@@ -60,17 +63,312 @@
     return jnp.sum(near * near) + jnp.sum(far * far)
 
 
-def take_rows(table, ids):
-    count = table.shape[0]
-    inside = (ids >= 0) & (ids < count)
-    rows = jnp.take(table, jnp.clip(ids, 0, count - 1), axis=0)
-    return jnp.where(inside[:, None], rows, jnp.zeros_like(rows))
-
-
-def add_into_rows(values, ids, count):
-    inside = (ids >= 0) & (ids < count)
-    slots = jnp.where(inside, ids, count)
-    return jax.ops.segment_sum(values, slots, num_segments=count + 1)[:count]
+MESH = pl.DeviceIdType.MESH
+
+
+def gather_kernel(sizes, whole, src, out, send, recv, local):
+    dp, fsdp = sizes
+    count = dp * fsdp if whole else fsdp
+    row, col = lax.axis_index("dp"), lax.axis_index("fsdp")
+    me = row * fsdp + col if whole else col
+
+    def target(step):
+        other = lax.rem(me + step, count)
+        return (other // fsdp, lax.rem(other, fsdp)) if whole else (row, other)
+
+    barrier = pltpu.get_barrier_semaphore()
+
+    def greet(step, carry):
+        pl.semaphore_signal(barrier, inc=1, device_id=target(step), device_id_type=MESH)
+        return carry
+
+    lax.fori_loop(1, count, greet, 0)
+    pl.semaphore_wait(barrier, count - 1)
+    own = pltpu.make_async_copy(src, out.at[me], local)
+    own.start()
+
+    def copy(step):
+        return pltpu.make_async_remote_copy(
+            src_ref=src,
+            dst_ref=out.at[me],
+            send_sem=send.at[step],
+            recv_sem=recv.at[step],
+            device_id=target(step),
+            device_id_type=MESH,
+        )
+
+    def begin(step, carry):
+        copy(step).start()
+        return carry
+
+    def end(step, carry):
+        copy(step).wait()
+        return carry
+
+    lax.fori_loop(1, count, begin, 0)
+    lax.fori_loop(1, count, end, 0)
+    own.wait()
+
+
+def gather_small(value, whole, collective):
+    dp, fsdp = lax.axis_size("dp"), lax.axis_size("fsdp")
+    count = dp * fsdp if whole else fsdp
+    return pl.pallas_call(
+        functools.partial(gather_kernel, (dp, fsdp), whole),
+        out_shape=jax.ShapeDtypeStruct((count,) + value.shape, value.dtype),
+        in_specs=[pl.BlockSpec(memory_space=pltpu.VMEM)],
+        out_specs=pl.BlockSpec(memory_space=pltpu.VMEM),
+        scratch_shapes=[
+            pltpu.SemaphoreType.DMA((count,)),
+            pltpu.SemaphoreType.DMA((count,)),
+            pltpu.SemaphoreType.DMA,
+        ],
+        compiler_params=pltpu.CompilerParams(collective_id=collective, has_side_effects=True),
+    )(value)
+
+
+LOOP = {8: (0, 2, 4, 6, 7, 5, 3, 1)}
+
+
+def swap_core(value):
+    return lax.ppermute(value, "dp", [(i, i ^ 1) for i in range(lax.axis_size("dp"))])
+
+
+def swap_x(value):
+    count = lax.axis_size("dp")
+    return lax.ppermute(value, "dp", [(i, (i + 2) % count) for i in range(count)])
+
+
+def sum_x(value):
+    count = lax.axis_size("dp")
+    total = value
+    for hop in range(2, count, 2):
+        moved = lax.ppermute(value, "dp", [(i, (i + hop) % count) for i in range(count)])
+        total = total.astype(jnp.float32) + moved.astype(jnp.float32)
+    return total
+
+
+def shift(value, step):
+    loop = LOOP[lax.axis_size("fsdp")]
+    size = len(loop)
+    return lax.ppermute(
+        value, "fsdp", [(loop[i], loop[(i + step) % size]) for i in range(size)]
+    )
+
+
+def loop_place():
+    loop = LOOP[lax.axis_size("fsdp")]
+    place = [0] * len(loop)
+    for i, device in enumerate(loop):
+        place[device] = i
+    return jnp.array(place, jnp.int32)[lax.axis_index("fsdp")], jnp.array(loop, jnp.int32)
+
+
+def ring_gather(part, sign):
+    size = lax.axis_size("fsdp")
+    place, loop = loop_place()
+    out = jnp.zeros((size,) + part.shape, part.dtype)
+
+    def put(out, block, offset):
+        at = loop[lax.rem(place + offset + size, size)]
+        return lax.dynamic_update_slice(out, block[None], (at, 0, 0))
+
+    out = put(out, part, 0)
+    ahead = behind = part
+    for hop in range(1, size // 2 + 1):
+        ahead = shift(ahead, sign)
+        out = put(out, ahead, -sign * hop)
+        if hop < size - size // 2:
+            behind = shift(behind, -sign)
+            out = put(out, behind, sign * hop)
+    return out
+
+
+def ring_reduce(parts, sign):
+    size = lax.axis_size("fsdp")
+    place, loop = loop_place()
+
+    def local(offset):
+        at = loop[lax.rem(place + offset + size, size)]
+        return lax.dynamic_index_in_dim(parts, at, 0, keepdims=False).astype(jnp.float32)
+
+    def flow(direction, hops):
+        arrived = None
+        for hop in range(hops):
+            value = local(direction * (hops - hop))
+            if arrived is not None:
+                value = value + arrived.astype(jnp.float32)
+            arrived = shift(value.astype(jnp.bfloat16), direction)
+        return arrived
+
+    far = flow(sign, size // 2)
+    near = flow(-sign, size - size // 2 - 1)
+    return local(0) + far.astype(jnp.float32) + near.astype(jnp.float32)
+
+
+def gather_halves(first, second, sign):
+    core = lax.rem(lax.axis_index("dp"), 2)
+    if lax.axis_size("fsdp") not in LOOP:
+        return lax.all_gather(first, "fsdp", axis=0), lax.all_gather(second, "fsdp", axis=0)
+    mine = ring_gather(jnp.where(core == 0, first, second), sign)
+    other = swap_core(mine)
+    return jnp.where(core == 0, mine, other), jnp.where(core == 0, other, mine)
+
+
+def reduce_halves(first, second, sign):
+    core = lax.rem(lax.axis_index("dp"), 2)
+    give = jnp.where(core == 0, second, first).astype(jnp.bfloat16)
+    keep = jnp.where(core == 0, first, second).astype(jnp.float32)
+    chip = (keep + swap_core(give).astype(jnp.float32)).astype(jnp.bfloat16)
+    if lax.axis_size("fsdp") in LOOP:
+        block = ring_reduce(chip, sign)
+    else:
+        block = lax.psum_scatter(chip.astype(jnp.float32), "fsdp", scatter_dimension=0)
+    total = sum_x(block.astype(jnp.bfloat16)).astype(jnp.bfloat16)
+    other = swap_core(total)
+    low = jnp.where(core == 0, total, other).astype(jnp.float32)
+    high = jnp.where(core == 0, other, total).astype(jnp.float32)
+    return low, high
+
+
+def split_rows(weight, parts):
+    return jnp.concatenate(jnp.split(weight, parts, axis=1), axis=0)
+
+
+def join_rows(blocks, parts):
+    count, rows, width = blocks.shape
+    return (
+        blocks.reshape(count, parts, rows // parts, width)
+        .transpose(0, 2, 1, 3)
+        .reshape(count * rows // parts, parts * width)
+    )
+
+
+def cut_rows(grad, count, parts):
+    rows, width = grad.shape[0] // count, grad.shape[1] // parts
+    return (
+        grad.reshape(count, rows, parts, width)
+        .transpose(0, 2, 1, 3)
+        .reshape(count, parts * rows, width)
+    )
+
+
+def pad_rows(value, rows):
+    return jnp.pad(value, [(0, 0)] * (value.ndim - 2) + [(0, rows - value.shape[-2]), (0, 0)])
+
+
+def round_up(value, step):
+    return -(-value // step) * step
+
+
+def bucket_size(tokens, owners):
+    mean = tokens / owners
+    return min(tokens, round_up(int(mean + 5.6 * math.sqrt(mean)), 16))
+
+
+def one_hot(index, count):
+    return (index[:, None] == lax.iota(jnp.int32, count)[None, :]).astype(jnp.bfloat16)
+
+
+class Routes:
+    def __init__(self, everyone, own_rows):
+        fsdp = lax.axis_size("fsdp")
+        self.rows = own_rows
+        tokens = everyone.shape[1]
+        self.cap = bucket_size(tokens, fsdp)
+        me = lax.axis_index("fsdp")
+        group = lax.dynamic_slice_in_dim(everyone, lax.axis_index("dp") * fsdp, fsdp, 0)
+        mine = lax.dynamic_index_in_dim(group, me, 0, keepdims=False)
+        owners = lax.iota(jnp.int32, fsdp)
+        every_count = jnp.sum(
+            (everyone // own_rows)[:, :, None] == owners[None, None, :], 1, dtype=jnp.int32
+        )
+        self.rounds = (jnp.max(every_count) + self.cap - 1) // self.cap
+        self.inner = group - me * own_rows
+        self.held = (self.inner >= 0) & (self.inner < own_rows)
+        self.held_place = jnp.cumsum(self.held.astype(jnp.int32), 1) - 1
+        self.owner = mine // own_rows
+        hot = (self.owner[None, :] == owners[:, None])
+        place = jnp.cumsum(hot.astype(jnp.int32), 1) - 1
+        self.hot = hot
+        self.place = place
+        self.my_place = jnp.sum(jnp.where(hot, place, 0), 0)
+
+    def slots(self, flag, place, value, turn):
+        slot = lax.iota(jnp.int32, self.cap)[None, :, None] + turn * self.cap
+        hit = flag[:, None, :] & (place[:, None, :] == slot)
+        return (jnp.sum(jnp.where(hit, value[:, None, :] + 1, 0), -1) - 1).reshape(-1)
+
+    def owner_rows(self, turn):
+        return self.slots(self.held, self.held_place, self.inner, turn)
+
+    def asker_tokens(self, turn):
+        tokens = lax.iota(jnp.int32, self.owner.shape[0])[None, :]
+        return self.slots(self.hot, self.place, tokens, turn)
+
+    def asker_slots(self, turn):
+        place = self.my_place - turn * self.cap
+        inside = (place >= 0) & (place < self.cap)
+        return jnp.where(inside, self.owner * self.cap + place, -1)
+
+
+def exchange(rows):
+    fsdp = lax.axis_size("fsdp")
+    blocks = rows.reshape(fsdp, rows.shape[0] // fsdp, rows.shape[1])
+    return lax.all_to_all(blocks, "fsdp", 0, 0).reshape(rows.shape)
+
+
+def fetch_round(table_low, routes, turn):
+    sent = matmul(one_hot(routes.owner_rows(turn), routes.rows), table_low).astype(jnp.bfloat16)
+    got = exchange(sent)
+    return matmul(one_hot(routes.asker_slots(turn), got.shape[0]), got)
+
+
+def fetch_rows(table_low, routes):
+    first = fetch_round(table_low, routes, 0)
+
+    def more(carry):
+        return carry[0] < routes.rounds
+
+    def body(carry):
+        turn, words = carry
+        return turn + 1, words + fetch_round(table_low, routes, turn)
+
+    return lax.while_loop(more, body, (jnp.int32(1), first))[1]
+
+
+def return_round(grad_low, routes, turn):
+    tokens = grad_low.shape[0]
+    sent = matmul(one_hot(routes.asker_tokens(turn), tokens), grad_low).astype(jnp.bfloat16)
+    got = exchange(sent)
+    return outer_sum(one_hot(routes.owner_rows(turn), routes.rows), got)
+
+
+def return_rows(grad_low, routes):
+    first = return_round(grad_low, routes, 0)
+
+    def more(carry):
+        return carry[0] < routes.rounds
+
+    def body(carry):
+        turn, total = carry
+        return turn + 1, total + return_round(grad_low, routes, turn)
+
+    return lax.while_loop(more, body, (jnp.int32(1), first))[1]
+
+
+def sum_groups(table):
+    core = lax.rem(lax.axis_index("dp"), 2)
+    half = table.shape[0] // 2
+    low = table.astype(jnp.bfloat16)
+    keep = lax.dynamic_slice_in_dim(table, core * half, half, 0)
+    give = lax.dynamic_slice_in_dim(low, (1 - core) * half, half, 0)
+    chip = (keep + swap_core(give).astype(jnp.float32)).astype(jnp.bfloat16)
+    total = sum_x(chip).astype(jnp.bfloat16)
+    other = swap_core(total)
+    return jnp.concatenate(
+        [jnp.where(core == 0, total, other), jnp.where(core == 0, other, total)], 0
+    ).astype(jnp.float32)
 
 
 def attention_logits(query, keys, live_bias, scale):
@@ -204,28 +502,46 @@
 ):
     batch, seq = token_ids.shape
     width = D
+    fsdp = lax.axis_size("fsdp")
+    me = lax.axis_index("fsdp")
     pos_low = pos_table.astype(jnp.bfloat16)
-    qkv_low = qkv_weight.astype(jnp.bfloat16)
+    qkv_low = split_rows(qkv_weight.astype(jnp.bfloat16), 3)
     out_low = out_weight.astype(jnp.bfloat16)
-    up_low = up_weight.astype(jnp.bfloat16)
+    up_low = split_rows(up_weight.astype(jnp.bfloat16), 4)
     down_low = down_weight.astype(jnp.bfloat16)
     small_low = small_params.astype(jnp.bfloat16)
     word_low = word_table.astype(jnp.bfloat16)
-    gathered = (
-        lax.all_gather(pos_low, "fsdp", axis=0, tiled=True),
-        lax.all_gather(qkv_low, "fsdp", axis=0, tiled=True),
-        lax.all_gather(out_low, "fsdp", axis=0, tiled=True),
-        lax.all_gather(up_low, "fsdp", axis=0, tiled=True),
-        lax.all_gather(down_low, "fsdp", axis=0, tiled=True),
-        lax.all_gather(small_low, "fsdp", axis=1, tiled=True),
-    )
-    params = (gathered[1], gathered[2], gathered[3], gathered[4], gathered[5].astype(jnp.float32))
-    flat_ids = token_ids.reshape(-1)
-    own_rows = word_table.shape[0]
-    words = take_rows(lax.all_gather(word_low, "fsdp", axis=0, tiled=True), flat_ids).astype(
-        jnp.float32
-    )
-    x = (words.reshape(batch, seq, width) + gathered[0].astype(jnp.float32)[None]).reshape(
+    tokens = batch * seq
+    everyone = gather_small(token_ids.reshape(-1, 128), True, 0).reshape(-1, tokens)
+    routes = Routes(everyone, word_table.shape[0])
+    shard = qkv_weight.shape[0]
+    pos_rows = pos_table.shape[0]
+    small_cols = small_params.shape[1]
+    small_block = jnp.pad(small_low, ((0, 2), (0, width - small_cols)))
+    tail = round_up(max(2 * shard, shard + pos_rows + 16), 16)
+    first_a = pad_rows(qkv_low[: 2 * shard], tail)
+    first_b = pad_rows(jnp.concatenate([qkv_low[2 * shard :], pos_low, small_block], 0), tail)
+    half = shard // 2
+    second_a = jnp.concatenate([down_low, out_low[:half]], 0)
+    second_b = jnp.concatenate([up_low, out_low[half:]], 0)
+    got_a, got_b = gather_halves(first_a, first_b, 1)
+    words = fetch_rows(word_low, routes)
+    got_c, got_d = gather_halves(second_a, second_b, -1)
+    qkv_full = join_rows(
+        jnp.concatenate([got_a[:, : 2 * shard], got_b[:, :shard]], 1), 3
+    )
+    pos_full = got_b[:, shard : shard + pos_rows].reshape(-1, width)
+    small_full = (
+        got_b[:, shard + pos_rows : shard + pos_rows + 14, :small_cols]
+        .transpose(1, 0, 2)
+        .reshape(14, width)
+    )
+    down_rows = down_weight.shape[0]
+    down_full = got_c[:, :down_rows].reshape(-1, width)
+    up_full = join_rows(got_d[:, :down_rows], 4)
+    out_full = jnp.concatenate([got_c[:, down_rows:], got_d[:, down_rows:]], 1).reshape(-1, width)
+    params = (qkv_full, out_full, up_full, down_full, small_full.astype(jnp.float32))
+    x = (words.reshape(batch, seq, width) + pos_full.astype(jnp.float32)[None]).reshape(
         -1, width
     )
     live = lax.iota(jnp.int32, seq)[None, :] < lengths[:, None]
@@ -234,50 +550,58 @@
     counts = lengths.astype(jnp.float32)
     h2, kept = layer_forward(x, params, live_bias, batch, seq)
     pooled = jnp.sum(h2.reshape(batch, seq, width) * live_f[:, :, None], 1) / counts[:, None]
-    everyone = lax.all_gather(pooled, ("dp", "fsdp"), axis=0, tiled=True)
-    loss, pull_loss = jax.vjp(lambda rows: pair_loss(rows, pair_ids, scores), everyone)
+    pooled_all = gather_small(pooled.reshape(-1, 128), True, 1).reshape(-1, width)
+    loss, pull_loss = jax.vjp(lambda rows: pair_loss(rows, pair_ids, scores), pooled_all)
     grad_all = pull_loss(jnp.ones((), jnp.float32))[0]
     grad_pooled = lax.dynamic_slice_in_dim(
         grad_all, lax.axis_index(("dp", "fsdp")) * batch, batch, 0
     )
     grad_h2 = (live_f[:, :, None] * (grad_pooled / counts[:, None])[:, None, :]).reshape(-1, width)
-    again = (
-        lax.all_gather(qkv_low, "fsdp", axis=0, tiled=True),
-        lax.all_gather(out_low, "fsdp", axis=0, tiled=True),
-        lax.all_gather(up_low, "fsdp", axis=0, tiled=True),
-        lax.all_gather(down_low, "fsdp", axis=0, tiled=True),
-        lax.all_gather(small_low, "fsdp", axis=1, tiled=True),
-    )
-    back_params = (again[0], again[1], again[2], again[3], again[4].astype(jnp.float32))
-    grad_x, layer_grads = layer_backward(grad_h2, kept, back_params, live_bias)
+    grad_x, layer_grads = layer_backward(grad_h2, kept, params, live_bias)
+    grad_qkvw, grad_outw, grad_upw, grad_downw, grad_small = layer_grads
+    sum_down, sum_up = reduce_halves(
+        cut_rows(grad_downw, fsdp, 1), cut_rows(grad_upw, fsdp, 4), 1
+    )
+    grad_table = return_rows(grad_x.astype(jnp.bfloat16), routes)
     grad_pos = jnp.sum(grad_x.reshape(batch, seq, width), 0)
-    reduced = (
-        lax.psum_scatter(grad_pos, "fsdp", scatter_dimension=0, tiled=True),
-        lax.psum_scatter(layer_grads[0], "fsdp", scatter_dimension=0, tiled=True),
-        lax.psum_scatter(layer_grads[1], "fsdp", scatter_dimension=0, tiled=True),
-        lax.psum_scatter(layer_grads[2], "fsdp", scatter_dimension=0, tiled=True),
-        lax.psum_scatter(layer_grads[3], "fsdp", scatter_dimension=0, tiled=True),
-        lax.psum_scatter(layer_grads[4], "fsdp", scatter_dimension=1, tiled=True),
-    )
-    grad_table = lax.psum_scatter(
-        add_into_rows(grad_x, flat_ids, own_rows * lax.axis_size("fsdp")),
-        "fsdp",
-        scatter_dimension=0,
-        tiled=True,
-    )
+    qkv_cut = cut_rows(grad_qkvw, fsdp, 3)
+    small_cut = jnp.pad(
+        grad_small.reshape(14, fsdp, small_cols).transpose(1, 0, 2),
+        ((0, 0), (0, 2), (0, width - small_cols)),
+    )
+    half_pos = pos_rows // 2
+    pos_cut = grad_pos.reshape(fsdp, pos_rows, width)
+    low_cut = jnp.concatenate([qkv_cut[:, : 2 * shard], pos_cut[:, :half_pos], small_cut], 1)
+    high_cut = pad_rows(
+        jnp.concatenate(
+            [qkv_cut[:, 2 * shard :], cut_rows(grad_outw, fsdp, 1), pos_cut[:, half_pos:]], 1
+        ),
+        low_cut.shape[1],
+    )
+    sum_low, sum_high = reduce_halves(low_cut, high_cut, -1)
+    sum_qkv = join_rows(
+        jnp.concatenate([sum_low[: 2 * shard], sum_high[:shard]], 0)[None], 3
+    )
+    sum_out = sum_high[shard : 2 * shard]
+    sum_pos = jnp.concatenate(
+        [sum_low[2 * shard : 2 * shard + half_pos], sum_high[2 * shard : 2 * shard + half_pos]], 0
+    )
+    small_at = 2 * shard + half_pos
+    sum_small = sum_low[small_at : small_at + 14, :small_cols]
+    sum_upw = join_rows(sum_up[None], 4)
     summed = (
-        lax.psum(grad_table.astype(jnp.bfloat16), "dp").astype(jnp.float32),
-        lax.psum(reduced[0].astype(jnp.bfloat16), "dp").astype(jnp.float32),
-        lax.psum(reduced[1].astype(jnp.bfloat16), "dp").astype(jnp.float32),
-        lax.psum(reduced[2].astype(jnp.bfloat16), "dp").astype(jnp.float32),
-        lax.psum(reduced[3].astype(jnp.bfloat16), "dp").astype(jnp.float32),
-        lax.psum(reduced[4].astype(jnp.bfloat16), "dp").astype(jnp.float32),
-        lax.psum(reduced[5].astype(jnp.bfloat16), "dp").astype(jnp.float32),
+        sum_groups(grad_table),
+        sum_pos,
+        sum_qkv,
+        sum_out,
+        sum_upw,
+        sum_down,
+        sum_small,
     )
     local_squares = jnp.zeros((), jnp.float32)
     for grad in summed:
         local_squares = local_squares + jnp.sum(grad * grad)
-    total = lax.psum(local_squares, "fsdp")
+    total = jnp.sum(gather_small(jnp.full((8, 128), local_squares), False, 2)[:, 0, 0])
     norm = jnp.sqrt(total)
     limit = 1e-05 * math.sqrt((VOCAB + LEN + 4 * D + 2 * FF + 14) * D)
     factor = jnp.minimum(1.0, limit / (norm + 1e-06))

time: 3800 us -> 900 us (0.24)
  waiting for transfers between devices: 2850 us -> 142 us
  blocking collectives: 246 us -> 0 us
  other arithmetic: 292 us -> 211 us
  starting transfers between devices: 0.54 us -> 56.7 us
    reduce_scatter x6 -> x0, waiting for transfers between devices: 1760 us -> none  [the longest x1 1450 us: shards(): lax.psum_scatter(add_into_rows(grad_x, flat_ids, own_rows * lax.axis_size...]
    all_gather x5 -> x0, waiting for transfers between devices: 891 us -> none  [the longest x1 749 us: shards(): lax.all_gather(word_low, 'fsdp', axis=0, tiled=True)]
    all_gather x3 -> x0, blocking collectives: 218 us -> none  [the longest x1 105 us: shards(): lax.all_gather(small_low, 'fsdp', axis=1, tiled=True)]
    ppermute x0 -> x39, waiting for transfers between devices: none -> 142 us  [the longest x28 121 us: shift(): lax.ppermute(value, 'fsdp', [(loop[i], loop[(i + step) % size]) for i in...]
    psum x1 -> x0, waiting for transfers between devices: 141 us -> none  [shards(): lax.psum(grad_table.astype(jnp.bfloat16), 'dp').astype(jnp.float32)]
    scatter-add x1 -> x0, other arithmetic: 131 us -> none  [add_into_rows(): return jax.ops.segment_sum(values, slots, num_segments=count + 1)[:count]]
    unnamed x14 -> x0, waiting for transfers between devices: 57.3 us -> none
    slice x1 -> x14, local copies, waits for them, and re-layouts: 63.9 us -> 14.4 us  [the longest x1 2.83 us: shards(): up_full = join_rows(got_d[:, :down_rows], 4)]
  transfers between devices with their start and end apart: 13 -> 41, of which waited for: 9 -> 15; matrix products, arithmetic and copies ran while one was open for 11% -> 34% of each run, Pallas kernels for 0% -> 2%
where the time goes in v1:
time: 900 us; the launch traced here: 886 us
  matrix products  230 us (26%)
  other arithmetic  211 us (23%)
  local copies, waits for them, and re-layouts  177 us (20%)
  waiting for transfers between devices  142 us (16%)
  starting transfers between devices  56.7 us (6%)
  between operations  35.8 us (4%)
  Pallas kernels  32.8 us (4%)
    ppermute x28, waiting for transfers between devices, shift(): lax.ppermute(value, 'fsdp', [(loop[i], loop[(i + step) % size]) for i in...  121 us
    dot_general x7, matrix products, matmul(): return jnp.dot(left, right, preferred_element_type=jnp.float32)  71.8 us
    dot_general x5, matrix products, outer_sum(): lax.dot_general(left, right, (((0,), (0,)), ((), ())), preferred_element_...  54.2 us
    ppermute x28, starting transfers between devices, shift(): lax.ppermute(value, 'fsdp', [(loop[i], loop[(i + step) % size]) for i in...  42.8 us
    unnamed x319, local copies, waits for them, and re-layouts  39.1 us
    add x7, other arithmetic, renew(): return (fresh, buffer, KEEP * average + (1.0 - KEEP) * fresh)  38.7 us
    dot_general x4, matrix products, back_mul(): lax.dot_general(grad, weight, (((1,), (1,)), ((), ())), preferred_element...  37.2 us
    pallas_call x3, Pallas kernels, gather_small(): pl.pallas_call(functools.partial(gather_kernel, (dp, fsdp), whole), out_s...  32.8 us
  transfers between devices with their start and end apart: 41, of which 15 were waited for; matrix products, arithmetic and copies ran while one was open for 34% of the time, Pallas kernels for 2%

profile of v1, /device:TPU:0, one launch (start us, length us, event | category | flops | bytes accessed | tf_op | source)
XLA Modules:
  0.0 886.1 jit_solution(7848240855132557741)
XLA Ops:
  24.0 13.3 %shard_map.488 = s32[32,8,128]{2,1,0:T(8,128)} custom-call(s32[8,128]{1,0:T(8,128)} %reshape.896.src), custom_call_target="tpu_custom_call" | custom-call | tf_op jit(solution)/shard_map/pallas_call | solution.py:116
  50.8 5.1 reduce-window.14
  60.5 5.1 reduce-window.16
  75.6 5.0 convert_element_type.380
  83.2 11.5 %fusion.40 = bf16[1536,768]{1,0:T(8,128)(2,1)} fusion(bf16[3840,768]{1,0:T(8,128)(2,1)S(1)} %convert_element_type.380, s32[1536]{0:T(1024)S(1)} %copy-done.121), kind=kOutput, calls=%fused_computation.108 | convolution fusion | flops 9066774528 | bytes 8263680 | tf_op jit(solution)/shard_map/dot_general | solution.py:35
  116.7 5.2 collective-permute-done.2
  124.6 5.5 collective-permute-done.4
  130.7 4.8 all-to-all-start.2
  159.6 30.5 %collective-permute-done.11 = bf16[432,768]{1,0:T(8,128)(2,1)} collective-permute-done((bf16[432,768]{1,0:T(8,128)(2,1)}, bf16[432,768]{1,0:T(8,128)(2,1)}, u32[]{:S(2)}, u32[]{:S(2)}) %collective-permute-start.11) | collective-permute-done | bytes 663584 | tf_op jit(solution)/shard_map/ppermute | solution.py:154
  190.2 12.8 %collective-permute-start.13 = (bf16[432,768]{1,0:T(8,128)(2,1)}, bf16[432,768]{1,0:T(8,128)(2,1)S(1)}, u32[]{:S(2)}, u32[]{:S(2)}) collective-permute-start(bf16[432,768]{1,0:T(8,128)(2,1)} %collective-permute-done.11), channel_id=1, source_target_pairs={{0,2},{2,4},{4,6},{6,7},{7,5},{5,3},{3,1},{1,0},{8,10},{10,12},{12... | collective-permute-start | bytes 1990664 | tf_op jit(solution)/shard_map/ppermute | solution.py:154
  206.8 10.0 %collective-permute-done.13 = bf16[432,768]{1,0:T(8,128)(2,1)S(1)} collective-permute-done((bf16[432,768]{1,0:T(8,128)(2,1)}, bf16[432,768]{1,0:T(8,128)(2,1)S(1)}, u32[]{:S(2)}, u32[]{:S(2)}) %collective-permute-start.13) | collective-permute-done | bytes 663584 | tf_op jit(solution)/shard_map/ppermute | solution.py:154
  217.7 7.0 collective-permute-done.14
  229.7 4.7 copy.126
  234.4 8.2 reshape.904
  248.6 6.2 fusion.36
  261.6 5.7 add_convert_fusion
  267.3 6.6 copy.127
  273.9 8.8 reshape.905
  282.8 4.9 fusion.143
  287.7 11.1 %fusion.16 = (f32[2,12,512]{2,1,0:T(8,128)S(1)}, f32[2,12,512,512]{2,3,1,0:T(8,128)}) fusion(f32[2,512]{1,0:T(2,128)S(1)} %copy-done.83, bf16[2,512,1,12,64]{1,0,4,3,2:T(2,128)(2,1)S(1)} %get-tuple-element.422, bf16[2,512,1,12,64]{1,0,4,3,2:T(2,128)(2,1)S(1)} %get-tuple-element.423), kind=kOutput, calls=%fused_computation.43 | convolution fusion | flops 824168448 | bytes 28364800 | tf_op jit(solution)/shard_map/bqhd,bkhd->bhqk/dot_general | solution.py:375
  298.8 11.0 %exponential_reduce_fusion = f32[2,12,512]{2,1,0:T(8,128)S(1)} fusion(f32[2,12,512,512]{2,3,1,0:T(8,128)} %get-tuple-element.474, f32[2,12,512]{2,1,0:T(8,128)S(1)} %get-tuple-element.473, f32[2,512]{1,0:T(2,128)S(1)} %copy-done.83), kind=kLoop, calls=%fused_computation.38 | loop fusion | flops 25153536 | bytes 25268224 | tf_op jit(solution)/shard_map/reduce_sum | solution.py:391
  309.9 11.3 %fusion.62 = bf16[2,512,12,64]{1,3,2,0:T(8,128)(2,1)S(1)} fusion(bf16[2,512,1,12,64]{1,0,4,3,2:T(2,128)(2,1)S(1)} %get-tuple-element.424, f32[2,12,512,512]{2,3,1,0:T(8,128)} %get-tuple-element.474, f32[2,12,512]{2,1,0:T(8,128)S(1)} %log_add_fusion, f32[2,512]{1,0:T(2,128)S(1)} %copy-done.83), kind=kOutput, calls=%fused_computation.163 | convolution fusion | flops 831258624 | bytes 28364800 | tf_op jit(solution)/shard_map/bhqk,bkhd->bqhd/dot_general | solution.py:393
  324.4 8.9 %broadcast_select_fusion.1 = (bf16[8,432,768]{2,1,0:T(8,128)(2,1)}, bf16[8,432,768]{2,1,0:T(8,128)(2,1)}) fusion(bf16[8,432,768]{2,1,0:T(8,128)(2,1)} %bitcast_dynamic-update-slice_fusion, bf16[8,432,768]{2,1,0:T(8,128)(2,1)} %collective-permute-done.15, pred[]{:T(512)S(6)} %eq.307), kind=kLoop, calls=%fused_computation.103 | loop fusion | flops 5308416 | bytes 21233664 | tf_op jit(solution)/shard_map/jit(_where)/select_n | solution.py:215
  343.7 3.6 copy.133
  348.6 35.4 %multiply_convert_fusion.1 = (bf16[1024,3072]{1,0:T(8,128)(2,1)S(1)}, f32[1024,3072]{1,0:T(8,128)}, f32[1024,3072]{1,0:T(8,128)}) fusion(f32[3072]{0:T(1024)S(1)} %copy-done.118, bf16[768,3072]{1,0:T(8,128)(2,1)S(1)} %bitcast.370, f32[1024,768]{1,0:T(8,128)S(1)} %get-tuple-element.476, f32[768]{0:T(1024)S(1)} %copy-done.93, f32[768]{0:T(1024)S(1)} %copy-done.90, ...), kind=kOutput, calls=%fused_computation.52 | convolution fusion | flops 5043388416 | bytes 39348224 | tf_op jit(solution)/shard_map/dot_general | solution.py:35
  384.0 5.4 fusion.150
  391.8 11.7 %shard_map.489 = f32[32,12,128]{2,1,0:T(8,128)} custom-call(f32[12,128]{1,0:T(8,128)} %broadcast_divide_fusion.src), custom_call_target="tpu_custom_call" | custom-call | tf_op jit(solution)/shard_map/pallas_call | solution.py:116
  417.5 11.9 %fusion.126 = f32[3072,768]{1,0:T(8,128)} fusion(bf16[1024,3072]{1,0:T(8,128)(2,1)} %copy-done.139, f32[1024,768]{1,0:T(8,128)S(1)} %get-tuple-element.394, f32[1024]{0:T(1024)S(1)} %negate_multiply_fusion.3), kind=kOutput, calls=%fused_computation.393 | convolution fusion | flops 4833411072 | bytes 18878464 | tf_op jit(solution)/shard_map/dot_general | solution.py:39
  429.5 19.0 %fusion.151 = (f32[3072]{0:T(1024)S(1)}, bf16[1024,3072]{1,0:T(8,128)(2,1)}) fusion(f32[1024,3072]{1,0:T(8,128)} %get-tuple-element.401, bf16[3072,768]{1,0:T(8,128)(2,1)} %bitcast.366, f32[1024,768]{1,0:T(8,128)} %copy-done.16, f32[1024]{0:T(1024)S(1)} %negate_multiply_fusion.3, f32[1024,3072]{1,0:T(8,128)} %get-tuple-element.477, f32[3072]{0:T(1024)S(1)} %copy-done.118), kind=kOutput, calls=%fused_computation.409 | convolution fusion | flops 4883739648 | bytes 39350272 | tf_op jit(solution)/shard_map/dot_general | solution.py:45
  448.4 11.2 %fusion.48 = f32[768,3072]{1,0:T(8,128)} fusion(bf16[1024,3072]{1,0:T(8,128)(2,1)} %get-tuple-element.485, f32[1024,768]{1,0:T(8,128)S(1)} %copy-done.2, f32[768]{0:T(1024)S(1)} %copy-done.93, f32[768]{0:T(1024)S(1)} %copy-done.90, f32[1024]{0:T(1024)S(1)} %fusion.118, f32[1024]{0:T(1024)S(1)} %broadcast_multiply_fusion.1), kind=kOutput, calls=%fused_computation.125 | convolution fusion | flops 4835770368 | bytes 18888704 | tf_op jit(solution)/shard_map/dot_general | solution.py:39
  459.7 8.4 multiply_reduce_fusion.2
  477.3 21.7 %multiply_reduce_fusion = (f32[2,12,512]{2,1,0:T(8,128)S(1)}, f32[2,12,512,512]{2,3,1,0:T(8,128)}) fusion(f32[2,12,512,512]{2,3,1,0:T(8,128)} %get-tuple-element.474, f32[2,12,512]{2,1,0:T(8,128)S(1)} %copy-done.68, f32[2,512]{1,0:T(2,128)S(1)} %copy-done.84, bf16[2,512,1,12,64]{1,0,4,3,2:T(2,128)(2,1)S(1)} %copy-done.31, ...), kind=kOutput, calls=%fused_computation.36 | convolution fusion | flops 836751360 | bytes 53579776 | tf_op jit(solution)/shard_map/bqhd,bkhd->bhqk/dot_general | solution.py:428
  499.0 17.6 %multiply_convert_fusion = bf16[2,12,512,512]{2,3,1,0:T(8,128)(2,1)S(1)} fusion(f32[2,12,512,512]{2,3,1,0:T(8,128)} %get-tuple-element.482, f32[2,12,512,512]{2,3,1,0:T(8,128)} %get-tuple-element.474, f32[2,12,512]{2,1,0:T(8,128)S(1)} %get-tuple-element.481, f32[2,12,512]{2,1,0:T(8,128)S(1)} %copy-done.68, f32[2,512]{1,0:T(2,128)S(1)} %copy-done.84), kind=kLoop, calls=%fused_computation.35 | loop fusion | flops 37748736 | bytes 63016960 | tf_op jit(solution)/shard_map/convert_element_type | solution.py:438
  516.6 4.6 copy-done
  523.3 8.5 multiply_bitcast_fusion
  531.8 12.6 %convolution_bitcast_fusion = f32[2,512,1,12,64]{1,4,3,0,2:T(8,128)S(1)} fusion(bf16[2,512,12,64]{1,0,3,2:T(2,128)(2,1)} %copy-done.12, f32[2,12,512,512]{2,3,1,0:T(8,128)} %get-tuple-element.474, f32[2,12,512]{2,1,0:T(8,128)S(1)} %copy-done.68, f32[2,512]{1,0:T(2,128)S(1)} %copy-done.84), kind=kOutput, calls=%fused_computation.154 | convolution fusion | flops 830472192 | bytes 29937664 | tf_op jit(solution)/shard_map/bhqk,bqhd->bkhd/dot_general | solution.py:431
  548.8 9.4 %copy.141 = bf16[2,512,3,12,64]{1,0,4,3,2:T(2,128)(2,1)} copy(bf16[2,512,3,12,64]{1,4,3,0,2:T(8,128)(2,1)} %fusion.35) | data formatting | bytes 9437184 | tf_op jit(solution)/shard_map/convert_element_type | solution.py:447
  558.2 4.0 copy.164
  562.5 8.4 fusion.133
  572.6 3.7 fusion.138
  578.9 5.7 fusion.41
  584.6 4.4 all-to-all-start.3
  589.0 6.7 fusion.152
  600.0 12.4 %reshape.919 = f32[8,96,4,768]{3,2,1,0:T(4,128)} reshape(f32[768,3072]{1,0:T(8,128)} %fusion.48) | data formatting | bytes 18874368 | tf_op jit(solution)/shard_map/reshape | solution.py:250
  612.4 9.0 %copy.146 = f32[8,4,96,768]{3,2,1,0:T(8,128)} copy(f32[8,4,96,768]{3,1,2,0:T(4,128)} %bitcast.353) | data formatting | bytes 18874368 | tf_op jit(solution)/shard_map/transpose | solution.py:251
  621.4 7.0 fusion.33
  651.6 22.9 %fusion.14 = f32[3840,768]{1,0:T(8,128)} fusion(bf16[1536,768]{1,0:T(8,128)(2,1)} %bitcast.80, s32[1536]{0:T(1024)S(1)} %copy-done.122), kind=kOutput, calls=%fused_computation.41 | convolution fusion | flops 9065594880 | bytes 14161920 | tf_op jit(solution)/shard_map/dot_general | solution.py:39
  674.8 4.8 dynamic-slice_convert_fusion
  680.1 6.2 add_convert_fusion.1
  690.7 5.8 add_convert_fusion.3
  697.0 3.9 fusion.32
  704.4 11.2 %collective-permute-done.30 = bf16[384,768]{1,0:T(8,128)(2,1)S(1)} collective-permute-done((bf16[384,768]{1,0:T(8,128)(2,1)S(1)}, bf16[384,768]{1,0:T(8,128)(2,1)S(1)}, u32[]{:S(2)}, u32[]{:S(2)}) %collective-permute-start.30) | collective-permute-done | bytes 589856 | tf_op jit(solution)/shard_map/ppermute | solution.py:154
  720.1 12.0 %collective-permute-done.31 = bf16[384,768]{1,0:T(8,128)(2,1)S(1)} collective-permute-done((bf16[384,768]{1,0:T(8,128)(2,1)S(1)}, bf16[384,768]{1,0:T(8,128)(2,1)S(1)}, u32[]{:S(2)}, u32[]{:S(2)}) %collective-permute-start.31) | collective-permute-done | bytes 589856 | tf_op jit(solution)/shard_map/ppermute | solution.py:154
  733.3 6.7 collective-permute-done.24
  742.4 10.4 %collective-permute-done.32 = bf16[384,768]{1,0:T(8,128)(2,1)S(1)} collective-permute-done((bf16[384,768]{1,0:T(8,128)(2,1)S(1)}, bf16[384,768]{1,0:T(8,128)(2,1)S(1)}, u32[]{:S(2)}, u32[]{:S(2)}) %collective-permute-start.32) | collective-permute-done | bytes 589856 | tf_op jit(solution)/shard_map/ppermute | solution.py:154
  754.5 7.8 collective-permute-done.17
  762.3 5.1 add_convert_fusion.2
  771.0 7.9 collective-permute-done.26
  779.6 11.6 %collective-permute-done.33 = bf16[384,768]{1,0:T(8,128)(2,1)S(1)} collective-permute-done((bf16[384,768]{1,0:T(8,128)(2,1)S(1)}, bf16[384,768]{1,0:T(8,128)(2,1)S(1)}, u32[]{:S(2)}, u32[]{:S(2)}) %collective-permute-start.33) | collective-permute-done | bytes 589856 | tf_op jit(solution)/shard_map/ppermute | solution.py:154
  793.4 13.0 %collective-permute-done.37 = bf16[384,768]{1,0:T(8,128)(2,1)S(1)} collective-permute-done((bf16[384,768]{1,0:T(8,128)(2,1)S(1)}, bf16[384,768]{1,0:T(8,128)(2,1)S(1)}, u32[]{:S(2)}, u32[]{:S(2)}) %collective-permute-start.37) | collective-permute-done | bytes 589856 | tf_op jit(solution)/shard_map/ppermute | solution.py:146
  818.6 3.6 fusion.28
  827.4 7.8 shard_map.490
  847.7 26.4 %multiply_add_fusion.2 = (f32[3840,768]{1,0:T(8,128)}, f32[3840,768]{1,0:T(8,128)}, f32[3840,768]{1,0:T(8,128)}) fusion(f32[3840,768]{1,0:T(8,128)} %param.55, f32[3840,768]{1,0:T(8,128)} %param.41, bf16[1920,768]{1,0:T(8,128)(2,1)} %copy-done.7, bf16[1920,768]{1,0:T(8,128)(2,1)S(1)} %get-tuple-element.416, f32[]{:T(128)S(6)} %min.3, f32[3840,768]{1,0:T(8,128)} %param.48), kind=kLoop, calls=%fused_computation.69 | loop fusion | flops 41287680 | bytes 76677120 | tf_op jit(solution)/shard_map/add | solution.py:473
  874.2 4.2 multiply_add_fusion.6
  (587 shorter events, 233.2 us)
Async XLA Ops:
  4.8 119.1 %collective-permute-start.8 = (bf16[432,768]{1,0:T(8,128)(2,1)}, bf16[432,768]{1,0:T(8,128)(2,1)}, u32[]{:S(2)}, u32[]{:S(2)}) collective-permute-start(bf16[432,768]{1,0:T(8,128)(2,1)} %maximum_select_fusion.1), channel_id=1, source_target_pairs={{0,1},{2,0},{4,2},{6,4},{7,6},{5,7},{3,5},{1,3},{8,9},{10,8},{12,1... | collective-permute-start | bytes 1990664 | tf_op jit(solution)/shard_map/ppermute | solution.py:154
  7.7 137.5 %collective-permute-start.9 = (bf16[432,768]{1,0:T(8,128)(2,1)}, bf16[432,768]{1,0:T(8,128)(2,1)}, u32[]{:S(2)}, u32[]{:S(2)}) collective-permute-start(bf16[432,768]{1,0:T(8,128)(2,1)} %maximum_select_fusion.1), channel_id=1, source_target_pairs={{0,2},{2,4},{4,6},{6,7},{7,5},{5,3},{3,1},{1,0},{8,10},{10,12},{12... | collective-permute-start | bytes 1990664 | tf_op jit(solution)/shard_map/ppermute | solution.py:154
  16.4 24.2 %copy-start.128 = (s32[2]{0:T(128)S(1)}, s32[2]{0:T(128)}, u32[]{:S(2)}) copy-start(s32[2]{0:T(128)} %param.38) | copy-start | bytes 28
  19.8 92.9 %collective-permute-start = (bf16[192,768]{1,0:T(8,128)(2,1)}, bf16[192,768]{1,0:T(8,128)(2,1)}, u32[]{:S(2)}, u32[]{:S(2)}) collective-permute-start(bf16[192,768]{1,0:T(8,128)(2,1)} %get-tuple-element.405), channel_id=1, source_target_pairs={{0,2},{2,4},{4,6},{6,7},{7,5},{5,3},{3,1},{1,0},{8,10},{10,12},{12... | collective-permute-start | bytes 884744 | tf_op jit(solution)/shard_map/ppermute | solution.py:154
  21.8 91.5 %collective-permute-start.1 = (bf16[192,768]{1,0:T(8,128)(2,1)}, bf16[192,768]{1,0:T(8,128)(2,1)}, u32[]{:S(2)}, u32[]{:S(2)}) collective-permute-start(bf16[192,768]{1,0:T(8,128)(2,1)} %get-tuple-element.405), channel_id=1, source_target_pairs={{0,1},{2,0},{4,2},{6,4},{7,6},{5,7},{3,5},{1,3},{8,9},{10,8},{12,1... | collective-permute-start | bytes 884744 | tf_op jit(solution)/shard_map/ppermute | solution.py:154
  50.2 31.1 %copy-start.81 = (s32[1,1024]{1,0:T(1,128)}, s32[1,1024]{1,0:T(1,128)S(1)}, u32[]{:S(2)}) copy-start(s32[1,1024]{1,0:T(1,128)S(1)} %get-tuple-element.408) | copy-start | bytes 12292
  112.6 9.2 %collective-permute-start.2 = (bf16[192,768]{1,0:T(8,128)(2,1)}, bf16[192,768]{1,0:T(8,128)(2,1)S(1)}, u32[]{:S(2)}, u32[]{:S(2)}) collective-permute-start(bf16[192,768]{1,0:T(8,128)(2,1)} %collective-permute-done), channel_id=1, source_target_pairs={{0,2},{2,4},{4,6},{6,7},{7,5},{5,3},{3,1},{1,0},{8,10},{10,12},{12... | collective-permute-start | bytes 884744 | tf_op jit(solution)/shard_map/ppermute | solution.py:154
  113.3 9.2 %collective-permute-start.3 = (bf16[192,768]{1,0:T(8,128)(2,1)}, bf16[192,768]{1,0:T(8,128)(2,1)S(1)}, u32[]{:S(2)}, u32[]{:S(2)}) collective-permute-start(bf16[192,768]{1,0:T(8,128)(2,1)} %collective-permute-done.1), channel_id=1, source_target_pairs={{0,1},{2,0},{4,2},{6,4},{7,6},{5,7},{3,5},{1,3},{8,9},{10,8},{12,1... | collective-permute-start | bytes 884744 | tf_op jit(solution)/shard_map/ppermute | solution.py:154
  121.8 8.2 collective-permute-start.4
  122.5 14.1 %collective-permute-start.5 = (bf16[192,768]{1,0:T(8,128)(2,1)S(1)}, bf16[192,768]{1,0:T(8,128)(2,1)}, u32[]{:S(2)}, u32[]{:S(2)}) collective-permute-start(bf16[192,768]{1,0:T(8,128)(2,1)S(1)} %collective-permute-done.3), channel_id=1, source_target_pairs={{0,1},{2,0},{4,2},{6,4},{7,6},{5,7},{3,5},{1,3},{8,9},{10,8},{12,1... | collective-permute-start | bytes 884744 | tf_op jit(solution)/shard_map/ppermute | solution.py:154
  123.9 28.2 %collective-permute-start.10 = (bf16[432,768]{1,0:T(8,128)(2,1)}, bf16[432,768]{1,0:T(8,128)(2,1)S(1)}, u32[]{:S(2)}, u32[]{:S(2)}) collective-permute-start(bf16[432,768]{1,0:T(8,128)(2,1)} %collective-permute-done.8), channel_id=1, source_target_pairs={{0,1},{2,0},{4,2},{6,4},{7,6},{5,7},{3,5},{1,3},{8,9},{10,8},{12,1... | collective-permute-start | bytes 1990664 | tf_op jit(solution)/shard_map/ppermute | solution.py:154
  130.1 9.7 %collective-permute-start.6 = (bf16[192,768]{1,0:T(8,128)(2,1)}, bf16[192,768]{1,0:T(8,128)(2,1)}, u32[]{:S(2)}, u32[]{:S(2)}) collective-permute-start(bf16[192,768]{1,0:T(8,128)(2,1)} %collective-permute-done.4), channel_id=1, source_target_pairs={{0,2},{2,4},{4,6},{6,7},{7,5},{5,3},{3,1},{1,0},{8,10},{10,12},{12... | collective-permute-start | bytes 884744 | tf_op jit(solution)/shard_map/ppermute | solution.py:154
  130.7 117.8 %all-to-all-start.2 = ((bf16[8,192,768]{2,1,0:T(8,128)(2,1)}), bf16[8,192,768]{2,1,0:T(8,128)(2,1)}, u32[]{:S(2)}, u32[]{:S(2)}) async-start(bf16[8,192,768]{2,1,0:T(8,128)(2,1)} %bitcast.381), calls=%async_computation.2 | async-start | bytes 4718592 | tf_op jit(solution)/shard_map/all_to_all | solution.py:318
  140.8 84.8 %collective-permute-start.7 = (bf16[8,192,768]{2,1,0:T(8,128)(2,1)S(1)}, bf16[8,192,768]{2,1,0:T(8,128)(2,1)}, u32[]{:S(2)}, u32[]{:S(2)}) collective-permute-start(bf16[8,192,768]{2,1,0:T(8,128)(2,1)S(1)} %bitcast_dynamic-update-slice_fusion.7), channel_id=1, source_target_pairs={{0,8},{8,0},{16,24},{24,16},{1,9},{9,1},{17,25},{25,17},{2,10},{10... | collective-permute-start | bytes 7077896 | tf_op jit(solution)/shard_map/ppermute | solution.py:134
  145.2 44.9 %collective-permute-start.11 = (bf16[432,768]{1,0:T(8,128)(2,1)}, bf16[432,768]{1,0:T(8,128)(2,1)}, u32[]{:S(2)}, u32[]{:S(2)}) collective-permute-start(bf16[432,768]{1,0:T(8,128)(2,1)} %collective-permute-done.9), channel_id=1, source_target_pairs={{0,2},{2,4},{4,6},{6,7},{7,5},{5,3},{3,1},{1,0},{8,10},{10,12},{12... | collective-permute-start | bytes 1990664 | tf_op jit(solution)/shard_map/ppermute | solution.py:154
  148.5 58.2 %copy-start.135 = (f32[2]{0:T(128)}, f32[2]{0:T(128)S(1)}, u32[]{:S(2)}) copy-start(f32[2]{0:T(128)S(1)} %convert_element_type.401) | copy-start | bytes 28
  152.1 51.8 %collective-permute-start.12 = (bf16[432,768]{1,0:T(8,128)(2,1)S(1)}, bf16[432,768]{1,0:T(8,128)(2,1)S(1)}, u32[]{:S(2)}, u32[]{:S(2)}) collective-permute-start(bf16[432,768]{1,0:T(8,128)(2,1)S(1)} %collective-permute-done.10), channel_id=1, source_target_pairs={{0,1},{2,0},{4,2},{6,4},{7,6},{5,7},{3,5},{1,3},{8,9},{10,8},{12,1... | collective-permute-start | bytes 1990664 | tf_op jit(solution)/shard_map/ppermute | solution.py:154
  190.2 26.6 %collective-permute-start.13 = (bf16[432,768]{1,0:T(8,128)(2,1)}, bf16[432,768]{1,0:T(8,128)(2,1)S(1)}, u32[]{:S(2)}, u32[]{:S(2)}) collective-permute-start(bf16[432,768]{1,0:T(8,128)(2,1)} %collective-permute-done.11), channel_id=1, source_target_pairs={{0,2},{2,4},{4,6},{6,7},{7,5},{5,3},{3,1},{1,0},{8,10},{10,12},{12... | collective-permute-start | bytes 1990664 | tf_op jit(solution)/shard_map/ppermute | solution.py:154
  203.9 20.8 %collective-permute-start.14 = (bf16[432,768]{1,0:T(8,128)(2,1)S(1)}, bf16[432,768]{1,0:T(8,128)(2,1)S(1)}, u32[]{:S(2)}, u32[]{:S(2)}) collective-permute-start(bf16[432,768]{1,0:T(8,128)(2,1)S(1)} %collective-permute-done.12), channel_id=1, source_target_pairs={{0,1},{2,0},{4,2},{6,4},{7,6},{5,7},{3,5},{1,3},{8,9},{10,8},{12,1... | collective-permute-start | bytes 1990664 | tf_op jit(solution)/shard_map/ppermute | solution.py:154
  225.6 98.8 %collective-permute-start.15 = (bf16[8,432,768]{2,1,0:T(8,128)(2,1)}, bf16[8,432,768]{2,1,0:T(8,128)(2,1)}, u32[]{:S(2)}, u32[]{:S(2)}) collective-permute-start(bf16[8,432,768]{2,1,0:T(8,128)(2,1)} %bitcast_dynamic-update-slice_fusion), channel_id=1, source_target_pairs={{0,8},{8,0},{16,24},{24,16},{1,9},{9,1},{17,25},{25,17},{2,10},{10... | collective-permute-start | bytes 15925256 | tf_op jit(solution)/shard_map/ppermute | solution.py:134
  243.8 96.5 %copy-start.111 = (f32[768]{0:T(1024)}, f32[768]{0:T(1024)S(1)}, u32[]{:S(2)}) copy-start(f32[768]{0:T(1024)S(1)} %add.1073) | copy-start | bytes 9220
  243.8 96.4 %copy-start.104 = (f32[768]{0:T(1024)}, f32[768]{0:T(1024)S(1)}, u32[]{:S(2)}) copy-start(f32[768]{0:T(1024)S(1)} %mul.655) | copy-start | bytes 9220
  259.4 80.9 %copy-start.3 = (f32[1024,768]{1,0:T(8,128)}, f32[1024,768]{1,0:T(8,128)S(1)}, u32[]{:S(2)}) copy-start(f32[1024,768]{1,0:T(8,128)S(1)} %get-tuple-element.403) | copy-start | bytes 9437188
  259.4 80.9 %copy-start.106 = (f32[1024]{0:T(1024)}, f32[1024]{0:T(1024)S(1)}, u32[]{:S(2)}) copy-start(f32[1024]{0:T(1024)S(1)} %fusion.117) | copy-start | bytes 12292
  287.7 22.2 %copy-start.30 = (bf16[2,512,1,12,64]{1,0,4,3,2:T(2,128)(2,1)}, bf16[2,512,1,12,64]{1,0,4,3,2:T(2,128)(2,1)S(1)}, u32[]{:S(2)}) copy-start(bf16[2,512,1,12,64]{1,0,4,3,2:T(2,128)(2,1)S(1)} %get-tuple-element.424) | copy-start | bytes 4718596
  342.2 41.8 %copy-start.1 = (f32[1024,768]{1,0:T(8,128)}, f32[1024,768]{1,0:T(8,128)S(1)}, u32[]{:S(2)}) copy-start(f32[1024,768]{1,0:T(8,128)S(1)} %get-tuple-element.476) | copy-start | bytes 9437188
  347.4 36.6 %slice-start.10 = ((s8[4718592]{0:T(1024)(128)(4,1)}), s8[524288]{0:T(1024)(128)(4,1)S(1)}, s32[]{:S(2)}) async-start(s8[4718592]{0:T(1024)(128)(4,1)} %bitcast.367), calls=%async_computation.14 | async-start | bytes 1048576
  348.5 35.5 %copy-start.37 = (bf16[96,8,4,768]{3,1,2,0:T(8,128)(2,1)}, bf16[96,8,4,768]{3,1,2,0:T(8,128)(2,1)S(1)}, u32[]{:S(2)}) copy-start(bf16[96,8,4,768]{3,1,2,0:T(8,128)(2,1)S(1)} %copy.161) | copy-start | bytes 14155780
  348.5 35.5 %slice-start.11 = ((s8[4718592]{0:T(1024)(128)(4,1)}), s8[4194304]{0:T(1024)(128)(4,1)S(1)}, s32[]{:S(2)}) async-start(s8[4718592]{0:T(1024)(128)(4,1)} %bitcast.367), calls=%async_computation.15 | async-start | bytes 8388608
  348.5 35.5 %copy-start.126 = (f32[768]{0:T(1024)S(1)}, f32[768]{0:T(1024)}, u32[]{:S(2)}) copy-start(f32[768]{0:T(1024)} %add.1124) | copy-start | bytes 9220
  390.2 22.7 %copy-start.136 = (f32[2]{0:T(128)S(1)}, f32[2]{0:T(128)}, u32[]{:S(2)}) copy-start(f32[2]{0:T(128)} %copy-done.135) | copy-start | bytes 28
  390.2 23.5 %copy-start.97 = (f32[1,4,2,128]{3,1,2,0:T(4,128)S(1)}, f32[1,4,2,128]{3,1,2,0:T(4,128)}, u32[]{:S(2)}) copy-start(f32[1,4,2,128]{3,1,2,0:T(4,128)} %copy.163) | copy-start | bytes 12292
  477.3 21.7 %copy-start.12 = (bf16[2,512,12,64]{1,0,3,2:T(2,128)(2,1)}, bf16[2,512,12,64]{1,0,3,2:T(2,128)(2,1)S(1)}, u32[]{:S(2)}) copy-start(bf16[2,512,12,64]{1,0,3,2:T(2,128)(2,1)S(1)} %reshape.913) | copy-start | bytes 4718596
  499.0 22.2 %copy-start.11 = (bf16[2,512,1,12,64]{1,0,4,3,2:T(2,128)(2,1)S(1)}, bf16[2,512,1,12,64]{1,0,4,3,2:T(2,128)(2,1)}, u32[]{:S(2)}) copy-start(bf16[2,512,1,12,64]{1,0,4,3,2:T(2,128)(2,1)} %copy-done.10) | copy-start | bytes 4718596
  584.6 66.9 %all-to-all-start.3 = ((bf16[8,192,768]{2,1,0:T(8,128)(2,1)}), bf16[8,192,768]{2,1,0:T(8,128)(2,1)}, u32[]{:S(2)}, u32[]{:S(2)}) async-start(bf16[8,192,768]{2,1,0:T(8,128)(2,1)} %bitcast.382), calls=%async_computation.3 | async-start | bytes 4718592 | tf_op jit(solution)/shard_map/all_to_all | solution.py:318
  628.4 68.5 %collective-permute-start.29 = (bf16[8,384,768]{2,1,0:T(8,128)(2,1)}, bf16[8,384,768]{2,1,0:T(8,128)(2,1)}, u32[]{:S(2)}, u32[]{:S(2)}) collective-permute-start(bf16[8,384,768]{2,1,0:T(8,128)(2,1)} %fusion.33), channel_id=1, source_target_pairs={{0,8},{8,0},{16,24},{24,16},{1,9},{9,1},{17,25},{25,17},{2,10},{10... | collective-permute-start | bytes 14155784 | tf_op jit(solution)/shard_map/ppermute | solution.py:134
  651.5 28.6 %collective-permute-start.19 = (bf16[8,240,768]{2,1,0:T(8,128)(2,1)}, bf16[8,240,768]{2,1,0:T(8,128)(2,1)}, u32[]{:S(2)}, u32[]{:S(2)}) collective-permute-start(bf16[8,240,768]{2,1,0:T(8,128)(2,1)} %select_convert_fusion), channel_id=1, source_target_pairs={{0,8},{8,0},{16,24},{24,16},{1,9},{9,1},{17,25},{25,17},{2,10},{10... | collective-permute-start | bytes 8847368 | tf_op jit(solution)/shard_map/ppermute | solution.py:134
  651.5 23.0 %copy-start.36 = (s32[8,1024]{1,0:T(8,128)S(1)}, s32[8,1024]{1,0:T(8,128)}, u32[]{:S(2)}) copy-start(s32[8,1024]{1,0:T(8,128)} %get-tuple-element.646) | copy-start | bytes 98308
  651.5 23.0 %copy-start.43 = (s32[8,1024]{1,0:T(8,128)S(1)}, s32[8,1024]{1,0:T(8,128)}, u32[]{:S(2)}) copy-start(s32[8,1024]{1,0:T(8,128)} %copy-done.41) | copy-start | bytes 98308
  651.6 23.0 %copy-start.56 = (s32[8,1024]{1,0:T(8,128)S(1)}, s32[8,1024]{1,0:T(8,128)}, u32[]{:S(2)}) copy-start(s32[8,1024]{1,0:T(8,128)} %get-tuple-element.647) | copy-start | bytes 98308
  651.6 23.0 %copy-start.66 = (pred[8,1024]{1,0:T(8,128)(4,1)S(1)}, pred[8,1024]{1,0:T(8,128)(4,1)}, u32[]{:S(2)}) copy-start(pred[8,1024]{1,0:T(8,128)(4,1)} %copy-done.65) | copy-start | bytes 24580
  651.6 23.0 %copy-start.82 = (s32[1,1024]{1,0:T(1,128)S(1)}, s32[1,1024]{1,0:T(1,128)}, u32[]{:S(2)}) copy-start(s32[1,1024]{1,0:T(1,128)} %copy-done.81) | copy-start | bytes 12292
  679.6 11.1 %collective-permute-start.16 = (bf16[1920,768]{1,0:T(8,128)(2,1)}, bf16[1920,768]{1,0:T(8,128)(2,1)}, u32[]{:S(2)}, u32[]{:S(2)}) collective-permute-start(bf16[1920,768]{1,0:T(8,128)(2,1)} %dynamic-slice_convert_fusion), channel_id=1, source_target_pairs={{0,8},{8,0},{16,24},{24,16},{1,9},{9,1},{17,25},{25,17},{2,10},{10... | collective-permute-start | bytes 8847368 | tf_op jit(solution)/shard_map/ppermute | solution.py:134
  689.0 13.0 %collective-permute-start.20 = (bf16[240,768]{1,0:T(8,128)(2,1)}, bf16[240,768]{1,0:T(8,128)(2,1)}, u32[]{:S(2)}, u32[]{:S(2)}) collective-permute-start(bf16[240,768]{1,0:T(8,128)(2,1)} %get-tuple-element.430), channel_id=1, source_target_pairs={{0,1},{2,0},{4,2},{6,4},{7,6},{5,7},{3,5},{1,3},{8,9},{10,8},{12,1... | collective-permute-start | bytes 1105928 | tf_op jit(solution)/shard_map/ppermute | solution.py:154
  696.5 65.8 %collective-permute-start.17 = (bf16[1920,768]{1,0:T(8,128)(2,1)}, bf16[1920,768]{1,0:T(8,128)(2,1)}, u32[]{:S(2)}, u32[]{:S(2)}) collective-permute-start(bf16[1920,768]{1,0:T(8,128)(2,1)} %add_convert_fusion.3), channel_id=1, source_target_pairs={{0,16},{8,24},{16,0},{24,8},{1,17},{9,25},{17,1},{25,9},{2,18},{10... | collective-permute-start | bytes 8847368 | tf_op jit(solution)/shard_map/ppermute | solution.py:146
  700.9 14.7 %collective-permute-start.30 = (bf16[384,768]{1,0:T(8,128)(2,1)S(1)}, bf16[384,768]{1,0:T(8,128)(2,1)S(1)}, u32[]{:S(2)}, u32[]{:S(2)}) collective-permute-start(bf16[384,768]{1,0:T(8,128)(2,1)S(1)} %get-tuple-element.420), channel_id=1, source_target_pairs={{0,2},{2,4},{4,6},{6,7},{7,5},{5,3},{3,1},{1,0},{8,10},{10,12},{12... | collective-permute-start | bytes 1769480 | tf_op jit(solution)/shard_map/ppermute | solution.py:154
  703.2 15.3 %collective-permute-start.21 = (bf16[240,768]{1,0:T(8,128)(2,1)S(1)}, bf16[240,768]{1,0:T(8,128)(2,1)S(1)}, u32[]{:S(2)}, u32[]{:S(2)}) collective-permute-start(bf16[240,768]{1,0:T(8,128)(2,1)S(1)} %fusion.82), channel_id=1, source_target_pairs={{0,1},{2,0},{4,2},{6,4},{7,6},{5,7},{3,5},{1,3},{8,9},{10,8},{12,1... | collective-permute-start | bytes 1105928 | tf_op jit(solution)/shard_map/ppermute | solution.py:154
  715.9 16.3 %collective-permute-start.31 = (bf16[384,768]{1,0:T(8,128)(2,1)S(1)}, bf16[384,768]{1,0:T(8,128)(2,1)S(1)}, u32[]{:S(2)}, u32[]{:S(2)}) collective-permute-start(bf16[384,768]{1,0:T(8,128)(2,1)S(1)} %fusion.75), channel_id=1, source_target_pairs={{0,2},{2,4},{4,6},{6,7},{7,5},{5,3},{3,1},{1,0},{8,10},{10,12},{12... | collective-permute-start | bytes 1769480 | tf_op jit(solution)/shard_map/ppermute | solution.py:154
  716.8 23.2 %collective-permute-start.24 = (bf16[240,768]{1,0:T(8,128)(2,1)S(1)}, bf16[240,768]{1,0:T(8,128)(2,1)S(1)}, u32[]{:S(2)}, u32[]{:S(2)}) collective-permute-start(bf16[240,768]{1,0:T(8,128)(2,1)S(1)} %get-tuple-element.431), channel_id=1, source_target_pairs={{0,2},{2,4},{4,6},{6,7},{7,5},{5,3},{3,1},{1,0},{8,10},{10,12},{12... | collective-permute-start | bytes 1105928 | tf_op jit(solution)/shard_map/ppermute | solution.py:154
  718.6 21.4 %collective-permute-start.22 = (bf16[240,768]{1,0:T(8,128)(2,1)S(1)}, bf16[240,768]{1,0:T(8,128)(2,1)S(1)}, u32[]{:S(2)}, u32[]{:S(2)}) collective-permute-start(bf16[240,768]{1,0:T(8,128)(2,1)S(1)} %fusion.83), channel_id=1, source_target_pairs={{0,1},{2,0},{4,2},{6,4},{7,6},{5,7},{3,5},{1,3},{8,9},{10,8},{12,1... | collective-permute-start | bytes 1105928 | tf_op jit(solution)/shard_map/ppermute | solution.py:154
  719.0 23.3 %collective-permute-start.34 = (bf16[384,768]{1,0:T(8,128)(2,1)S(1)}, bf16[384,768]{1,0:T(8,128)(2,1)S(1)}, u32[]{:S(2)}, u32[]{:S(2)}) collective-permute-start(bf16[384,768]{1,0:T(8,128)(2,1)S(1)} %get-tuple-element.421), channel_id=1, source_target_pairs={{0,1},{2,0},{4,2},{6,4},{7,6},{5,7},{3,5},{1,3},{8,9},{10,8},{12,1... | collective-permute-start | bytes 1769480 | tf_op jit(solution)/shard_map/ppermute | solution.py:154
  732.3 20.4 %collective-permute-start.32 = (bf16[384,768]{1,0:T(8,128)(2,1)S(1)}, bf16[384,768]{1,0:T(8,128)(2,1)S(1)}, u32[]{:S(2)}, u32[]{:S(2)}) collective-permute-start(bf16[384,768]{1,0:T(8,128)(2,1)S(1)} %fusion.76), channel_id=1, source_target_pairs={{0,2},{2,4},{4,6},{6,7},{7,5},{5,3},{3,1},{1,0},{8,10},{10,12},{12... | collective-permute-start | bytes 1769480 | tf_op jit(solution)/shard_map/ppermute | solution.py:154
  740.3 27.1 %collective-permute-start.25 = (bf16[240,768]{1,0:T(8,128)(2,1)S(1)}, bf16[240,768]{1,0:T(8,128)(2,1)S(1)}, u32[]{:S(2)}, u32[]{:S(2)}) collective-permute-start(bf16[240,768]{1,0:T(8,128)(2,1)S(1)} %get-tuple-element.429), channel_id=1, source_target_pairs={{0,2},{2,4},{4,6},{6,7},{7,5},{5,3},{3,1},{1,0},{8,10},{10,12},{12... | collective-permute-start | bytes 1105928 | tf_op jit(solution)/shard_map/ppermute | solution.py:154
  741.3 29.7 %collective-permute-start.23 = (bf16[240,768]{1,0:T(8,128)(2,1)S(1)}, bf16[240,768]{1,0:T(8,128)(2,1)S(1)}, u32[]{:S(2)}, u32[]{:S(2)}) collective-permute-start(bf16[240,768]{1,0:T(8,128)(2,1)S(1)} %get-tuple-element.428), channel_id=1, source_target_pairs={{0,1},{2,0},{4,2},{6,4},{7,6},{5,7},{3,5},{1,3},{8,9},{10,8},{12,1... | collective-permute-start | bytes 1105928 | tf_op jit(solution)/shard_map/ppermute | solution.py:154
  753.0 17.1 %collective-permute-start.35 = (bf16[384,768]{1,0:T(8,128)(2,1)S(1)}, bf16[384,768]{1,0:T(8,128)(2,1)S(1)}, u32[]{:S(2)}, u32[]{:S(2)}) collective-permute-start(bf16[384,768]{1,0:T(8,128)(2,1)S(1)} %get-tuple-element.419), channel_id=1, source_target_pairs={{0,1},{2,0},{4,2},{6,4},{7,6},{5,7},{3,5},{1,3},{8,9},{10,8},{12,1... | collective-permute-start | bytes 1769480 | tf_op jit(solution)/shard_map/ppermute | solution.py:154
  767.4 46.6 %collective-permute-start.18 = (bf16[1920,768]{1,0:T(8,128)(2,1)}, bf16[1920,768]{1,0:T(8,128)(2,1)}, u32[]{:S(2)}, u32[]{:S(2)}) collective-permute-start(bf16[1920,768]{1,0:T(8,128)(2,1)} %add_convert_fusion.2), channel_id=1, source_target_pairs={{0,8},{8,0},{16,24},{24,16},{1,9},{9,1},{17,25},{25,17},{2,10},{10... | collective-permute-start | bytes 8847368 | tf_op jit(solution)/shard_map/ppermute | solution.py:134
  767.5 11.4 %collective-permute-start.26 = (bf16[240,768]{1,0:T(8,128)(2,1)S(1)}, bf16[240,768]{1,0:T(8,128)(2,1)S(1)}, u32[]{:S(2)}, u32[]{:S(2)}) collective-permute-start(bf16[240,768]{1,0:T(8,128)(2,1)S(1)} %fusion.81), channel_id=1, source_target_pairs={{0,2},{2,4},{4,6},{6,7},{7,5},{5,3},{3,1},{1,0},{8,10},{10,12},{12... | collective-permute-start | bytes 1105928 | tf_op jit(solution)/shard_map/ppermute | solution.py:154
  768.5 22.7 %collective-permute-start.33 = (bf16[384,768]{1,0:T(8,128)(2,1)S(1)}, bf16[384,768]{1,0:T(8,128)(2,1)S(1)}, u32[]{:S(2)}, u32[]{:S(2)}) collective-permute-start(bf16[384,768]{1,0:T(8,128)(2,1)S(1)} %get-tuple-element.418), channel_id=1, source_target_pairs={{0,2},{2,4},{4,6},{6,7},{7,5},{5,3},{3,1},{1,0},{8,10},{10,12},{12... | collective-permute-start | bytes 1769480 | tf_op jit(solution)/shard_map/ppermute | solution.py:154
  770.3 20.9 %collective-permute-start.36 = (bf16[384,768]{1,0:T(8,128)(2,1)S(1)}, bf16[384,768]{1,0:T(8,128)(2,1)S(1)}, u32[]{:S(2)}, u32[]{:S(2)}) collective-permute-start(bf16[384,768]{1,0:T(8,128)(2,1)S(1)} %fusion.74), channel_id=1, source_target_pairs={{0,1},{2,0},{4,2},{6,4},{7,6},{5,7},{3,5},{1,3},{8,9},{10,8},{12,1... | collective-permute-start | bytes 1769480 | tf_op jit(solution)/shard_map/ppermute | solution.py:154
  779.1 12.9 %collective-permute-start.27 = (bf16[240,768]{1,0:T(8,128)(2,1)S(1)}, bf16[240,768]{1,0:T(8,128)(2,1)S(1)}, u32[]{:S(2)}, u32[]{:S(2)}) collective-permute-start(bf16[240,768]{1,0:T(8,128)(2,1)S(1)} %fusion.86), channel_id=1, source_target_pairs={{0,16},{8,24},{16,0},{24,8},{1,17},{9,25},{17,1},{25,9},{2,18},{10... | collective-permute-start | bytes 1105928 | tf_op jit(solution)/shard_map/ppermute | solution.py:146
  791.4 15.0 %collective-permute-start.37 = (bf16[384,768]{1,0:T(8,128)(2,1)S(1)}, bf16[384,768]{1,0:T(8,128)(2,1)S(1)}, u32[]{:S(2)}, u32[]{:S(2)}) collective-permute-start(bf16[384,768]{1,0:T(8,128)(2,1)S(1)} %fusion.79), channel_id=1, source_target_pairs={{0,16},{8,24},{16,0},{24,8},{1,17},{9,25},{17,1},{25,9},{2,18},{10... | collective-permute-start | bytes 1769480 | tf_op jit(solution)/shard_map/ppermute | solution.py:146
  792.0 15.7 %collective-permute-start.28 = (bf16[240,768]{1,0:T(8,128)(2,1)S(1)}, bf16[240,768]{1,0:T(8,128)(2,1)S(1)}, u32[]{:S(2)}, u32[]{:S(2)}) collective-permute-start(bf16[240,768]{1,0:T(8,128)(2,1)S(1)} %add_convert_fusion.7), channel_id=1, source_target_pairs={{0,8},{8,0},{16,24},{24,16},{1,9},{9,1},{17,25},{25,17},{2,10},{10... | collective-permute-start | bytes 1105928 | tf_op jit(solution)/shard_map/ppermute | solution.py:134
  807.7 4.5 collective-permute-start.38
  847.7 26.4 %copy-start.54 = (bf16[384,768]{1,0:T(8,128)(2,1)S(1)}, bf16[384,768]{1,0:T(8,128)(2,1)}, u32[]{:S(2)}) copy-start(bf16[384,768]{1,0:T(8,128)(2,1)} %get-tuple-element.388) | copy-start | bytes 1769476
  (129 other events, 736.9 us)

commit v2 on v1

--- a/solution.py
+++ b/solution.py
@@ -20,17 +20,6 @@
 KEEP = 0.9
 
 
-def layer_norm(v, gain, shift):
-    mean = jnp.mean(v, -1, keepdims=True)
-    cent = v - mean
-    var = jnp.mean(cent * cent, -1, keepdims=True)
-    return cent * lax.rsqrt(var + 1e-12) * gain + shift
-
-
-def gelu_exact(v):
-    return jax.nn.gelu(v, approximate=False)
-
-
 def matmul(left, right):
     return jnp.dot(left, right, preferred_element_type=jnp.float32)
 
@@ -45,6 +34,518 @@
     return lax.dot_general(
         grad, weight, (((1,), (1,)), ((), ())), preferred_element_type=jnp.float32
     )
+
+
+TILE = 256
+EPS = 1e-12
+VMEM_GRANT = 60 * 1024 * 1024
+
+
+def whole_spec(shape):
+    return pl.BlockSpec(shape, lambda *_: (0,) * len(shape))
+
+
+def rows_spec(width, rows=TILE):
+    return pl.BlockSpec((rows, width), lambda i, *_: (i, 0))
+
+
+def weight_spec(rows, at):
+    return pl.BlockSpec((rows, D), lambda i, *_: (at, 0))
+
+
+def call(kernel, name, grid, in_specs, out_specs, out_shape, scratch=(), prefetch=0, flops=0, moved=0):
+    return pl.pallas_call(
+        kernel,
+        name=name,
+        grid_spec=pltpu.PrefetchScalarGridSpec(
+            num_scalar_prefetch=prefetch,
+            grid=grid,
+            in_specs=in_specs,
+            out_specs=out_specs,
+            scratch_shapes=scratch,
+        ),
+        out_shape=out_shape,
+        compiler_params=pltpu.CompilerParams(vmem_limit_bytes=VMEM_GRANT),
+        cost_estimate=pl.CostEstimate(flops=flops, bytes_accessed=moved, transcendentals=0),
+    )
+
+
+def normed(v):
+    mean = jnp.mean(v, -1, keepdims=True)
+    cent = v - mean
+    scale = lax.rsqrt(jnp.mean(cent * cent, -1, keepdims=True) + EPS)
+    return cent * scale, scale
+
+
+def norm_back(grad, hat, scale, gain):
+    inner = grad * gain
+    middle = jnp.mean(inner, -1, keepdims=True)
+    along = jnp.mean(inner * hat, -1, keepdims=True)
+    return (
+        scale * (inner - middle - hat * along),
+        jnp.sum(grad * hat, 0, keepdims=True),
+        jnp.sum(grad, 0, keepdims=True),
+    )
+
+
+def add_row(ref, row, value):
+    ref[row : row + 1, :] += value
+
+
+def embed_kernel(slot, got, extra, pos, weight, small, x_out, h0_out, qkv_out):
+    count = got.shape[0]
+    pick = (slot[:, 0:1] == lax.broadcasted_iota(jnp.int32, (slot.shape[0], count), 1)).astype(
+        jnp.bfloat16
+    )
+    words = matmul(pick, got[...]) + extra[...].astype(jnp.float32)
+    x = words + pos[...].astype(jnp.float32)
+    hat, _ = normed(x)
+    h0 = hat * small[0:1, :] + small[1:2, :]
+    x_out[...] = x
+    h0_out[...] = h0
+    low = h0.astype(jnp.bfloat16)
+    for third, bias in enumerate((2, None, 3)):
+        value = matmul(low, weight[third * D : (third + 1) * D, :])
+        if bias is not None:
+            value = value + small[bias : bias + 1, :]
+        qkv_out[:, third * D : (third + 1) * D] = value.astype(jnp.bfloat16)
+
+
+def embed(slot, got, extra, pos, weight, small):
+    tokens = slot.shape[0]
+    turns = pos.shape[0] // TILE
+    return call(
+        embed_kernel,
+        "embed_qkv",
+        (tokens // TILE,),
+        [
+            rows_spec(128),
+            whole_spec(got.shape),
+            rows_spec(D),
+            pl.BlockSpec((TILE, D), lambda i: (lax.rem(i, turns), 0)),
+            weight_spec(3 * D, 0),
+            whole_spec(small.shape),
+        ],
+        [rows_spec(D), rows_spec(D), rows_spec(3 * D)],
+        [
+            jax.ShapeDtypeStruct((tokens, D), jnp.float32),
+            jax.ShapeDtypeStruct((tokens, D), jnp.float32),
+            jax.ShapeDtypeStruct((tokens, 3 * D), jnp.bfloat16),
+        ],
+        flops=2 * tokens * D * (3 * D + got.shape[0]),
+        moved=tokens * D * 20,
+    )(slot, got, extra, pos, weight, small)
+
+
+def head_masks(rows):
+    lane = lax.broadcasted_iota(jnp.int32, (rows, 128), 1)
+    return (lane < 64, lane >= 64)
+
+
+def live_row(length, seq):
+    return jnp.where(
+        lax.broadcasted_iota(jnp.int32, (1, seq), 1) < length, 0.0, -1000000000.0
+    ).astype(jnp.float32)
+
+
+def attend_kernel(lengths, qkv, mixed_out, log_out):
+    seq = qkv.shape[0]
+    bias = live_row(lengths[pl.program_id(0)], seq)
+    masks = head_masks(seq)
+    lane = lax.broadcasted_iota(jnp.int32, (seq, 128), 1)
+    logs = jnp.zeros((seq, 128), jnp.float32)
+    for pair in range(H // 2):
+        at = pair * 128
+        query = qkv[:, at : at + 128] * jnp.bfloat16(0.125)
+        keys = qkv[:, D + at : D + at + 128]
+        values = qkv[:, 2 * D + at : 2 * D + at + 128]
+        sides = []
+        for side, mask in enumerate(masks):
+            logits = back_mul(jnp.where(mask, query, jnp.zeros_like(query)), keys) + bias
+            top = jnp.max(logits, -1, keepdims=True)
+            raised = jnp.exp(logits - top)
+            total = jnp.sum(raised, -1, keepdims=True)
+            probs = (raised * (1.0 / total)).astype(jnp.bfloat16)
+            sides.append(matmul(probs, values))
+            logs = jnp.where(lane == 2 * pair + side, top + jnp.log(total), logs)
+        mixed_out[:, at : at + 128] = jnp.where(masks[0], sides[0], sides[1]).astype(jnp.bfloat16)
+    log_out[...] = logs
+
+
+def attend(lengths, qkv, seq):
+    tokens = qkv.shape[0]
+    return call(
+        attend_kernel,
+        "attention",
+        (tokens // seq,),
+        [rows_spec(3 * D, seq)],
+        [rows_spec(D, seq), rows_spec(128, seq)],
+        [
+            jax.ShapeDtypeStruct((tokens, D), jnp.bfloat16),
+            jax.ShapeDtypeStruct((tokens, 128), jnp.float32),
+        ],
+        prefetch=1,
+        flops=4 * tokens * seq * D,
+        moved=tokens * D * 8,
+    )(lengths, qkv)
+
+
+def feed_kernel(
+    lengths, mixed, h0, out_w, up_w, down_w, small, r1_out, h1_out, act_out, slope_out, r2_out, pooled
+):
+    step = pl.program_id(0)
+    turns = LEN // TILE
+    r1 = h0[...] + (matmul(mixed[...], out_w[...]) + small[4:5, :])
+    hat, _ = normed(r1)
+    h1 = hat * small[5:6, :] + small[6:7, :]
+    low = h1.astype(jnp.bfloat16)
+    r1_out[...] = r1
+    h1_out[...] = low
+    ffn = jnp.zeros(r1.shape, jnp.float32)
+    for part in range(FF // D):
+        up = matmul(low, up_w[part * D : (part + 1) * D, :]) + small[7 + part : 8 + part, :]
+        below = 0.5 * (1.0 + lax.erf(up * math.sqrt(0.5)))
+        act = (up * below).astype(jnp.bfloat16)
+        slope = below + up * jnp.exp(-0.5 * up * up) * (1.0 / math.sqrt(2.0 * math.pi))
+        act_out[:, part * D : (part + 1) * D] = act
+        slope_out[:, part * D : (part + 1) * D] = slope.astype(jnp.bfloat16)
+        ffn = ffn + matmul(act, down_w[part * D : (part + 1) * D, :])
+    r2 = h1 + (ffn + small[11:12, :])
+    r2_out[...] = r2
+    hat2, _ = normed(r2)
+    h2 = hat2 * small[12:13, :] + small[13:14, :]
+    length = lengths[step // turns]
+    at = lax.rem(step, turns) * TILE + lax.broadcasted_iota(jnp.int32, (TILE, 1), 0)
+    part_sum = jnp.sum(jnp.where(at < length, h2, 0.0), 0, keepdims=True)
+
+    @pl.when(lax.rem(step, turns) == 0)
+    def _():
+        pooled[...] = jnp.zeros_like(pooled)
+
+    pooled[0, 0:1, :] += part_sum / length.astype(jnp.float32)
+
+
+def feed(lengths, mixed, h0, weight, small):
+    tokens = mixed.shape[0]
+    turns = LEN // TILE
+    return call(
+        feed_kernel,
+        "feed_forward",
+        (tokens // TILE,),
+        [
+            rows_spec(D),
+            rows_spec(D),
+            weight_spec(D, 3),
+            weight_spec(FF, 1),
+            weight_spec(FF, 2),
+            whole_spec(small.shape),
+        ],
+        [
+            rows_spec(D),
+            rows_spec(D),
+            rows_spec(FF),
+            rows_spec(FF),
+            rows_spec(D),
+            pl.BlockSpec((1, 8, D), lambda i, *_: (i // turns, 0, 0)),
+        ],
+        [
+            jax.ShapeDtypeStruct((tokens, D), jnp.float32),
+            jax.ShapeDtypeStruct((tokens, D), jnp.bfloat16),
+            jax.ShapeDtypeStruct((tokens, FF), jnp.bfloat16),
+            jax.ShapeDtypeStruct((tokens, FF), jnp.bfloat16),
+            jax.ShapeDtypeStruct((tokens, D), jnp.float32),
+            jax.ShapeDtypeStruct((tokens // LEN, 8, D), jnp.float32),
+        ],
+        prefetch=1,
+        flops=2 * tokens * D * (D + 2 * FF),
+        moved=tokens * D * 32,
+    )(lengths, mixed, h0, weight, weight, weight, small)
+
+
+def feed_back_kernel(
+    lengths, share, r1, r2, slope, out_w, up_w, down_w, small, f_out, u_out, r1_grad, a_out, mixed_out, sums
+):
+    step = pl.program_id(0)
+    turns = LEN // TILE
+
+    @pl.when(step == 0)
+    def _():
+        sums[...] = jnp.zeros_like(sums)
+
+    length = lengths[step // turns]
+    at = lax.rem(step, turns) * TILE + lax.broadcasted_iota(jnp.int32, (TILE, 1), 0)
+    grad_h2 = jnp.where(at < length, share[0, 0:1, :], 0.0)
+    hat2, scale2 = normed(r2[...])
+    grad_r2, gain2, shift2 = norm_back(grad_h2, hat2, scale2, small[12:13, :])
+    add_row(sums, 12, gain2)
+    add_row(sums, 13, shift2)
+    add_row(sums, 11, jnp.sum(grad_r2, 0, keepdims=True))
+    low_f = grad_r2.astype(jnp.bfloat16)
+    f_out[...] = low_f
+    grad_h1 = grad_r2
+    for part in range(FF // D):
+        span = slice(part * D, (part + 1) * D)
+        grad_up = back_mul(low_f, down_w[span, :]) * slope[:, span].astype(jnp.float32)
+        add_row(sums, 7 + part, jnp.sum(grad_up, 0, keepdims=True))
+        low_u = grad_up.astype(jnp.bfloat16)
+        u_out[:, span] = low_u
+        grad_h1 = grad_h1 + back_mul(low_u, up_w[span, :])
+    hat1, scale1 = normed(r1[...])
+    grad_r1, gain1, shift1 = norm_back(grad_h1, hat1, scale1, small[5:6, :])
+    add_row(sums, 5, gain1)
+    add_row(sums, 6, shift1)
+    add_row(sums, 4, jnp.sum(grad_r1, 0, keepdims=True))
+    r1_grad[...] = grad_r1
+    low_a = grad_r1.astype(jnp.bfloat16)
+    a_out[...] = low_a
+    mixed_out[...] = back_mul(low_a, out_w[...]).astype(jnp.bfloat16)
+
+
+def feed_back(lengths, share, r1, r2, slope, weight, small):
+    tokens = r1.shape[0]
+    turns = LEN // TILE
+    return call(
+        feed_back_kernel,
+        "feed_forward_back",
+        (tokens // TILE,),
+        [
+            pl.BlockSpec((1, 8, D), lambda i, *_: (i // turns, 0, 0)),
+            rows_spec(D),
+            rows_spec(D),
+            rows_spec(FF),
+            weight_spec(D, 3),
+            weight_spec(FF, 1),
+            weight_spec(FF, 2),
+            whole_spec(small.shape),
+        ],
+        [
+            rows_spec(D),
+            rows_spec(FF),
+            rows_spec(D),
+            rows_spec(D),
+            rows_spec(D),
+            whole_spec((16, D)),
+        ],
+        [
+            jax.ShapeDtypeStruct((tokens, D), jnp.bfloat16),
+            jax.ShapeDtypeStruct((tokens, FF), jnp.bfloat16),
+            jax.ShapeDtypeStruct((tokens, D), jnp.float32),
+            jax.ShapeDtypeStruct((tokens, D), jnp.bfloat16),
+            jax.ShapeDtypeStruct((tokens, D), jnp.bfloat16),
+            jax.ShapeDtypeStruct((16, D), jnp.float32),
+        ],
+        prefetch=1,
+        flops=2 * tokens * D * (D + 2 * FF),
+        moved=tokens * D * 32,
+    )(lengths, share, r1, r2, slope, weight, weight, weight, small)
+
+
+def outer_kernel(act, low_f, low_h1, low_u, mixed, low_a, out):
+    step = pl.program_id(0)
+    parts = FF // D
+
+    @pl.when(step < parts)
+    def _():
+        out[...] = outer_sum(act[...], low_f[...]).astype(jnp.bfloat16)
+
+    @pl.when((step >= parts) & (step < 2 * parts))
+    def _():
+        out[...] = outer_sum(low_h1[...], low_u[...]).astype(jnp.bfloat16)
+
+    @pl.when(step == 2 * parts)
+    def _():
+        out[...] = outer_sum(mixed[...], low_a[...]).astype(jnp.bfloat16)
+
+
+def feed_weights(act, low_f, low_h1, low_u, mixed, low_a):
+    tokens = act.shape[0]
+    parts = FF // D
+    return call(
+        outer_kernel,
+        "feed_forward_weights",
+        (2 * parts + 1,),
+        [
+            pl.BlockSpec((tokens, D), lambda i: (0, jnp.minimum(i, parts - 1))),
+            whole_spec((tokens, D)),
+            whole_spec((tokens, D)),
+            pl.BlockSpec((tokens, D), lambda i: (0, jnp.clip(i - parts, 0, parts - 1))),
+            whole_spec((tokens, D)),
+            whole_spec((tokens, D)),
+        ],
+        [pl.BlockSpec((D, D), lambda i: (i, 0))],
+        [jax.ShapeDtypeStruct(((2 * parts + 1) * D, D), jnp.bfloat16)],
+        flops=2 * tokens * D * (D + 2 * FF),
+        moved=tokens * D * 24,
+    )(act, low_f, low_h1, low_u, mixed, low_a)[0]
+
+
+def attend_back_kernel(lengths, qkv, grad_mixed, logs, out, sums):
+    seq = qkv.shape[0]
+    bias = live_row(lengths[pl.program_id(0)], seq)
+    masks = head_masks(seq)
+
+    @pl.when(pl.program_id(0) == 0)
+    def _():
+        sums[...] = jnp.zeros_like(sums)
+
+    for pair in range(H // 2):
+        at = pair * 128
+        query = qkv[:, at : at + 128] * jnp.bfloat16(0.125)
+        keys = qkv[:, D + at : D + at + 128]
+        values = qkv[:, 2 * D + at : 2 * D + at + 128]
+        above = grad_mixed[:, at : at + 128]
+        queries = []
+        key_sum = value_sum = None
+        for side, mask in enumerate(masks):
+            head = 2 * pair + side
+            side_query = jnp.where(mask, query, jnp.zeros_like(query))
+            side_above = jnp.where(mask, above, jnp.zeros_like(above))
+            probs = jnp.exp(back_mul(side_query, keys) + (bias - logs[:, head : head + 1]))
+            grad_probs = back_mul(side_above, values)
+            inner = jnp.sum(probs * grad_probs, -1, keepdims=True)
+            grad_logits = (probs * (grad_probs - inner)).astype(jnp.bfloat16)
+            side_value = outer_sum(probs.astype(jnp.bfloat16), side_above)
+            side_key = outer_sum(grad_logits, side_query)
+            queries.append(matmul(grad_logits, keys))
+            value_sum = side_value if side == 0 else value_sum + side_value
+            key_sum = side_key if side == 0 else key_sum + side_key
+        grad_query = jnp.where(masks[0], queries[0], queries[1]) * 0.125
+        out[:, at : at + 128] = grad_query.astype(jnp.bfloat16)
+        out[:, D + at : D + at + 128] = key_sum.astype(jnp.bfloat16)
+        out[:, 2 * D + at : 2 * D + at + 128] = value_sum.astype(jnp.bfloat16)
+        sums[2:3, at : at + 128] += jnp.sum(grad_query, 0, keepdims=True)
+        sums[3:4, at : at + 128] += jnp.sum(value_sum, 0, keepdims=True)
+
+
+def attend_back(lengths, qkv, grad_mixed, logs, seq):
+    tokens = qkv.shape[0]
+    return call(
+        attend_back_kernel,
+        "attention_back",
+        (tokens // seq,),
+        [rows_spec(3 * D, seq), rows_spec(D, seq), rows_spec(128, seq)],
+        [rows_spec(3 * D, seq), whole_spec((16, D))],
+        [
+            jax.ShapeDtypeStruct((tokens, 3 * D), jnp.bfloat16),
+            jax.ShapeDtypeStruct((16, D), jnp.float32),
+        ],
+        prefetch=1,
+        flops=10 * tokens * seq * D,
+        moved=tokens * D * 16,
+    )(lengths, qkv, grad_mixed, logs)
+
+
+def embed_back_kernel(grad_r1, grad_qkv, weight, x, small, x_out, pos_out, sums):
+    spot, sentence = pl.program_id(0), pl.program_id(1)
+
+    @pl.when((spot == 0) & (sentence == 0))
+    def _():
+        sums[...] = jnp.zeros_like(sums)
+
+    @pl.when(sentence == 0)
+    def _():
+        pos_out[...] = jnp.zeros_like(pos_out)
+
+    grad_h0 = grad_r1[...]
+    for third in range(3):
+        span = slice(third * D, (third + 1) * D)
+        grad_h0 = grad_h0 + back_mul(grad_qkv[:, span], weight[span, :])
+    hat, scale = normed(x[...])
+    grad_x, gain, shift = norm_back(grad_h0, hat, scale, small[0:1, :])
+    add_row(sums, 0, gain)
+    add_row(sums, 1, shift)
+    x_out[...] = grad_x.astype(jnp.bfloat16)
+    pos_out[...] += grad_x
+
+
+def embed_back(grad_r1, grad_qkv, weight, x, small, seq):
+    tokens = x.shape[0]
+    turns = seq // TILE
+
+    def rows(width):
+        return pl.BlockSpec((TILE, width), lambda p, b: (b * turns + p, 0))
+
+    return call(
+        embed_back_kernel,
+        "embed_back",
+        (turns, tokens // seq),
+        [rows(D), rows(3 * D), whole_spec((3 * D, D)), rows(D), whole_spec(small.shape)],
+        [rows(D), pl.BlockSpec((TILE, D), lambda p, b: (p, 0)), whole_spec((16, D))],
+        [
+            jax.ShapeDtypeStruct((tokens, D), jnp.bfloat16),
+            jax.ShapeDtypeStruct((seq, D), jnp.float32),
+            jax.ShapeDtypeStruct((16, D), jnp.float32),
+        ],
+        flops=6 * tokens * D * D,
+        moved=tokens * D * 20,
+    )(grad_r1, grad_qkv, weight, x, small)
+
+
+def qkv_outer_kernel(h0, grad_qkv, out, low):
+    @pl.when(pl.program_id(0) == 0)
+    def _():
+        low[...] = h0[...].astype(jnp.bfloat16)
+
+    out[...] = outer_sum(low[...], grad_qkv[...]).astype(jnp.bfloat16)
+
+
+def qkv_weights(h0, grad_qkv):
+    tokens = h0.shape[0]
+    return call(
+        qkv_outer_kernel,
+        "qkv_weights",
+        (3,),
+        [whole_spec((tokens, D)), pl.BlockSpec((tokens, D), lambda i: (0, i))],
+        [pl.BlockSpec((D, D), lambda i: (i, 0))],
+        [jax.ShapeDtypeStruct((3 * D, D), jnp.bfloat16)],
+        scratch=[pltpu.VMEM((tokens, D), jnp.bfloat16)],
+        flops=6 * tokens * D * D,
+        moved=tokens * D * 12,
+    )(h0, grad_qkv)[0]
+
+
+def bucket_kernel(slot, grad, out):
+    size = out.shape[0]
+    at = pl.program_id(0) * size + lax.broadcasted_iota(jnp.int32, (size, slot.shape[1]), 0)
+    pick = (slot[...] == at).astype(jnp.bfloat16)
+    out[...] = matmul(pick, grad[...]).astype(jnp.bfloat16)
+
+
+def bucket_rows(slot, grad, count):
+    tokens = grad.shape[0]
+    size = count // 4
+    return call(
+        bucket_kernel,
+        "bucket_rows",
+        (count // size,),
+        [whole_spec((1, tokens)), whole_spec((tokens, D))],
+        [pl.BlockSpec((size, D), lambda i: (i, 0))],
+        [jax.ShapeDtypeStruct((count, D), jnp.bfloat16)],
+        flops=2 * tokens * D * count,
+        moved=tokens * D * 4,
+    )(slot, grad)[0]
+
+
+def scatter_kernel(row, got, out):
+    size = out.shape[0]
+    at = pl.program_id(0) * size + lax.broadcasted_iota(jnp.int32, (size, row.shape[1]), 0)
+    pick = (row[...] == at).astype(jnp.bfloat16)
+    out[...] = matmul(pick, got[...])
+
+
+def scatter_rows(row, got, rows):
+    size = math.gcd(rows, 480)
+    count = got.shape[0]
+    return call(
+        scatter_kernel,
+        "scatter_rows",
+        (rows // size,),
+        [whole_spec((1, count)), whole_spec((count, D))],
+        [pl.BlockSpec((size, D), lambda i: (i, 0))],
+        [jax.ShapeDtypeStruct((rows, D), jnp.float32)],
+        flops=2 * rows * D * count,
+        moved=rows * D * 8,
+    )(row, got)[0]
 
 
 def cosine(first, second):
@@ -127,6 +628,364 @@
     )(value)
 
 
+LOOP_SIZE = 8
+CHUNK = 480
+
+
+def grid_place(device):
+    z, y = device // 2, lax.rem(device, 2)
+    return z + y * (LOOP_SIZE - 1 - 2 * z)
+
+
+def grid_device(place):
+    place = lax.rem(place + LOOP_SIZE, LOOP_SIZE)
+    y = place // (LOOP_SIZE // 2)
+    return 2 * (place + y * (LOOP_SIZE - 1 - 2 * place)) + y
+
+
+def fetch_kernel(
+    cap,
+    own_rows,
+    ids,
+    pieces,
+    pos_low,
+    small,
+    table,
+    everyone,
+    weight,
+    pos,
+    smalls,
+    got,
+    held_rows,
+    asker_row,
+    asker_col,
+    most,
+    stage,
+    table_low,
+    sent,
+    before,
+    id_send,
+    id_recv,
+    hop_send,
+    hop_recv,
+    word_send,
+    word_recv,
+    small_send,
+    small_recv,
+    stage_sem,
+    local_sem,
+):
+    fsdp = LOOP_SIZE
+    row, col = lax.axis_index("dp"), lax.axis_index("fsdp")
+    count = lax.axis_size("dp") * fsdp
+    tokens = ids.shape[1]
+    me = row * fsdp + col
+    shard = pieces.shape[0] // 12
+    pos_rows = pos_low.shape[0]
+    quarter = row
+    place = grid_place(col)
+    core_mate = row + 1 - 2 * lax.rem(row, 2)
+    x_mate = lax.rem(row + 2, 4)
+    right = (row, grid_device(place + 1))
+    left = (row, grid_device(place - 1))
+
+    def anyone(step):
+        other = lax.rem(me + step, count)
+        return (other // fsdp, lax.rem(other, fsdp))
+
+    barrier = pltpu.get_barrier_semaphore()
+
+    def greet(step, carry):
+        pl.semaphore_signal(barrier, inc=1, device_id=anyone(step), device_id_type=MESH)
+        return carry
+
+    lax.fori_loop(1, count, greet, 0)
+    pl.semaphore_wait(barrier, count - 1)
+
+    def id_copy(step):
+        return pltpu.make_async_remote_copy(
+            src_ref=ids,
+            dst_ref=everyone.at[me],
+            send_sem=id_send.at[step],
+            recv_sem=id_recv.at[step],
+            device_id=anyone(step),
+            device_id_type=MESH,
+        )
+
+    def id_start(step, carry):
+        id_copy(step).start()
+        return carry
+
+    lax.fori_loop(1, count, id_start, 0)
+    everyone[pl.ds(me, 1)] = ids[...][None]
+
+    def weight_at(piece, block):
+        late = piece // 8
+        early_at = piece * D + block * shard
+        late_at = 8 * D + block * 4 * shard + (piece - 8) * shard
+        return pl.ds(pl.multiple_of(early_at + late * (late_at - early_at), 16), shard)
+
+    def pos_at(part, block):
+        size = pos_rows // 4
+        return pl.ds(pl.multiple_of(block * pos_rows + part * size, 16), size)
+
+    def hop(slot, block, part, target, own=False):
+        copies = []
+        for i in range(4):
+            if i < 3:
+                piece = part * 3 + i
+                there = weight.at[weight_at(piece, block), :]
+                here = there
+                if own:
+                    here = pieces.at[pl.ds(pl.multiple_of(piece * shard, 16), shard), :]
+            else:
+                there = pos.at[pos_at(part, block), :]
+                here = there
+                if own:
+                    size = pos_rows // 4
+                    here = pos_low.at[pl.ds(pl.multiple_of(part * size, 16), size), :]
+            copies.append(
+                pltpu.make_async_remote_copy(
+                    src_ref=here,
+                    dst_ref=there,
+                    send_sem=hop_send.at[4 * slot + i],
+                    recv_sem=hop_recv.at[4 * slot + i],
+                    device_id=target,
+                    device_id_type=MESH,
+                )
+            )
+        return copies
+
+    started = []
+
+    def begin(copies):
+        for copy in copies:
+            copy.start()
+        started.extend(copies)
+
+    def arrive(copies):
+        for copy in copies:
+            copy.wait_recv()
+
+    events = []
+    for k in range(1, LOOP_SIZE // 2 + 1):
+        events.append((k, 1))
+        if k < LOOP_SIZE // 2:
+            events.append((k, -1))
+    slot_of = {event: i for i, event in enumerate(events)}
+    total = len(events)
+
+    def block_of(event):
+        return grid_device(place - event[0] * event[1])
+
+    begin(hop(slot_of[(1, 1)], col, quarter, right, own=True))
+    begin(hop(slot_of[(1, -1)], col, quarter, left, own=True))
+
+    def small_copy(step):
+        return pltpu.make_async_remote_copy(
+            src_ref=small,
+            dst_ref=smalls.at[col],
+            send_sem=small_send.at[step],
+            recv_sem=small_recv.at[step],
+            device_id=(row, lax.rem(col + step, fsdp)),
+            device_id_type=MESH,
+        )
+
+    for step in range(1, fsdp):
+        small_copy(step).start()
+    local = [pltpu.make_async_copy(small, smalls.at[col], local_sem.at[0])]
+    local.append(
+        pltpu.make_async_copy(
+            pos_low, pos.at[pl.ds(pl.multiple_of(col * pos_rows, 16), pos_rows), :], local_sem.at[1]
+        )
+    )
+    local.append(
+        pltpu.make_async_copy(
+            pieces.at[pl.ds(8 * shard, 4 * shard), :],
+            weight.at[pl.ds(pl.multiple_of(8 * D + col * 4 * shard, 16), 4 * shard), :],
+            local_sem.at[2],
+        )
+    )
+    for piece in range(8):
+        local.append(
+            pltpu.make_async_copy(
+                pieces.at[pl.ds(piece * shard, shard), :],
+                weight.at[pl.ds(pl.multiple_of(piece * D + col * shard, 16), shard), :],
+                local_sem.at[3 + piece],
+            )
+        )
+    for copy in local:
+        copy.start()
+
+    chunks = own_rows // CHUNK
+
+    def stage_copy(chunk, slot):
+        return pltpu.make_async_copy(
+            table.at[pl.ds(chunk * CHUNK, CHUNK), :], stage.at[slot], stage_sem.at[slot]
+        )
+
+    stage_copy(0, 0).start()
+    across = lax.broadcasted_iota(jnp.int32, (tokens, tokens), 1)
+    down = lax.broadcasted_iota(jnp.int32, (tokens, tokens), 0)
+    before[...] = (down <= across).astype(jnp.float32).astype(jnp.bfloat16)
+    for chunk in range(chunks):
+        if chunk + 1 < chunks:
+            stage_copy(chunk + 1, (chunk + 1) % 2).start()
+        stage_copy(chunk, chunk % 2).wait()
+        table_low[chunk * CHUNK : (chunk + 1) * CHUNK, :] = stage[chunk % 2].astype(jnp.bfloat16)
+
+    mine = jnp.broadcast_to(ids[...], (8, tokens))
+    owner = lax.broadcasted_iota(jnp.int32, (8, tokens), 0)
+    hot = (mine >= owner * own_rows) & (mine < (owner + 1) * own_rows)
+    so_far = matmul(hot.astype(jnp.float32).astype(jnp.bfloat16), before[...]).astype(jnp.int32) - 1
+    slot = jnp.sum(
+        jnp.where(hot & (so_far < cap), owner * cap + so_far + 1, 0), 0, keepdims=True
+    ) - 1
+    asker_row[...] = slot
+    asker_col[...] = jnp.broadcast_to(slot, (128, tokens)).T
+
+    def word_copy(step):
+        return pltpu.make_async_remote_copy(
+            src_ref=sent.at[lax.rem(col + step, fsdp)],
+            dst_ref=got.at[col],
+            send_sem=word_send.at[step],
+            recv_sem=word_recv.at[step],
+            device_id=(row, lax.rem(col + step, fsdp)),
+            device_id_type=MESH,
+        )
+
+    def bucket(step):
+        asker = lax.rem(col + step, fsdp)
+        if step:
+            id_copy(lax.rem(me - row * fsdp - asker + count, count)).wait_recv()
+        theirs = everyone[row * fsdp + asker] - col * own_rows
+        held = (theirs >= 0) & (theirs < own_rows)
+        flag = jnp.broadcast_to(held, (8, tokens)).astype(jnp.float32).astype(jnp.bfloat16)
+        rank = matmul(flag, before[...])[0:1, :].astype(jnp.int32) - 1
+        rank = jnp.where(held, rank, -1)
+        hit = lax.broadcasted_iota(jnp.int32, (cap, tokens), 0) == rank
+        inner = jnp.sum(jnp.where(hit, theirs + 1, 0), 1, keepdims=True) - 1
+        held_rows[pl.ds(asker, 1)] = jnp.broadcast_to(inner, (cap, 128)).T[0:1, :][None]
+        rows = jnp.zeros((cap, D), jnp.float32)
+        wide = own_rows // 4
+        for part in range(4):
+            pick = inner == part * wide + lax.broadcasted_iota(jnp.int32, (cap, wide), 1)
+            rows = rows + matmul(
+                pick.astype(jnp.float32).astype(jnp.bfloat16),
+                table_low[part * wide : (part + 1) * wide, :],
+            )
+        sent[pl.ds(asker, 1)] = rows.astype(jnp.bfloat16)[None]
+        if step:
+            word_copy(step).start()
+
+    def spread(index):
+        event = events[index]
+        hops, sign = event
+        block = block_of(event)
+        here = hop(index, block, quarter, right)
+        arrive(here)
+        follow = (hops + 1, sign)
+        if follow in slot_of:
+            begin(hop(slot_of[follow], block, quarter, right if sign == 1 else left))
+        begin(hop(total + index, block, quarter, (x_mate, col)))
+        begin(hop(2 * total + index, block, quarter, (core_mate, col)))
+
+    def pass_on(index):
+        block = block_of(events[index])
+        arrive(hop(total + index, block, x_mate, (x_mate, col)))
+        begin(hop(3 * total + index, block, x_mate, (core_mate, col)))
+
+    for step in range(1, fsdp):
+        bucket(step)
+        if step >= 2 and step - 2 < total:
+            spread(step - 2)
+        if step >= 4 and step - 4 < total:
+            pass_on(step - 4)
+    bucket(0)
+    own_words = pltpu.make_async_copy(sent.at[col], got.at[col], local_sem.at[11])
+    own_words.start()
+    spread(fsdp - 2)
+    for index in range(fsdp - 4, total):
+        pass_on(index)
+
+    def id_end(step, carry):
+        copy = id_copy(step)
+        copy.wait_send()
+
+        @pl.when(lax.rem(lax.rem(me - step + count, count) // fsdp - row + count, count) != 0)
+        def _():
+            copy.wait_recv()
+
+        return carry
+
+    lax.fori_loop(1, count, id_end, 0)
+    ids_all = everyone[...]
+    largest = jnp.zeros((1, 1), jnp.int32)
+    for part in range(fsdp):
+        inside = (ids_all >= part * own_rows) & (ids_all < (part + 1) * own_rows)
+        number = jnp.sum(inside.astype(jnp.int32), -1)
+        largest = jnp.maximum(largest, jnp.max(number, 0, keepdims=True))
+    most[...] = jnp.broadcast_to(largest, (8, 128))
+    for index in range(total):
+        block = block_of(events[index])
+        arrive(hop(2 * total + index, block, core_mate, (core_mate, col)))
+        arrive(hop(3 * total + index, block, lax.rem(core_mate + 2, 4), (core_mate, col)))
+    for step in range(1, fsdp):
+        small_copy(step).wait()
+        word_copy(step).wait()
+    own_words.wait()
+    for copy in local:
+        copy.wait()
+    for copy in started:
+        copy.wait_send()
+
+
+def fetch(ids, pieces, pos_low, small, table, cap):
+    fsdp = lax.axis_size("fsdp")
+    count = lax.axis_size("dp") * fsdp
+    tokens = ids.shape[1]
+    own_rows = table.shape[0]
+    hops = 16 * (fsdp - 1)
+    vmem = pl.BlockSpec(memory_space=pltpu.VMEM)
+    anywhere = pl.BlockSpec(memory_space=pl.ANY)
+    return pl.pallas_call(
+        functools.partial(fetch_kernel, cap, own_rows),
+        name="fetch",
+        in_specs=[vmem, anywhere, anywhere, anywhere, anywhere],
+        out_specs=[vmem, anywhere, anywhere, anywhere, anywhere, vmem, vmem, vmem, vmem],
+        out_shape=[
+            jax.ShapeDtypeStruct((count, 1, tokens), jnp.int32),
+            jax.ShapeDtypeStruct((12 * D, D), jnp.bfloat16),
+            jax.ShapeDtypeStruct((fsdp * pos_low.shape[0], D), jnp.bfloat16),
+            jax.ShapeDtypeStruct((fsdp,) + small.shape, jnp.bfloat16),
+            jax.ShapeDtypeStruct((fsdp, cap, D), jnp.bfloat16),
+            jax.ShapeDtypeStruct((fsdp, 1, cap), jnp.int32),
+            jax.ShapeDtypeStruct((1, tokens), jnp.int32),
+            jax.ShapeDtypeStruct((tokens, 128), jnp.int32),
+            jax.ShapeDtypeStruct((8, 128), jnp.int32),
+        ],
+        scratch_shapes=[
+            pltpu.VMEM((2, CHUNK, D), jnp.float32),
+            pltpu.VMEM((own_rows, D), jnp.bfloat16),
+            pltpu.VMEM((fsdp, cap, D), jnp.bfloat16),
+            pltpu.VMEM((tokens, tokens), jnp.bfloat16),
+            pltpu.SemaphoreType.DMA((count,)),
+            pltpu.SemaphoreType.DMA((count,)),
+            pltpu.SemaphoreType.DMA((hops,)),
+            pltpu.SemaphoreType.DMA((hops,)),
+            pltpu.SemaphoreType.DMA((fsdp,)),
+            pltpu.SemaphoreType.DMA((fsdp,)),
+            pltpu.SemaphoreType.DMA((fsdp,)),
+            pltpu.SemaphoreType.DMA((fsdp,)),
+            pltpu.SemaphoreType.DMA((2,)),
+            pltpu.SemaphoreType.DMA((12,)),
+        ],
+        compiler_params=pltpu.CompilerParams(
+            collective_id=0, has_side_effects=True, vmem_limit_bytes=VMEM_GRANT
+        ),
+    )(ids, pieces, pos_low, small, table)
+
+
 LOOP = {8: (0, 2, 4, 6, 7, 5, 3, 1)}
 
 
@@ -244,12 +1103,10 @@
     )
 
 
-def cut_rows(grad, count, parts):
-    rows, width = grad.shape[0] // count, grad.shape[1] // parts
+def cut_parts(grad, count, parts):
+    width = grad.shape[-1]
     return (
-        grad.reshape(count, rows, parts, width)
-        .transpose(0, 2, 1, 3)
-        .reshape(count, parts * rows, width)
+        grad.reshape(parts, count, -1, width).transpose(1, 0, 2, 3).reshape(count, -1, width)
     )
 
 
@@ -318,43 +1175,87 @@
     return lax.all_to_all(blocks, "fsdp", 0, 0).reshape(rows.shape)
 
 
-def fetch_round(table_low, routes, turn):
-    sent = matmul(one_hot(routes.owner_rows(turn), routes.rows), table_low).astype(jnp.bfloat16)
-    got = exchange(sent)
-    return matmul(one_hot(routes.asker_slots(turn), got.shape[0]), got)
-
-
-def fetch_rows(table_low, routes):
-    first = fetch_round(table_low, routes, 0)
-
+def gather_table(table_low, routes, turn):
+    return matmul(one_hot(routes.owner_rows(turn), routes.rows), table_low).astype(jnp.bfloat16)
+
+
+def more_words(everyone, table, rounds, tokens):
     def more(carry):
-        return carry[0] < routes.rounds
+        return carry[0] < rounds
 
     def body(carry):
         turn, words = carry
-        return turn + 1, words + fetch_round(table_low, routes, turn)
-
-    return lax.while_loop(more, body, (jnp.int32(1), first))[1]
-
-
-def return_round(grad_low, routes, turn):
-    tokens = grad_low.shape[0]
-    sent = matmul(one_hot(routes.asker_tokens(turn), tokens), grad_low).astype(jnp.bfloat16)
-    got = exchange(sent)
-    return outer_sum(one_hot(routes.owner_rows(turn), routes.rows), got)
-
-
-def return_rows(grad_low, routes):
-    first = return_round(grad_low, routes, 0)
+        ids, turn = lax.optimization_barrier((everyone, turn))
+        routes = Routes(ids, table.shape[0])
+        got = exchange(gather_table(table.astype(jnp.bfloat16), routes, turn))
+        mine = matmul(one_hot(routes.asker_slots(turn), got.shape[0]), got)
+        return turn + 1, words + mine.astype(jnp.bfloat16)
+
+    start = (jnp.int32(1), jnp.zeros((tokens, D), jnp.bfloat16))
+    return lax.while_loop(more, body, start)[1]
+
+
+def return_round(grad_low, asker, held, rows):
+    sent = bucket_rows(asker, grad_low, held.shape[1])
+    return scatter_rows(held, exchange(sent), rows)
+
+
+def return_rows(grad_low, plan, rows):
+    first = return_round(grad_low, plan.asker_row, plan.held_rows, rows)
 
     def more(carry):
-        return carry[0] < routes.rounds
+        return carry[0] < plan.rounds
 
     def body(carry):
         turn, total = carry
-        return turn + 1, total + return_round(grad_low, routes, turn)
+        ids, turn = lax.optimization_barrier((plan.everyone, turn))
+        routes = Routes(ids, rows)
+        asker, held = routes.asker_slots(turn)[None, :], routes.owner_rows(turn)[None, :]
+        return turn + 1, total + return_round(grad_low, asker, held, rows)
 
     return lax.while_loop(more, body, (jnp.int32(1), first))[1]
+
+
+class Plan:
+    def __init__(self, ids, pieces, pos_low, small, table):
+        fsdp = lax.axis_size("fsdp")
+        tokens = ids.shape[0]
+        cap = bucket_size(tokens, fsdp)
+        cols = small.shape[1]
+        block = jnp.pad(small, ((0, 2), (0, 128 - cols)))
+        if fsdp == LOOP_SIZE and lax.axis_size("dp") == 4:
+            everyone, self.weight, self.pos, smalls, got, held, row, col, most = fetch(
+                ids.reshape(1, tokens), pieces, pos_low, block, table, cap
+            )
+            self.everyone = everyone.reshape(-1, tokens)
+            self.rounds = (most[0, 0] + cap - 1) // cap
+            self.asker_row, self.asker_col = row, col
+            self.held_rows = held.reshape(1, -1)
+            self.got = got.reshape(-1, D)
+        else:
+            self.everyone = gather_small(ids.reshape(-1, 128), True, 0).reshape(-1, tokens)
+            routes = Routes(self.everyone, table.shape[0])
+            self.rounds = routes.rounds
+            slot = routes.asker_slots(0)
+            self.asker_row = slot[None, :]
+            self.asker_col = jnp.broadcast_to(slot[:, None], (tokens, 128))
+            self.held_rows = routes.owner_rows(0)[None, :]
+            self.got = exchange(gather_table(table.astype(jnp.bfloat16), routes, 0))
+            both = lax.all_gather(pieces, "fsdp", axis=0)
+            early = pieces.shape[0] * 2 // 3
+            self.weight = jnp.concatenate(
+                [
+                    both[:, :early].reshape(fsdp, 8, -1, D).transpose(1, 0, 2, 3).reshape(-1, D),
+                    both[:, early:].reshape(-1, D),
+                ],
+                0,
+            )
+            self.pos = lax.all_gather(pos_low, "fsdp", axis=0, tiled=True)
+            smalls = lax.all_gather(block, "fsdp", axis=0)
+        self.small = (
+            smalls[:, :, :cols].transpose(1, 0, 2).reshape(16, D).astype(jnp.float32)
+        )
+        self.extra = more_words(self.everyone, table, self.rounds, tokens)
 
 
 def sum_groups(table):
@@ -369,101 +1270,6 @@
     return jnp.concatenate(
         [jnp.where(core == 0, total, other), jnp.where(core == 0, other, total)], 0
     ).astype(jnp.float32)
-
-
-def attention_logits(query, keys, live_bias, scale):
-    raw = jnp.einsum("bqhd,bkhd->bhqk", query, keys, preferred_element_type=jnp.float32) * scale
-    return raw + live_bias[:, None, None, :]
-
-
-def layer_forward(x, params, live_bias, batch, seq):
-    qkv_w, out_w, up_w, down_w, small = params
-    width = x.shape[1]
-    size = width // H
-    scale = size ** (-0.5)
-    h0 = layer_norm(x, small[0], small[1])
-    qkv_bias = jnp.concatenate([small[2], jnp.zeros_like(small[2]), small[3]])
-    qkv = matmul(h0.astype(jnp.bfloat16), qkv_w) + qkv_bias
-    parts = qkv.astype(jnp.bfloat16).reshape(batch, seq, 3, H, size)
-    query, keys, values = (parts[:, :, 0], parts[:, :, 1], parts[:, :, 2])
-    logits = attention_logits(query, keys, live_bias, scale)
-    top = jnp.max(logits, -1, keepdims=True)
-    total_log = top + jnp.log(jnp.sum(jnp.exp(logits - top), -1, keepdims=True))
-    probs = jnp.exp(logits - total_log).astype(jnp.bfloat16)
-    mixed = jnp.einsum("bhqk,bkhd->bqhd", probs, values, preferred_element_type=jnp.float32)
-    mixed = mixed.astype(jnp.bfloat16).reshape(-1, width)
-    first_sum = h0 + (matmul(mixed, out_w) + small[4])
-    h1 = layer_norm(first_sum, small[5], small[6])
-    up = matmul(h1.astype(jnp.bfloat16), up_w) + small[7:11].reshape(-1)
-    act = gelu_exact(up).astype(jnp.bfloat16)
-    second_sum = h1 + (matmul(act, down_w) + small[11])
-    h2 = layer_norm(second_sum, small[12], small[13])
-    kept = (x, h0, query, keys, values, total_log, mixed, first_sum, h1, up, act, second_sum)
-    return (h2, kept)
-
-
-def layer_backward(grad_h2, kept, params, live_bias):
-    qkv_w, out_w, up_w, down_w, small = params
-    x, h0, query, keys, values, total_log, mixed, first_sum, h1, up, act, second_sum = kept
-    batch, seq, heads, size = query.shape
-    width = heads * size
-    scale = size ** (-0.5)
-    _, pull_two = jax.vjp(layer_norm, second_sum, small[12], small[13])
-    grad_r2, grad_g2, grad_b2 = pull_two(grad_h2)
-    grad_ffn = grad_r2.astype(jnp.bfloat16)
-    grad_down = outer_sum(act, grad_ffn)
-    grad_act = back_mul(grad_ffn, down_w)
-    _, pull_gelu = jax.vjp(gelu_exact, up)
-    grad_up = pull_gelu(grad_act)[0]
-    grad_upb = grad_up.astype(jnp.bfloat16)
-    grad_upw = outer_sum(h1.astype(jnp.bfloat16), grad_upb)
-    grad_h1 = grad_r2 + back_mul(grad_upb, up_w)
-    _, pull_one = jax.vjp(layer_norm, first_sum, small[5], small[6])
-    grad_r1, grad_g1, grad_b1 = pull_one(grad_h1)
-    grad_att = grad_r1.astype(jnp.bfloat16)
-    grad_outw = outer_sum(mixed, grad_att)
-    grad_mixed = back_mul(grad_att, out_w).astype(jnp.bfloat16).reshape(batch, seq, heads, size)
-    logits = attention_logits(query, keys, live_bias, scale)
-    probs = jnp.exp(logits - total_log)
-    grad_probs = jnp.einsum(
-        "bqhd,bkhd->bhqk", grad_mixed, values, preferred_element_type=jnp.float32
-    )
-    grad_values = jnp.einsum(
-        "bhqk,bqhd->bkhd",
-        probs.astype(jnp.bfloat16),
-        grad_mixed,
-        preferred_element_type=jnp.float32,
-    )
-    inner = jnp.sum(probs * grad_probs, -1, keepdims=True)
-    grad_logits = (probs * (grad_probs - inner)).astype(jnp.bfloat16)
-    grad_query = (
-        jnp.einsum("bhqk,bkhd->bqhd", grad_logits, keys, preferred_element_type=jnp.float32) * scale
-    )
-    grad_keys = (
-        jnp.einsum("bhqk,bqhd->bkhd", grad_logits, query, preferred_element_type=jnp.float32)
-        * scale
-    )
-    grad_qkv = jnp.stack([grad_query, grad_keys, grad_values], 2).reshape(-1, 3 * width)
-    grad_qkvb = grad_qkv.astype(jnp.bfloat16)
-    grad_qkvw = outer_sum(h0.astype(jnp.bfloat16), grad_qkvb)
-    grad_h0 = grad_r1 + back_mul(grad_qkvb, qkv_w)
-    _, pull_zero = jax.vjp(layer_norm, x, small[0], small[1])
-    grad_x, grad_g0, grad_b0 = pull_zero(grad_h0)
-    column_sums = jnp.sum(grad_qkv, 0)
-    head_rows = jnp.stack(
-        [
-            grad_g0,
-            grad_b0,
-            column_sums[:width],
-            column_sums[2 * width :],
-            jnp.sum(grad_r1, 0),
-            grad_g1,
-            grad_b1,
-        ]
-    )
-    tail_rows = jnp.stack([jnp.sum(grad_r2, 0), grad_g2, grad_b2])
-    grad_small = jnp.concatenate([head_rows, jnp.sum(grad_up, 0).reshape(4, width), tail_rows], 0)
-    return (grad_x, (grad_qkvw, grad_outw, grad_upw, grad_down, grad_small))
 
 
 def renew(weight, moment, average, grad, factor):
@@ -503,78 +1309,68 @@
     batch, seq = token_ids.shape
     width = D
     fsdp = lax.axis_size("fsdp")
-    me = lax.axis_index("fsdp")
-    pos_low = pos_table.astype(jnp.bfloat16)
-    qkv_low = split_rows(qkv_weight.astype(jnp.bfloat16), 3)
-    out_low = out_weight.astype(jnp.bfloat16)
-    up_low = split_rows(up_weight.astype(jnp.bfloat16), 4)
-    down_low = down_weight.astype(jnp.bfloat16)
-    small_low = small_params.astype(jnp.bfloat16)
-    word_low = word_table.astype(jnp.bfloat16)
     tokens = batch * seq
-    everyone = gather_small(token_ids.reshape(-1, 128), True, 0).reshape(-1, tokens)
-    routes = Routes(everyone, word_table.shape[0])
     shard = qkv_weight.shape[0]
     pos_rows = pos_table.shape[0]
     small_cols = small_params.shape[1]
-    small_block = jnp.pad(small_low, ((0, 2), (0, width - small_cols)))
-    tail = round_up(max(2 * shard, shard + pos_rows + 16), 16)
-    first_a = pad_rows(qkv_low[: 2 * shard], tail)
-    first_b = pad_rows(jnp.concatenate([qkv_low[2 * shard :], pos_low, small_block], 0), tail)
-    half = shard // 2
-    second_a = jnp.concatenate([down_low, out_low[:half]], 0)
-    second_b = jnp.concatenate([up_low, out_low[half:]], 0)
-    got_a, got_b = gather_halves(first_a, first_b, 1)
-    words = fetch_rows(word_low, routes)
-    got_c, got_d = gather_halves(second_a, second_b, -1)
-    qkv_full = join_rows(
-        jnp.concatenate([got_a[:, : 2 * shard], got_b[:, :shard]], 1), 3
-    )
-    pos_full = got_b[:, shard : shard + pos_rows].reshape(-1, width)
-    small_full = (
-        got_b[:, shard + pos_rows : shard + pos_rows + 14, :small_cols]
-        .transpose(1, 0, 2)
-        .reshape(14, width)
-    )
-    down_rows = down_weight.shape[0]
-    down_full = got_c[:, :down_rows].reshape(-1, width)
-    up_full = join_rows(got_d[:, :down_rows], 4)
-    out_full = jnp.concatenate([got_c[:, down_rows:], got_d[:, down_rows:]], 1).reshape(-1, width)
-    params = (qkv_full, out_full, up_full, down_full, small_full.astype(jnp.float32))
-    x = (words.reshape(batch, seq, width) + pos_full.astype(jnp.float32)[None]).reshape(
-        -1, width
-    )
-    live = lax.iota(jnp.int32, seq)[None, :] < lengths[:, None]
-    live_bias = jnp.where(live, 0.0, -1000000000.0).astype(jnp.float32)
-    live_f = live.astype(jnp.float32)
-    counts = lengths.astype(jnp.float32)
-    h2, kept = layer_forward(x, params, live_bias, batch, seq)
-    pooled = jnp.sum(h2.reshape(batch, seq, width) * live_f[:, :, None], 1) / counts[:, None]
-    pooled_all = gather_small(pooled.reshape(-1, 128), True, 1).reshape(-1, width)
+    pieces = jnp.concatenate(
+        [
+            split_rows(qkv_weight.astype(jnp.bfloat16), 3),
+            out_weight.astype(jnp.bfloat16),
+            split_rows(up_weight.astype(jnp.bfloat16), 4),
+            down_weight.astype(jnp.bfloat16),
+        ],
+        0,
+    )
+    plan = Plan(
+        token_ids.reshape(-1),
+        pieces,
+        pos_table.astype(jnp.bfloat16),
+        small_params.astype(jnp.bfloat16),
+        word_table,
+    )
+    weight, small_full = plan.weight, plan.small
+    half_pos = pos_rows // 2
+    x, h0, qkv = embed(plan.asker_col, plan.got, plan.extra, plan.pos, weight, small_full)
+    mixed, logs = attend(lengths, qkv, seq)
+    r1, low_h1, act, slope, r2, pooled = feed(lengths, mixed, h0, weight, small_full)
+    pooled_all = gather_small(pooled[:, 0].reshape(-1, 128), True, 1).reshape(-1, width)
     loss, pull_loss = jax.vjp(lambda rows: pair_loss(rows, pair_ids, scores), pooled_all)
     grad_all = pull_loss(jnp.ones((), jnp.float32))[0]
     grad_pooled = lax.dynamic_slice_in_dim(
         grad_all, lax.axis_index(("dp", "fsdp")) * batch, batch, 0
     )
-    grad_h2 = (live_f[:, :, None] * (grad_pooled / counts[:, None])[:, None, :]).reshape(-1, width)
-    grad_x, layer_grads = layer_backward(grad_h2, kept, params, live_bias)
-    grad_qkvw, grad_outw, grad_upw, grad_downw, grad_small = layer_grads
+    share = jnp.broadcast_to(
+        (grad_pooled / lengths.astype(jnp.float32)[:, None])[:, None, :], (batch, 8, width)
+    )
+    low_f, low_u, grad_r1, low_a, grad_mixed, sums_feed = feed_back(
+        lengths, share, r1, r2, slope, weight, small_full
+    )
+    feed_grads = feed_weights(act, low_f, low_h1, low_u, mixed, low_a)
     sum_down, sum_up = reduce_halves(
-        cut_rows(grad_downw, fsdp, 1), cut_rows(grad_upw, fsdp, 4), 1
-    )
-    grad_table = return_rows(grad_x.astype(jnp.bfloat16), routes)
-    grad_pos = jnp.sum(grad_x.reshape(batch, seq, width), 0)
-    qkv_cut = cut_rows(grad_qkvw, fsdp, 3)
+        feed_grads[:FF].reshape(fsdp, -1, width),
+        cut_parts(feed_grads[FF : 2 * FF], fsdp, 4),
+        1,
+    )
+    grad_qkv, sums_attend = attend_back(lengths, qkv, grad_mixed, logs, seq)
+    grad_x, grad_pos, sums_embed = embed_back(grad_r1, grad_qkv, weight, x, small_full, seq)
+    grad_table = return_rows(grad_x, plan, word_table.shape[0])
+    qkv_cut = cut_parts(qkv_weights(h0, grad_qkv), fsdp, 3)
+    grad_small = sums_feed + sums_attend + sums_embed
     small_cut = jnp.pad(
-        grad_small.reshape(14, fsdp, small_cols).transpose(1, 0, 2),
-        ((0, 0), (0, 2), (0, width - small_cols)),
-    )
-    half_pos = pos_rows // 2
-    pos_cut = grad_pos.reshape(fsdp, pos_rows, width)
+        grad_small.reshape(16, fsdp, small_cols).transpose(1, 0, 2),
+        ((0, 0), (0, 0), (0, width - small_cols)),
+    ).astype(jnp.bfloat16)
+    pos_cut = grad_pos.reshape(fsdp, pos_rows, width).astype(jnp.bfloat16)
     low_cut = jnp.concatenate([qkv_cut[:, : 2 * shard], pos_cut[:, :half_pos], small_cut], 1)
     high_cut = pad_rows(
         jnp.concatenate(
-            [qkv_cut[:, 2 * shard :], cut_rows(grad_outw, fsdp, 1), pos_cut[:, half_pos:]], 1
+            [
+                qkv_cut[:, 2 * shard :],
+                feed_grads[2 * FF :].reshape(fsdp, shard, width),
+                pos_cut[:, half_pos:],
+            ],
+            1,
         ),
         low_cut.shape[1],
     )

time: 900 us -> 584 us (0.65)
  Pallas kernels: 32.8 us -> 299 us
  matrix products: 230 us -> 0 us
  local copies, waits for them, and re-layouts: 177 us -> 45.6 us
  other arithmetic: 211 us -> 112 us
  waiting for transfers between devices: 142 us -> 52.9 us
  starting transfers between devices: 56.7 us -> 27.7 us
    pallas_call x0 -> x11, Pallas kernels: none -> 273 us  [the longest x1 115 us: fetch(): pl.pallas_call(functools.partial(fetch_kernel, cap, own_rows), name='fetc...]
    dot_general x22 -> x0, matrix products: 230 us -> none  [the longest x7 71.8 us: matmul(): return jnp.dot(left, right, preferred_element_type=jnp.float32)]
    ppermute x28 -> x14, waiting for transfers between devices: 121 us -> 39.1 us  [shift(): lax.ppermute(value, 'fsdp', [(loop[i], loop[(i + step) % size]) for i in...]
    reduce_sum x18 -> x0, other arithmetic: 39.4 us -> none  [the longest x1 11 us: layer_forward(): total_log = top + jnp.log(jnp.sum(jnp.exp(logits - top), -1, keepdims=True))]
    reshape x7 -> x4, local copies, waits for them, and re-layouts: 38.7 us -> 3.98 us  [the longest x2 2.31 us: shards(): grad_small.reshape(16, fsdp, small_cols).transpose(1, 0, 2)]
    convert_element_type x16 -> x8, other arithmetic: 42.4 us -> 11.1 us  [the longest x1 7.56 us: body(): got = exchange(gather_table(table.astype(jnp.bfloat16), routes, turn))]
    unnamed x319 -> x139, local copies, waits for them, and re-layouts: 39.1 us -> 10.1 us
    ppermute x28 -> x14, starting transfers between devices: 42.8 us -> 17.3 us  [shift(): lax.ppermute(value, 'fsdp', [(loop[i], loop[(i + step) % size]) for i in...]
  transfers between devices with their start and end apart: 41 -> 24, of which waited for: 15 -> 9; matrix products, arithmetic and copies ran while one was open for 34% -> 13% of each run, Pallas kernels for 2% -> 7%
where the time goes in v2:
time: 584 us; the launch traced here: 573 us
  Pallas kernels  299 us (51%)
  other arithmetic  112 us (19%)
  waiting for transfers between devices  52.9 us (9%)
  local copies, waits for them, and re-layouts  45.6 us (8%)
  between operations  35 us (6%)
  starting transfers between devices  27.7 us (5%)
    pallas_call x1, Pallas kernels, fetch(): pl.pallas_call(functools.partial(fetch_kernel, cap, own_rows), name='fetc...  115 us
    ppermute x14, waiting for transfers between devices, shift(): lax.ppermute(value, 'fsdp', [(loop[i], loop[(i + step) % size]) for i in...  39.1 us
    add x7, other arithmetic, renew(): return (fresh, buffer, KEEP * average + (1.0 - KEEP) * fresh)  38.7 us
    pallas_call x1, Pallas kernels, attend_back(): call(attend_back_kernel, 'attention_back', (tokens // seq,), [rows_spec(3...  26.2 us
    pallas_call x2, Pallas kernels, gather_small(): pl.pallas_call(functools.partial(gather_kernel, (dp, fsdp), whole), out_s...  26.2 us
    pallas_call x1, Pallas kernels, feed(): call(feed_kernel, 'feed_forward', (tokens // TILE,), [rows_spec(D), rows_...  24.6 us
    pallas_call x1, Pallas kernels, feed_back(): call(feed_back_kernel, 'feed_forward_back', (tokens // TILE,), [pl.BlockS...  22.7 us
    pallas_call x1, Pallas kernels, feed_weights(): call(outer_kernel, 'feed_forward_weights', (2 * parts + 1,), [pl.BlockSpe...  19.2 us
  transfers between devices with their start and end apart: 24, of which 9 were waited for; matrix products, arithmetic and copies ran while one was open for 13% of the time, Pallas kernels for 7%

profile of v2, /device:TPU:0, one launch (start us, length us, event | category | flops | bytes accessed | tf_op | source)
XLA Modules:
  0.0 572.8 jit_solution(14133700953349548837)
XLA Ops:
  4.9 115.0 %fetch.1 = (s32[32,1,1024]{2,1,0:T(1,128)}, bf16[9216,768]{1,0:T(8,128)(2,1)}, bf16[512,768]{1,0:T(8,128)(2,1)}, bf16[8,16,128]{2,1,0:T(8,128)(2,1)}, bf16[8,192...) custom-call(s32[1,1024]{1,0:T(1,128)} %bitcast.239, ...), custom_call_target="tpu_custom_call" | custom-call | tf_op jit(solution)/shard_map/fetch/pallas_call | solution.py:951
  121.9 7.6 %convert_element_type.323 = bf16[3840,768]{1,0:T(8,128)(2,1)} convert(f32[3840,768]{1,0:T(8,128)} %table.1) | non-fusion elementwise | flops 2949120 | bytes 17694720 | tf_op jit(solution)/shard_map/while/body/convert_element_type | solution.py:1190
  131.7 13.6 %embed_qkv.1 = (f32[1024,768]{1,0:T(8,128)}, f32[1024,768]{1,0:T(8,128)}, bf16[1024,2304]{1,0:T(8,128)(2,1)}) custom-call(s32[1024,128]{1,0:T(8,128)} %get-tuple-element.241.slot, bf16[1536,768]{1,0:T(8,128)(2,1)} %bitcast.243, bf16[1024,768]{1,0:T(8,128)(2,1)} %get-tuple-element.245.extra, bf16[512,768]{1,0:T(8,128)(2,1)} %get-tuple-element.246.pos, ...), custom_call_target="tpu_custom_call" | custom-call | flops 6039797760 | bytes 15728640 | tf_op jit(solution)/shard_map/embed_qkv/pallas_call | solution.py:117
  145.3 14.2 %attention.1 = (bf16[1024,768]{1,0:T(8,128)(2,1)}, f32[1024,128]{1,0:T(8,128)}) custom-call(s32[2]{0:T(128)} %lengths.7, bf16[1024,2304]{1,0:T(8,128)(2,1)} %get-tuple-element.249.qkv), custom_call_target="tpu_custom_call" | custom-call | flops 1610612736 | bytes 6291456 | tf_op jit(solution)/shard_map/attention/pallas_call | solution.py:177
  159.5 24.6 %feed_forward.1 = (f32[1024,768]{1,0:T(8,128)}, bf16[1024,768]{1,0:T(8,128)(2,1)}, bf16[1024,3072]{1,0:T(8,128)(2,1)}, bf16[1024,3072]{1,0:T(8,128)(2,1)}, f32[1024,768]{1,0:T(8,128)}, /*index=5*/f32[2,8,768]{2,1,0:T(8,128)}) custom-call(s32[2]{0:T(128)} %lengths.7, bf16[1024,768]{1,0:T(8,128)(2,1)} %get-tuple-element.250.mixed, ...), custom_call_target="tpu_custom_call" | custom-call | flops 10871635968 | bytes 25165824 | tf_op jit(solution)/shard_map/feed_forward/pallas_call | solution.py:231
  185.5 18.1 %shard_map.452 = f32[32,12,128]{2,1,0:T(8,128)} custom-call(f32[12,128]{1,0:T(8,128)} %reshape_squeeze.3.src), custom_call_target="tpu_custom_call" | custom-call | tf_op jit(solution)/shard_map/pallas_call | solution.py:617
  211.0 22.7 %feed_forward_back.1 = (bf16[1024,768]{1,0:T(8,128)(2,1)}, bf16[1024,3072]{1,0:T(8,128)(2,1)}, f32[1024,768]{1,0:T(8,128)}, bf16[1024,768]{1,0:T(8,128)(2,1)}, b...) custom-call(s32[2]{0:T(128)} %lengths.7, f32[2,8,768]{2,1,0:T(8,128)} %broadcast_in_dim.111.share, ...), custom_call_target="tpu_custom_call" | custom-call | flops 10871635968 | bytes 25165824 | tf_op jit(solution)/shard_map/feed_forward_back/pallas_call | solution.py:307
  233.7 26.2 %attention_back.1 = (bf16[1024,2304]{1,0:T(8,128)(2,1)}, f32[16,768]{1,0:T(8,128)}) custom-call(s32[2]{0:T(128)} %lengths.7, bf16[1024,2304]{1,0:T(8,128)(2,1)} %get-tuple-element.249.qkv, bf16[1024,768]{1,0:T(8,128)(2,1)} %get-tuple-element.259.grad_mixed, f32[1024,128]{1,0:T(8,128)} %get-tuple-element.260.logs), custom_call_target="tpu_custom_call" | custom-call | flops 4026531840 | bytes 12582912 | tf_op jit(solution)/shard_map/attention_back/pallas_call | solution.py:422
  259.9 10.5 %embed_back.1 = (bf16[1024,768]{1,0:T(8,128)(2,1)S(1)}, f32[512,768]{1,0:T(8,128)}, f32[16,768]{1,0:T(8,128)}) custom-call(f32[1024,768]{1,0:T(8,128)} %get-tuple-element.258.grad_r1, bf16[1024,2304]{1,0:T(8,128)(2,1)} %get-tuple-element.261.grad_qkv, bf16[9216,768]{1,0:T(8,128)(2,1)} %get-tuple-element.247.weight.out_w.up_w.down_w, ...), custom_call_target="tpu_custom_call" | custom-call | flops 3623878656 | bytes 15728640 | tf_op jit(solution)/shard_map/embed_back/pallas_call | solution.py:468
  270.4 4.9 bucket_rows.6
  275.3 4.4 all-to-all-start.2
  279.7 19.2 %feed_forward_weights.1 = bf16[6912,768]{1,0:T(8,128)(2,1)} custom-call(bf16[1024,3072]{1,0:T(8,128)(2,1)} %get-tuple-element.269.act, bf16[1024,768]{1,0:T(8,128)(2,1)} %get-tuple-element.270.low_f, bf16[1024,768]{1,0:T(8,128)(2,1)} %get-tuple-element.271.low_h1, bf16[1024,3072]{1,0:T(8,128)(2,1)} %get-tuple-element.272.low_u, ...), custom_call_target="tpu_custom_call" | custom-call | flops 10871635968 | bytes 18874368 | tf_op jit(solution)/shard_map/feed_forward_weights/pallas_call | solution.py:363
  299.0 6.6 %fusion.73 = (bf16[3072,768]{1,0:T(8,128)(2,1)S(1)}, bf16[3072,768]{1,0:T(8,128)(2,1)}) fusion(bf16[6912,768]{1,0:T(8,128)(2,1)} %feed_forward_weights.1), kind=kLoop, calls=%fused_computation.220 | loop fusion | bytes 18874368 | tf_op jit(solution)/shard_map/slice | solution.py:1352
  305.5 2.5 copy.73
  308.1 5.0 bitcast_select_fusion
  315.3 8.3 %qkv_weights.1 = bf16[2304,768]{1,0:T(8,128)(2,1)} custom-call(f32[1024,768]{1,0:T(8,128)} %get-tuple-element.251.h0, bf16[1024,2304]{1,0:T(8,128)(2,1)} %get-tuple-element.261.grad_qkv), custom_call_target="tpu_custom_call" | custom-call | flops 3623878656 | bytes 9437184 | tf_op jit(solution)/shard_map/qkv_weights/pallas_call | solution.py:494
  323.6 2.2 copy.71
  327.9 1.5 reshape.568
  330.2 1.5 convert_element_type.335
  331.8 2.0 broadcast_select_fusion
  334.6 13.5 %scatter_rows.6 = f32[3840,768]{1,0:T(8,128)} custom-call(s32[1,1536]{1,0:T(1,128)} %reshape.563.row, bf16[1536,768]{1,0:T(8,128)(2,1)} %bitcast.25.got), custom_call_target="tpu_custom_call" | custom-call | flops 9059696640 | bytes 23592960 | tf_op jit(solution)/shard_map/scatter_rows/pallas_call | solution.py:539
  348.3 4.7 dynamic-slice_convert_fusion
  368.5 3.1 add_convert_fusion.1
  372.4 1.6 collective-permute-start.4
  374.0 1.5 copy-done
  375.5 4.4 add_convert_fusion.3
  380.0 1.4 collective-permute-start.1
  381.4 5.6 add_convert_fusion
  388.0 1.6 collective-permute-start.14
  389.6 1.9 fusion.42
  392.3 9.3 %collective-permute-done.14 = bf16[384,768]{1,0:T(8,128)(2,1)S(1)} collective-permute-done((bf16[384,768]{1,0:T(8,128)(2,1)S(1)}, bf16[384,768]{1,0:T(8,128)(2,1)S(1)}, u32[]{:S(2)}, u32[]{:S(2)}) %collective-permute-start.14) | collective-permute-done | bytes 589856 | tf_op jit(solution)/shard_map/ppermute | solution.py:1013
  402.5 1.6 collective-permute-start.15
  408.0 1.5 collective-permute-start.8
  411.8 7.2 %collective-permute-done.15 = bf16[384,768]{1,0:T(8,128)(2,1)S(1)} collective-permute-done((bf16[384,768]{1,0:T(8,128)(2,1)}, bf16[384,768]{1,0:T(8,128)(2,1)S(1)}, u32[]{:S(2)}, u32[]{:S(2)}) %collective-permute-start.15) | collective-permute-done | bytes 589856 | tf_op jit(solution)/shard_map/ppermute | solution.py:1013
  420.2 1.7 collective-permute-start.16
  426.9 2.0 fusion.44
  428.9 1.6 collective-permute-start.9
  431.0 3.9 collective-permute-done.18
  434.8 4.7 collective-permute-done.16
  439.5 2.3 fusion.37
  441.9 1.6 collective-permute-start.19
  443.5 2.6 collective-permute-done.1
  446.1 3.5 add_convert_fusion.2
  449.7 2.1 fusion.41
  451.7 1.6 collective-permute-start.10
  453.4 1.5 collective-permute-start.17
  454.8 2.0 fusion.34
  459.6 3.9 collective-permute-done.10
  464.8 1.5 collective-permute-start.11
  466.3 9.0 %collective-permute-done.17 = bf16[384,768]{1,0:T(8,128)(2,1)S(1)} collective-permute-done((bf16[384,768]{1,0:T(8,128)(2,1)}, bf16[384,768]{1,0:T(8,128)(2,1)S(1)}, u32[]{:S(2)}, u32[]{:S(2)}) %collective-permute-start.17) | collective-permute-done | bytes 589856 | tf_op jit(solution)/shard_map/ppermute | solution.py:1013
  476.1 1.6 fusion.39
  477.8 1.5 collective-permute-start.21
  481.4 11.2 %collective-permute-done.21 = bf16[384,768]{1,0:T(8,128)(2,1)} collective-permute-done((bf16[384,768]{1,0:T(8,128)(2,1)S(1)}, bf16[384,768]{1,0:T(8,128)(2,1)}, u32[]{:S(2)}, u32[]{:S(2)}) %collective-permute-start.21) | collective-permute-done | bytes 589856 | tf_op jit(solution)/shard_map/ppermute | solution.py:1005
  492.6 1.4 add_convert_fusion.4
  499.4 1.7 fusion.32
  501.2 2.2 broadcast_select_fusion.2
  503.4 1.6 copy-done.2
  505.0 3.6 fusion.19
  513.8 8.1 %shard_map.453 = f32[8,8,128]{2,1,0:T(8,128)} custom-call(f32[8,128]{1,0:T(8,128)} %broadcast_in_dim.112.src), custom_call_target="tpu_custom_call" | custom-call | tf_op jit(solution)/shard_map/pallas_call | solution.py:617
  531.6 1.9 multiply_add_fusion.6
  534.4 26.4 %multiply_add_fusion = (f32[3840,768]{1,0:T(8,128)}, f32[3840,768]{1,0:T(8,128)}, f32[3840,768]{1,0:T(8,128)}) fusion(f32[3840,768]{1,0:T(8,128)} %param.51, f32[3840,768]{1,0:T(8,128)} %table.1, bf16[1920,768]{1,0:T(8,128)(2,1)} %copy-done.2, bf16[1920,768]{1,0:T(8,128)(2,1)S(1)} %get-tuple-element.337, f32[]{:T(128)S(6)} %min.3, f32[3840,768]{1,0:T(8,128)} %param.44), kind=kLoop, calls=%fused_computation.62 | loop fusion | flops 41287680 | bytes 76677120 | tf_op jit(solution)/shard_map/add | solution.py:1279
  560.9 4.2 multiply_add_fusion.1
  565.2 2.2 multiply_add_fusion.2
  568.4 1.7 multiply_add_fusion.4
  (232 shorter events, 53.3 us)
Async XLA Ops:
  121.9 7.6 %copy-start.45 = (s32[32,1,1024]{2,1,0:T(1,128)S(1)}, s32[32,1,1024]{2,1,0:T(1,128)}, u32[]{:S(2)}) copy-start(s32[32,1,1024]{2,1,0:T(1,128)} %get-tuple-element.244) | copy-start | bytes 393220
  121.9 7.6 %copy-start.50 = (bf16[8,16,128]{2,1,0:T(8,128)(2,1)S(1)}, bf16[8,16,128]{2,1,0:T(8,128)(2,1)}, u32[]{:S(2)}) copy-start(bf16[8,16,128]{2,1,0:T(8,128)(2,1)} %get-tuple-element.248) | copy-start | bytes 98308
  121.9 8.4 %copy-start.57 = (s32[2]{0:T(128)S(1)}, s32[2]{0:T(128)}, u32[]{:S(2)}) copy-start(s32[2]{0:T(128)} %lengths.7) | copy-start | bytes 28
  131.6 13.6 %copy-start.10 = (s32[32,1024]{1,0:T(8,128)}, s32[32,1024]{1,0:T(8,128)S(1)}, u32[]{:S(2)}) copy-start(s32[32,1024]{1,0:T(8,128)S(1)} %get-tuple-element.563) | copy-start | bytes 393220
  159.5 45.1 %copy-start.58 = (s32[3,24]{1,0:T(4,128)S(1)}, s32[3,24]{1,0:T(4,128)}, u32[]{:S(2)}) copy-start(s32[3,24]{1,0:T(4,128)} %param.35) | copy-start | bytes 868
  184.1 22.7 %copy-start.59 = (f32[2,24]{1,0:T(2,128)S(1)}, f32[2,24]{1,0:T(2,128)}, u32[]{:S(2)}) copy-start(f32[2,24]{1,0:T(2,128)} %param.36) | copy-start | bytes 580
  270.4 4.9 copy-start.60
  275.3 59.2 %all-to-all-start.2 = ((bf16[8,192,768]{2,1,0:T(8,128)(2,1)}), bf16[8,192,768]{2,1,0:T(8,128)(2,1)}, u32[]{:S(2)}, u32[]{:S(2)}) async-start(bf16[8,192,768]{2,1,0:T(8,128)(2,1)} %bitcast.226), calls=%async_computation.2 | async-start | bytes 4718592 | tf_op jit(solution)/shard_map/all_to_all | solution.py:1175
  313.1 68.3 %collective-permute-start.13 = (bf16[8,384,768]{2,1,0:T(8,128)(2,1)}, bf16[8,384,768]{2,1,0:T(8,128)(2,1)}, u32[]{:S(2)}, u32[]{:S(2)}) collective-permute-start(bf16[8,384,768]{2,1,0:T(8,128)(2,1)} %bitcast_select_fusion), channel_id=1, source_target_pairs={{0,8},{8,0},{16,24},{24,16},{1,9},{9,1},{17,25},{25,17},{2,10},{10... | collective-permute-start | bytes 14155784 | tf_op jit(solution)/shard_map/ppermute | solution.py:993
  326.0 5.7 %copy-start.3 = (bf16[8,192,768]{2,1,0:T(8,128)(2,1)}, bf16[8,192,768]{2,1,0:T(8,128)(2,1)S(1)}, u32[]{:S(2)}) copy-start(bf16[8,192,768]{2,1,0:T(8,128)(2,1)S(1)} %slice.154) | copy-start | bytes 7077892
  330.2 3.6 copy-start.40
  333.8 34.7 %collective-permute-start.3 = (bf16[8,240,768]{2,1,0:T(8,128)(2,1)}, bf16[8,240,768]{2,1,0:T(8,128)(2,1)}, u32[]{:S(2)}, u32[]{:S(2)}) collective-permute-start(bf16[8,240,768]{2,1,0:T(8,128)(2,1)} %broadcast_select_fusion), channel_id=1, source_target_pairs={{0,8},{8,0},{16,24},{24,16},{1,9},{9,1},{17,25},{25,17},{2,10},{10... | collective-permute-start | bytes 8847368 | tf_op jit(solution)/shard_map/ppermute | solution.py:993
  334.6 13.5 %copy-start.61 = (bf16[1024,768]{1,0:T(8,128)(2,1)S(1)}, bf16[1024,768]{1,0:T(8,128)(2,1)}, u32[]{:S(2)}) copy-start(bf16[1024,768]{1,0:T(8,128)(2,1)} %copy-done.60) | copy-start | bytes 4718596
  348.3 5.2 copy-start.63
  348.3 11.7 %copy-start.49 = (s32[8]{0:T(128)S(1)}, s32[8]{0:T(128)}, u32[]{:S(2)}) copy-start(s32[8]{0:T(128)} %constant.421.clone) | copy-start | bytes 100
  348.3 20.1 %copy-start.4 = (bf16[8,192,768]{2,1,0:T(8,128)(2,1)S(1)}, bf16[8,192,768]{2,1,0:T(8,128)(2,1)}, u32[]{:S(2)}) copy-start(bf16[8,192,768]{2,1,0:T(8,128)(2,1)} %copy-done.3) | copy-start | bytes 7077892
  353.0 21.0 %collective-permute-start = (bf16[1920,768]{1,0:T(8,128)(2,1)}, bf16[1920,768]{1,0:T(8,128)(2,1)}, u32[]{:S(2)}, u32[]{:S(2)}) collective-permute-start(bf16[1920,768]{1,0:T(8,128)(2,1)} %dynamic-slice_convert_fusion), channel_id=1, source_target_pairs={{0,8},{8,0},{16,24},{24,16},{1,9},{9,1},{17,25},{25,17},{2,10},{10... | collective-permute-start | bytes 8847368 | tf_op jit(solution)/shard_map/ppermute | solution.py:993
  368.5 7.0 %copy-start = (f32[3840,768]{1,0:T(8,128)S(1)}, f32[3840,768]{1,0:T(8,128)}, u32[]{:S(2)}) copy-start(f32[3840,768]{1,0:T(8,128)} %get-tuple-element.588) | copy-start | bytes 35389444
  368.5 12.9 %slice-start = ((s8[4718592]{0:T(1024)(128)(4,1)}), s8[4194304]{0:T(1024)(128)(4,1)S(1)}, s32[]{:S(2)}) async-start(s8[4718592]{0:T(1024)(128)(4,1)} %bitcast.206), calls=%async_computation.3 | async-start | bytes 8388608
  371.6 8.4 %copy-start.6 = (bf16[8,240,768]{2,1,0:T(8,128)(2,1)}, bf16[8,240,768]{2,1,0:T(8,128)(2,1)S(1)}, u32[]{:S(2)}) copy-start(bf16[8,240,768]{2,1,0:T(8,128)(2,1)S(1)} %add_convert_fusion.1) | copy-start | bytes 8847364
  371.6 9.8 %slice-start.1 = ((s8[4718592]{0:T(1024)(128)(4,1)}), s8[524288]{0:T(1024)(128)(4,1)S(1)}, s32[]{:S(2)}) async-start(s8[4718592]{0:T(1024)(128)(4,1)} %bitcast.206), calls=%async_computation.4 | async-start | bytes 1048576
  372.4 17.2 %collective-permute-start.4 = (bf16[240,768]{1,0:T(8,128)(2,1)}, bf16[240,768]{1,0:T(8,128)(2,1)}, u32[]{:S(2)}, u32[]{:S(2)}) collective-permute-start(bf16[240,768]{1,0:T(8,128)(2,1)} %get-tuple-element.345), channel_id=1, source_target_pairs={{0,1},{2,0},{4,2},{6,4},{7,6},{5,7},{3,5},{1,3},{8,9},{10,8},{12,1... | collective-permute-start | bytes 1105928 | tf_op jit(solution)/shard_map/ppermute | solution.py:1013
  380.0 66.1 %collective-permute-start.1 = (bf16[1920,768]{1,0:T(8,128)(2,1)}, bf16[1920,768]{1,0:T(8,128)(2,1)}, u32[]{:S(2)}, u32[]{:S(2)}) collective-permute-start(bf16[1920,768]{1,0:T(8,128)(2,1)} %add_convert_fusion.3), channel_id=1, source_target_pairs={{0,16},{8,24},{16,0},{24,8},{1,17},{9,25},{17,1},{25,9},{2,18},{10... | collective-permute-start | bytes 8847368 | tf_op jit(solution)/shard_map/ppermute | solution.py:1005
  387.0 14.6 %copy-start.5 = (bf16[8,384,768]{2,1,0:T(8,128)(2,1)}, bf16[8,384,768]{2,1,0:T(8,128)(2,1)S(1)}, u32[]{:S(2)}) copy-start(bf16[8,384,768]{2,1,0:T(8,128)(2,1)S(1)} %add_convert_fusion) | copy-start | bytes 14155780
  388.0 13.5 %collective-permute-start.14 = (bf16[384,768]{1,0:T(8,128)(2,1)S(1)}, bf16[384,768]{1,0:T(8,128)(2,1)S(1)}, u32[]{:S(2)}, u32[]{:S(2)}) collective-permute-start(bf16[384,768]{1,0:T(8,128)(2,1)S(1)} %get-tuple-element.341), channel_id=1, source_target_pairs={{0,2},{2,4},{4,6},{6,7},{7,5},{5,3},{3,1},{1,0},{8,10},{10,12},{12... | collective-permute-start | bytes 1769480 | tf_op jit(solution)/shard_map/ppermute | solution.py:1013
  391.5 18.0 %collective-permute-start.5 = (bf16[240,768]{1,0:T(8,128)(2,1)}, bf16[240,768]{1,0:T(8,128)(2,1)}, u32[]{:S(2)}, u32[]{:S(2)}) collective-permute-start(bf16[240,768]{1,0:T(8,128)(2,1)} %fusion.42), channel_id=1, source_target_pairs={{0,1},{2,0},{4,2},{6,4},{7,6},{5,7},{3,5},{1,3},{8,9},{10,8},{12,1... | collective-permute-start | bytes 1105928 | tf_op jit(solution)/shard_map/ppermute | solution.py:1013
  402.5 16.5 %collective-permute-start.15 = (bf16[384,768]{1,0:T(8,128)(2,1)}, bf16[384,768]{1,0:T(8,128)(2,1)S(1)}, u32[]{:S(2)}, u32[]{:S(2)}) collective-permute-start(bf16[384,768]{1,0:T(8,128)(2,1)} %fusion.35), channel_id=1, source_target_pairs={{0,2},{2,4},{4,6},{6,7},{7,5},{5,3},{3,1},{1,0},{8,10},{10,12},{12... | collective-permute-start | bytes 1769480 | tf_op jit(solution)/shard_map/ppermute | solution.py:1013
  408.0 18.9 %collective-permute-start.8 = (bf16[240,768]{1,0:T(8,128)(2,1)S(1)}, bf16[240,768]{1,0:T(8,128)(2,1)S(1)}, u32[]{:S(2)}, u32[]{:S(2)}) collective-permute-start(bf16[240,768]{1,0:T(8,128)(2,1)S(1)} %get-tuple-element.346), channel_id=1, source_target_pairs={{0,2},{2,4},{4,6},{6,7},{7,5},{5,3},{3,1},{1,0},{8,10},{10,12},{12... | collective-permute-start | bytes 1105928 | tf_op jit(solution)/shard_map/ppermute | solution.py:1013
  410.7 16.2 %collective-permute-start.6 = (bf16[240,768]{1,0:T(8,128)(2,1)S(1)}, bf16[240,768]{1,0:T(8,128)(2,1)S(1)}, u32[]{:S(2)}, u32[]{:S(2)}) collective-permute-start(bf16[240,768]{1,0:T(8,128)(2,1)S(1)} %fusion.43), channel_id=1, source_target_pairs={{0,1},{2,0},{4,2},{6,4},{7,6},{5,7},{3,5},{1,3},{8,9},{10,8},{12,1... | collective-permute-start | bytes 1105928 | tf_op jit(solution)/shard_map/ppermute | solution.py:1013
  411.3 23.5 %collective-permute-start.18 = (bf16[384,768]{1,0:T(8,128)(2,1)}, bf16[384,768]{1,0:T(8,128)(2,1)S(1)}, u32[]{:S(2)}, u32[]{:S(2)}) collective-permute-start(bf16[384,768]{1,0:T(8,128)(2,1)} %get-tuple-element.342), channel_id=1, source_target_pairs={{0,1},{2,0},{4,2},{6,4},{7,6},{5,7},{3,5},{1,3},{8,9},{10,8},{12,1... | collective-permute-start | bytes 1769480 | tf_op jit(solution)/shard_map/ppermute | solution.py:1013
  420.2 19.3 %collective-permute-start.16 = (bf16[384,768]{1,0:T(8,128)(2,1)S(1)}, bf16[384,768]{1,0:T(8,128)(2,1)S(1)}, u32[]{:S(2)}, u32[]{:S(2)}) collective-permute-start(bf16[384,768]{1,0:T(8,128)(2,1)S(1)} %fusion.36), channel_id=1, source_target_pairs={{0,2},{2,4},{4,6},{6,7},{7,5},{5,3},{3,1},{1,0},{8,10},{10,12},{12... | collective-permute-start | bytes 1769480 | tf_op jit(solution)/shard_map/ppermute | solution.py:1013
  428.9 20.7 %collective-permute-start.9 = (bf16[240,768]{1,0:T(8,128)(2,1)S(1)}, bf16[240,768]{1,0:T(8,128)(2,1)S(1)}, u32[]{:S(2)}, u32[]{:S(2)}) collective-permute-start(bf16[240,768]{1,0:T(8,128)(2,1)S(1)} %get-tuple-element.344), channel_id=1, source_target_pairs={{0,2},{2,4},{4,6},{6,7},{7,5},{5,3},{3,1},{1,0},{8,10},{10,12},{12... | collective-permute-start | bytes 1105928 | tf_op jit(solution)/shard_map/ppermute | solution.py:1013
  430.5 29.1 %collective-permute-start.7 = (bf16[240,768]{1,0:T(8,128)(2,1)}, bf16[240,768]{1,0:T(8,128)(2,1)}, u32[]{:S(2)}, u32[]{:S(2)}) collective-permute-start(bf16[240,768]{1,0:T(8,128)(2,1)} %get-tuple-element.343), channel_id=1, source_target_pairs={{0,1},{2,0},{4,2},{6,4},{7,6},{5,7},{3,5},{1,3},{8,9},{10,8},{12,1... | collective-permute-start | bytes 1105928 | tf_op jit(solution)/shard_map/ppermute | solution.py:1013
  441.9 13.0 %collective-permute-start.19 = (bf16[384,768]{1,0:T(8,128)(2,1)S(1)}, bf16[384,768]{1,0:T(8,128)(2,1)S(1)}, u32[]{:S(2)}, u32[]{:S(2)}) collective-permute-start(bf16[384,768]{1,0:T(8,128)(2,1)S(1)} %get-tuple-element.340), channel_id=1, source_target_pairs={{0,1},{2,0},{4,2},{6,4},{7,6},{5,7},{3,5},{1,3},{8,9},{10,8},{12,1... | collective-permute-start | bytes 1769480 | tf_op jit(solution)/shard_map/ppermute | solution.py:1013
  449.6 28.2 %copy-start.7 = (bf16[1920,768]{1,0:T(8,128)(2,1)}, bf16[1920,768]{1,0:T(8,128)(2,1)S(1)}, u32[]{:S(2)}) copy-start(bf16[1920,768]{1,0:T(8,128)(2,1)S(1)} %add_convert_fusion.2) | copy-start | bytes 8847364
  449.6 51.6 %collective-permute-start.2 = (bf16[1920,768]{1,0:T(8,128)(2,1)S(1)}, bf16[1920,768]{1,0:T(8,128)(2,1)}, u32[]{:S(2)}, u32[]{:S(2)}) collective-permute-start(bf16[1920,768]{1,0:T(8,128)(2,1)S(1)} %add_convert_fusion.2), channel_id=1, source_target_pairs={{0,8},{8,0},{16,24},{24,16},{1,9},{9,1},{17,25},{25,17},{2,10},{10... | collective-permute-start | bytes 8847368 | tf_op jit(solution)/shard_map/ppermute | solution.py:993
  451.7 11.7 %collective-permute-start.10 = (bf16[240,768]{1,0:T(8,128)(2,1)}, bf16[240,768]{1,0:T(8,128)(2,1)}, u32[]{:S(2)}, u32[]{:S(2)}) collective-permute-start(bf16[240,768]{1,0:T(8,128)(2,1)} %fusion.41), channel_id=1, source_target_pairs={{0,2},{2,4},{4,6},{6,7},{7,5},{5,3},{3,1},{1,0},{8,10},{10,12},{12... | collective-permute-start | bytes 1105928 | tf_op jit(solution)/shard_map/ppermute | solution.py:1013
  453.4 22.0 %collective-permute-start.17 = (bf16[384,768]{1,0:T(8,128)(2,1)}, bf16[384,768]{1,0:T(8,128)(2,1)S(1)}, u32[]{:S(2)}, u32[]{:S(2)}) collective-permute-start(bf16[384,768]{1,0:T(8,128)(2,1)} %get-tuple-element.339), channel_id=1, source_target_pairs={{0,2},{2,4},{4,6},{6,7},{7,5},{5,3},{3,1},{1,0},{8,10},{10,12},{12... | collective-permute-start | bytes 1769480 | tf_op jit(solution)/shard_map/ppermute | solution.py:1013
  456.9 19.2 %collective-permute-start.20 = (bf16[384,768]{1,0:T(8,128)(2,1)}, bf16[384,768]{1,0:T(8,128)(2,1)}, u32[]{:S(2)}, u32[]{:S(2)}) collective-permute-start(bf16[384,768]{1,0:T(8,128)(2,1)} %fusion.34), channel_id=1, source_target_pairs={{0,1},{2,0},{4,2},{6,4},{7,6},{5,7},{3,5},{1,3},{8,9},{10,8},{12,1... | collective-permute-start | bytes 1769480 | tf_op jit(solution)/shard_map/ppermute | solution.py:1013
  464.8 14.5 %collective-permute-start.11 = (bf16[240,768]{1,0:T(8,128)(2,1)S(1)}, bf16[240,768]{1,0:T(8,128)(2,1)S(1)}, u32[]{:S(2)}, u32[]{:S(2)}) collective-permute-start(bf16[240,768]{1,0:T(8,128)(2,1)S(1)} %fusion.46), channel_id=1, source_target_pairs={{0,16},{8,24},{16,0},{24,8},{1,17},{9,25},{17,1},{25,9},{2,18},{10... | collective-permute-start | bytes 1105928 | tf_op jit(solution)/shard_map/ppermute | solution.py:1005
  477.8 3.6 copy-start.23
  477.8 14.8 %collective-permute-start.21 = (bf16[384,768]{1,0:T(8,128)(2,1)S(1)}, bf16[384,768]{1,0:T(8,128)(2,1)}, u32[]{:S(2)}, u32[]{:S(2)}) collective-permute-start(bf16[384,768]{1,0:T(8,128)(2,1)S(1)} %fusion.39), channel_id=1, source_target_pairs={{0,16},{8,24},{16,0},{24,8},{1,17},{9,25},{17,1},{25,9},{2,18},{10... | collective-permute-start | bytes 1769480 | tf_op jit(solution)/shard_map/ppermute | solution.py:1005
  480.1 13.9 %collective-permute-start.12 = (bf16[240,768]{1,0:T(8,128)(2,1)}, bf16[240,768]{1,0:T(8,128)(2,1)}, u32[]{:S(2)}, u32[]{:S(2)}) collective-permute-start(bf16[240,768]{1,0:T(8,128)(2,1)} %add_convert_fusion.5), channel_id=1, source_target_pairs={{0,8},{8,0},{16,24},{24,16},{1,9},{9,1},{17,25},{25,17},{2,10},{10... | collective-permute-start | bytes 1105928 | tf_op jit(solution)/shard_map/ppermute | solution.py:993
  494.0 5.4 collective-permute-start.22
  495.3 8.1 %copy-start.16 = (f32[240,768]{1,0:T(8,128)}, f32[240,768]{1,0:T(8,128)S(1)}, u32[]{:S(2)}) copy-start(f32[240,768]{1,0:T(8,128)S(1)} %get-tuple-element.353) | copy-start | bytes 2211844
  495.3 8.1 %copy-start.21 = (f32[240,768]{1,0:T(8,128)}, f32[240,768]{1,0:T(8,128)S(1)}, u32[]{:S(2)}) copy-start(f32[240,768]{1,0:T(8,128)S(1)} %get-tuple-element.352) | copy-start | bytes 2211844
  495.3 5.9 %copy-start.8 = (bf16[1920,768]{1,0:T(8,128)(2,1)S(1)}, bf16[1920,768]{1,0:T(8,128)(2,1)}, u32[]{:S(2)}) copy-start(bf16[1920,768]{1,0:T(8,128)(2,1)} %copy-done.7) | copy-start | bytes 8847364
  495.4 8.1 %copy-start.11 = (f32[192,768]{1,0:T(8,128)}, f32[192,768]{1,0:T(8,128)S(1)}, u32[]{:S(2)}) copy-start(f32[192,768]{1,0:T(8,128)S(1)} %slice.161) | copy-start | bytes 1769476
  498.0 5.4 copy-start.22
  499.4 4.0 copy-start.24
  527.3 4.3 copy-start.28
  527.3 4.3 copy-start.41
  527.3 4.3 copy-start.42
  528.5 5.0 copy-start.34
  528.5 5.0 copy-start.36
  528.5 5.0 copy-start.38
  528.5 5.0 copy-start.43
  528.5 5.0 copy-start.44
  534.4 26.4 %copy-start.25 = (bf16[384,768]{1,0:T(8,128)(2,1)S(1)}, bf16[384,768]{1,0:T(8,128)(2,1)}, u32[]{:S(2)}) copy-start(bf16[384,768]{1,0:T(8,128)(2,1)} %get-tuple-element.328) | copy-start | bytes 1769476
  560.8 4.3 copy-start.13
  560.8 4.3 copy-start.14
  560.8 4.3 copy-start.29
  560.9 4.3 copy-start.30
  565.2 3.2 copy-start.32
  (24 other events, 46.2 us)
